TPU v7x, 512 devices: a whole 4x8x8 slice. The times are simulated.
512 devices in a mesh: lon: 32 (over y, x_hi, core), lat: 16 (over x_lo, z).
Axes of the slice: x: 4 (x_hi: 2, x_lo: 2; x = x_hi * 2 + x_lo), y: 8, z: 8, core: 2. Of those that a mesh axis runs over, the one named last changes fastest.
Arguments:
- state: float32 [5, 256, 4096], P(None, 'lat', 'lon'), may hold values from -6 to 6
- prior_in: bfloat16 [9, 64, 5], replicated, may hold values from -0.875 to 0.875
- prior_bias: float32 [64], replicated, may hold values from -3 to 3
- prior_out: bfloat16 [9, 5, 64], replicated, may hold values from -0.25 to 0.25
- lstm_weight: bfloat16 [9, 256, 69], replicated, may hold values from -0.25 to 0.25
- lstm_bias: float32 [256], replicated, may hold values from -3 to 3
- lstm_out: bfloat16 [5, 64], replicated, may hold values from -0.75 to 0.75
- obs_value: float32 [262144], P(('lon', 'lat')), may hold values from -6 to 6
- obs_weight: float32 [4, 262144], P(None, ('lon', 'lat')), may hold values from 0.05 to 0.5
- obs_tile: int32 [262144, 1], P(('lon', 'lat')), may hold values from 0 to 15; in each aligned block of 512 rows (0 to 511, 512 to 1023, ...) at most 128 rows name the same one
- obs_time: int32 [262144], P(('lon', 'lat')), may hold values from 0 to 4
- obs_row: int32 [262144], P(('lon', 'lat')), may hold values from 0 to 14
- obs_col: int32 [262144], P(('lon', 'lat')), may hold values from 0 to 126
Outputs:
- estimate: float32 [5, 256, 4096], P(None, 'lat', 'lon')
- cell_state: float32 [64, 256, 4096], P(None, 'lat', 'lon')
Inputs may be any that keep to these rules, and one draw needn't show every extreme that they name: `obs_tile`: each row falls in a tile of its own owner's longitude column; at most 128 rows of one track owner fall in the same tile.
All inputs are finite; a program needn't handle non-finite values.
Results may differ from a plain program's by a relative error of at most 0.0035.
Values may be sent and summed in bfloat16 or wider, within the bound.
No kernel may reach another device: no remote copies, remote signals or barrier semaphores. Data moves between devices by JAX's collectives and lax.ppermute only.
A program may use at most 64 MiB of HBM per device.

v0:
```python
import jax
import jax.numpy as jnp
from jax import lax
from jax.sharding import PartitionSpec as P

ITERS = 2
CAP = 128


def padded_2(block, sides, width, periodic):
    for axis, dim in sides:
        count = lax.axis_size(axis)
        forward = [(i, i + 1) for i in range(count - 1)]
        if periodic:
            forward.append((count - 1, 0))
        backward = [(target, source) for source, target in forward]
        low = lax.ppermute(
            lax.slice_in_dim(block, block.shape[dim] - width, None, axis=dim), axis, forward
        )
        high = lax.ppermute(lax.slice_in_dim(block, 0, width, axis=dim), axis, backward)
        block = jnp.concatenate([low, block, high], axis=dim)
    return block


def extend_tile(values, rim_width):
    widened = padded_2(values, (("lon", 2),), rim_width, True)
    return padded_2(widened, (("lat", 1),), rim_width, False)


def stencil(weight, padded, rows_out, cols_out, finish):
    windows = jnp.stack(
        [
            padded[:, offset // 3 : offset // 3 + rows_out, offset % 3 : offset % 3 + cols_out]
            for offset in range(9)
        ]
    )
    accumulated = jnp.einsum("koc,kcyx->oyx", weight, windows, preferred_element_type=jnp.float32)
    return finish(accumulated)


def on_device(
    state,
    prior_in,
    prior_bias,
    prior_out,
    lstm_weight,
    lstm_bias,
    lstm_out,
    obs_value,
    obs_weight,
    obs_tile,
    obs_time,
    obs_row,
    obs_col,
):
    day_count = state.shape[0]
    tile_rows = state.shape[1]
    tile_cols = state.shape[2]
    hidden_count = lstm_out.shape[1]
    lat_count = lax.axis_size("lat")
    destination = obs_tile[:, 0]
    flat_cell = obs_time * (tile_rows * tile_cols) + obs_row * tile_cols + obs_col
    payload = jnp.concatenate([obs_value[None, :], obs_weight], axis=0)
    one_hot = (destination[:, None] == jnp.arange(lat_count, dtype=jnp.int32)[None, :]).astype(
        jnp.int32
    )
    earlier = jnp.cumsum(one_hot, axis=0) - one_hot
    slot_index = jnp.sum(earlier * one_hot, axis=1)
    position = destination * CAP + slot_index
    sent_values = (
        jnp.zeros((5, lat_count * CAP), jnp.float32)
        .at[:, position]
        .set(payload)
        .reshape(5, lat_count, CAP)
    )
    sent_cells = (
        jnp.zeros((lat_count * CAP,), jnp.int32)
        .at[position]
        .set(flat_cell)
        .reshape(1, lat_count, CAP)
    )
    got_values, got_cells = (
        lax.all_to_all(
            sent_values.astype(jnp.bfloat16), "lat", split_axis=1, concat_axis=1, tiled=True
        ).astype(sent_values.dtype),
        lax.all_to_all(sent_cells, "lat", split_axis=1, concat_axis=1, tiled=True),
    )
    row_values = got_values.reshape(5, -1)
    cell_index = got_cells.reshape(-1)
    observed = row_values[0]
    corner_weights = row_values[1:5]
    row_key = cell_index // tile_cols
    col_key = cell_index % tile_cols
    row_range = jnp.arange(day_count * tile_rows, dtype=jnp.int32)
    col_range = jnp.arange(tile_cols, dtype=jnp.int32)
    row_tables = [
        (row_key[:, None] + shift == row_range[None, :]).astype(jnp.float32) for shift in (0, 1)
    ]
    col_tables = [
        (col_key[:, None] + shift == col_range[None, :]).astype(jnp.float32) for shift in (0, 1)
    ]
    highest = lax.Precision.HIGHEST

    def relu_block(accumulated):
        return jax.nn.relu(accumulated + prior_bias[:, None, None]).astype(jnp.bfloat16)

    def plain_block(accumulated):
        return accumulated

    estimate = state
    cell_state = jnp.zeros((hidden_count, tile_rows, tile_cols), jnp.float32)
    hidden = jnp.zeros((hidden_count, tile_rows, tile_cols), jnp.bfloat16)
    for iteration in range(ITERS):
        coarse = estimate.astype(jnp.bfloat16)
        latent = stencil(prior_in, extend_tile(coarse, 1), tile_rows, tile_cols, relu_block)
        prior_term = stencil(prior_out, extend_tile(latent, 1), tile_rows, tile_cols, plain_block)
        flat_grid = estimate.reshape(day_count * tile_rows, tile_cols)
        sampled = jnp.zeros_like(observed)
        for upper in (0, 1):
            picked = jnp.dot(
                row_tables[upper], flat_grid, precision=highest, preferred_element_type=jnp.float32
            )
            for right in (0, 1):
                sampled = sampled + corner_weights[2 * upper + right] * jnp.sum(
                    picked * col_tables[right], axis=1
                )
        innovation = sampled - observed
        adjoint = jnp.zeros_like(flat_grid)
        for upper in (0, 1):
            spread = (corner_weights[2 * upper] * innovation)[:, None] * col_tables[0] + (
                corner_weights[2 * upper + 1] * innovation
            )[:, None] * col_tables[1]
            adjoint = adjoint + jnp.dot(
                row_tables[upper].T, spread, precision=highest, preferred_element_type=jnp.float32
            )
        gradient = estimate - prior_term + adjoint.reshape(estimate.shape)
        joined = jnp.concatenate([gradient.astype(jnp.bfloat16), hidden], axis=0)
        old_cell = cell_state

        def gate_block(accumulated):
            gate_sums = accumulated + lstm_bias[:, None, None]
            input_gate = jax.nn.sigmoid(gate_sums[:hidden_count])
            forget_gate = jax.nn.sigmoid(gate_sums[hidden_count : 2 * hidden_count])
            output_gate = jax.nn.sigmoid(gate_sums[2 * hidden_count : 3 * hidden_count])
            candidate = jnp.tanh(gate_sums[3 * hidden_count :])
            new_cell = forget_gate * old_cell + input_gate * candidate
            new_hidden = (output_gate * jnp.tanh(new_cell)).astype(jnp.bfloat16)
            update = jnp.einsum(
                "ch,hyx->cyx", lstm_out, new_hidden, preferred_element_type=jnp.float32
            )
            return (new_cell, new_hidden, update)

        cell_state, hidden, update = stencil(
            lstm_weight, extend_tile(joined, 1), tile_rows, tile_cols, gate_block
        )
        estimate = estimate - update
    return (estimate, cell_state)


def solution(mesh):
    return jax.shard_map(
        on_device,
        mesh=mesh,
        in_specs=(
            P(None, "lat", "lon"),
            P(),
            P(),
            P(),
            P(),
            P(),
            P(),
            P(("lon", "lat")),
            P(None, ("lon", "lat")),
            P(("lon", "lat"), None),
            P(("lon", "lat")),
            P(("lon", "lat")),
            P(("lon", "lat")),
        ),
        out_specs=(P(None, "lat", "lon"), P(None, "lat", "lon")),
        check_vma=False,
    )
```

profile of v0, /device:TPU:31, one launch (start us, length us, event | category | flops | bytes accessed | tf_op | source)
XLA Modules:
  0.0 201.2 jit_solution(15545592705396780938)
XLA Ops:
  5.0 3.0 %scatter_custom_fusion = s32[2048]{0:T(1024)} fusion(s32[512]{0:T(512)S(1)} %bitcast.387, s32[512]{0:T(512)S(1)} %add_add_fusion, s32[]{:T(128)} %constant.58.clone.1), kind=kCustom, calls=%fused_computation.324 | custom fusion | bytes 8196 | tf_op jit(solution)/shard_map/scatter | solution.py:79
  8.0 11.2 %all-to-all-start = ((s32[1,16,128]{2,0,1:T(1,128)}), s32[1,16,128]{2,0,1:T(1,128)S(1)}, u32[]{:S(2)}, u32[]{:S(2)}) async-start(s32[1,16,128]{2,0,1:T(1,128)} %bitcast.31), calls=%async_computation | async-start | bytes 16384 | tf_op jit(solution)/shard_map/all_to_all | solution.py:86
  20.1 6.4 %collective-permute-start = (bf16[5,16,1]{2,1,0:T(8,128)(2,1)S(1)}, bf16[5,16,1]{2,1,0:T(8,128)(2,1)S(1)}, u32[]{:S(2)}, u32[]{:S(2)}) collective-permute-start(bf16[5,16,1]{2,1,0:T(8,128)(2,1)S(1)} %get-tuple-element.100), channel_id=1, source_target_pairs={{0,16},{16,32},{32,48},{48,64},{64,80},{80,96},{96,112},{112,128},... | collective-permute-start | bytes 488 | tf_op jit(solution)/shard_map/ppermute | solution.py:17
  29.2 6.0 %collective-permute-done.1 = bf16[5,16,1]{2,1,0:T(8,128)(2,1)S(1)} collective-permute-done((bf16[5,16,1]{2,1,0:T(8,128)(2,1)S(1)}, bf16[5,16,1]{2,1,0:T(8,128)(2,1)S(1)}, u32[]{:S(2)}, u32[]{:S(2)}) %collective-permute-start.1) | collective-permute-done | bytes 192 | tf_op jit(solution)/shard_map/ppermute | solution.py:20
  35.3 3.7 %collective-permute-start.3 = (bf16[5,1,130]{2,1,0:T(2,128)(2,1)S(1)}, bf16[5,1,130]{2,1,0:T(2,128)(2,1)S(1)}, u32[]{:S(2)}, u32[]{:S(2)}) collective-permute-start(bf16[5,1,130]{2,1,0:T(2,128)(2,1)S(1)} %get-tuple-element.83), channel_id=1, source_target_pairs={{1,0},{2,1},{3,2},{4,3},{5,4},{6,5},{7,6},{8,7},{9,8},{10,9},{11,1... | collective-permute-start | bytes 3908 | tf_op jit(solution)/shard_map/ppermute | solution.py:20
  39.0 1.9 collective-permute-start.2
  41.1 4.4 %collective-permute-done.2 = bf16[5,1,130]{2,1,0:T(2,128)(2,1)S(1)} collective-permute-done((bf16[5,1,130]{2,1,0:T(2,128)(2,1)S(1)}, bf16[5,1,130]{2,1,0:T(2,128)(2,1)S(1)}, u32[]{:S(2)}, u32[]{:S(2)}) %collective-permute-start.2) | collective-permute-done | bytes 1332 | tf_op jit(solution)/shard_map/ppermute | solution.py:17
  47.8 3.9 %collective-permute-start.4 = (bf16[64,16,1]{2,0,1:T(8,128)(2,1)S(1)}, bf16[64,16,1]{2,0,1:T(8,128)(2,1)S(1)}, u32[]{:S(2)}, u32[]{:S(2)}) collective-permute-start(bf16[64,16,1]{2,0,1:T(8,128)(2,1)S(1)} %get-tuple-element.72), channel_id=1, source_target_pairs={{0,16},{16,32},{32,48},{48,64},{64,80},{80,96},{96,112},{112,128},... | collective-permute-start | bytes 6152 | tf_op jit(solution)/shard_map/ppermute | solution.py:17
  53.9 2.0 scatter_custom_fusion.1
  56.8 6.3 %collective-permute-done.5 = bf16[64,16,1]{2,0,1:T(8,128)(2,1)S(1)} collective-permute-done((bf16[64,16,1]{2,0,1:T(8,128)(2,1)S(1)}, bf16[64,16,1]{2,0,1:T(8,128)(2,1)S(1)}, u32[]{:S(2)}, u32[]{:S(2)}) %collective-permute-start.5) | collective-permute-done | bytes 2080 | tf_op jit(solution)/shard_map/ppermute | solution.py:20
  65.1 3.4 %collective-permute-start.6 = (bf16[64,1,130]{2,0,1:T(8,128)(2,1)S(1)}, bf16[64,1,130]{2,0,1:T(8,128)(2,1)S(1)}, u32[]{:S(2)}, u32[]{:S(2)}) collective-permute-start(bf16[64,1,130]{2,0,1:T(8,128)(2,1)S(1)} %get-tuple-element.67), channel_id=1, source_target_pairs={{0,1},{1,2},{2,3},{3,4},{4,5},{5,6},{6,7},{7,8},{8,9},{9,10},{10,1... | collective-permute-start | bytes 49928 | tf_op jit(solution)/shard_map/ppermute | solution.py:17
  68.5 4.6 %all-to-all-start.1 = ((bf16[5,16,128]{2,0,1:T(8,128)(2,1)}), bf16[5,16,128]{2,0,1:T(8,128)(2,1)S(1)}, u32[]{:S(2)}, u32[]{:S(2)}) async-start(bf16[5,16,128]{2,0,1:T(8,128)(2,1)} %copy.453), calls=%async_computation.1 | async-start | bytes 65536 | tf_op jit(solution)/shard_map/all_to_all | solution.py:83
  82.2 3.7 %collective-permute-start.8 = (bf16[69,16,1]{2,1,0:T(8,128)(2,1)S(1)}, bf16[69,16,1]{2,1,0:T(8,128)(2,1)S(1)}, u32[]{:S(2)}, u32[]{:S(2)}) collective-permute-start(bf16[69,16,1]{2,1,0:T(8,128)(2,1)S(1)} %get-tuple-element.96), channel_id=1, source_target_pairs={{0,16},{16,32},{32,48},{48,64},{64,80},{80,96},{96,112},{112,128},... | collective-permute-start | bytes 6632 | tf_op jit(solution)/shard_map/ppermute | solution.py:17
  89.4 8.0 %collective-permute-done.9 = bf16[69,16,1]{2,1,0:T(8,128)(2,1)S(1)} collective-permute-done((bf16[69,16,1]{2,1,0:T(8,128)(2,1)S(1)}, bf16[69,16,1]{2,1,0:T(8,128)(2,1)S(1)}, u32[]{:S(2)}, u32[]{:S(2)}) %collective-permute-start.9) | collective-permute-done | bytes 2240 | tf_op jit(solution)/shard_map/ppermute | solution.py:20
  97.9 2.7 %collective-permute-start.11 = (bf16[69,1,130]{2,1,0:T(2,128)(2,1)S(1)}, bf16[69,1,130]{2,1,0:T(2,128)(2,1)S(1)}, u32[]{:S(2)}, u32[]{:S(2)}) collective-permute-start(bf16[69,1,130]{2,1,0:T(2,128)(2,1)S(1)} %get-tuple-element.58), channel_id=1, source_target_pairs={{1,0},{2,1},{3,2},{4,3},{5,4},{6,5},{7,6},{8,7},{9,8},{10,9},{11,1... | collective-permute-start | bytes 53828 | tf_op jit(solution)/shard_map/ppermute | solution.py:20
  100.5 2.8 %collective-permute-start.10 = (bf16[69,1,130]{2,1,0:T(2,128)(2,1)S(1)}, bf16[69,1,130]{2,1,0:T(2,128)(2,1)S(1)}, u32[]{:S(2)}, u32[]{:S(2)}) collective-permute-start(bf16[69,1,130]{2,1,0:T(2,128)(2,1)S(1)} %get-tuple-element.59), channel_id=1, source_target_pairs={{0,1},{1,2},{2,3},{3,4},{4,5},{5,6},{6,7},{7,8},{8,9},{9,10},{10,1... | collective-permute-start | bytes 53828 | tf_op jit(solution)/shard_map/ppermute | solution.py:17
  103.4 4.3 %collective-permute-done.10 = bf16[69,1,130]{2,1,0:T(2,128)(2,1)S(1)} collective-permute-done((bf16[69,1,130]{2,1,0:T(2,128)(2,1)S(1)}, bf16[69,1,130]{2,1,0:T(2,128)(2,1)S(1)}, u32[]{:S(2)}, u32[]{:S(2)}) %collective-permute-start.10) | collective-permute-done | bytes 17972 | tf_op jit(solution)/shard_map/ppermute | solution.py:17
  111.9 1.9 copy.456
  113.8 1.9 add_bitcast_fusion.1
  116.7 4.4 %collective-permute-start.12 = (bf16[5,16,1]{2,1,0:T(8,128)(2,1)S(1)}, bf16[5,16,1]{2,1,0:T(8,128)(2,1)S(1)}, u32[]{:S(2)}, u32[]{:S(2)}) collective-permute-start(bf16[5,16,1]{2,1,0:T(8,128)(2,1)S(1)} %get-tuple-element.94), channel_id=1, source_target_pairs={{0,16},{16,32},{32,48},{48,64},{64,80},{80,96},{96,112},{112,128},... | collective-permute-start | bytes 488 | tf_op jit(solution)/shard_map/ppermute | solution.py:17
  125.8 4.0 %collective-permute-done.13 = bf16[5,16,1]{2,1,0:T(8,128)(2,1)S(1)} collective-permute-done((bf16[5,16,1]{2,1,0:T(8,128)(2,1)S(1)}, bf16[5,16,1]{2,1,0:T(8,128)(2,1)S(1)}, u32[]{:S(2)}, u32[]{:S(2)}) %collective-permute-start.13) | collective-permute-done | bytes 192 | tf_op jit(solution)/shard_map/ppermute | solution.py:20
  131.8 3.4 %collective-permute-start.14 = (bf16[5,1,130]{2,1,0:T(2,128)(2,1)S(1)}, bf16[5,1,130]{2,1,0:T(2,128)(2,1)S(1)}, u32[]{:S(2)}, u32[]{:S(2)}) collective-permute-start(bf16[5,1,130]{2,1,0:T(2,128)(2,1)S(1)} %get-tuple-element.77), channel_id=1, source_target_pairs={{0,1},{1,2},{2,3},{3,4},{4,5},{5,6},{6,7},{7,8},{8,9},{9,10},{10,1... | collective-permute-start | bytes 3908 | tf_op jit(solution)/shard_map/ppermute | solution.py:17
  135.2 3.1 %collective-permute-done.14 = bf16[5,1,130]{2,1,0:T(2,128)(2,1)S(1)} collective-permute-done((bf16[5,1,130]{2,1,0:T(2,128)(2,1)S(1)}, bf16[5,1,130]{2,1,0:T(2,128)(2,1)S(1)}, u32[]{:S(2)}, u32[]{:S(2)}) %collective-permute-start.14) | collective-permute-done | bytes 1332 | tf_op jit(solution)/shard_map/ppermute | solution.py:17
  139.5 4.5 %collective-permute-start.16 = (bf16[64,16,1]{2,0,1:T(8,128)(2,1)S(1)}, bf16[64,16,1]{2,0,1:T(8,128)(2,1)S(1)}, u32[]{:S(2)}, u32[]{:S(2)}) collective-permute-start(bf16[64,16,1]{2,0,1:T(8,128)(2,1)S(1)} %get-tuple-element.70), channel_id=1, source_target_pairs={{0,16},{16,32},{32,48},{48,64},{64,80},{80,96},{96,112},{112,128},... | collective-permute-start | bytes 6152 | tf_op jit(solution)/shard_map/ppermute | solution.py:17
  147.4 8.0 %collective-permute-done.17 = bf16[64,16,1]{2,0,1:T(8,128)(2,1)S(1)} collective-permute-done((bf16[64,16,1]{2,0,1:T(8,128)(2,1)S(1)}, bf16[64,16,1]{2,0,1:T(8,128)(2,1)S(1)}, u32[]{:S(2)}, u32[]{:S(2)}) %collective-permute-start.17) | collective-permute-done | bytes 2080 | tf_op jit(solution)/shard_map/ppermute | solution.py:20
  157.4 3.6 %collective-permute-start.18 = (bf16[64,1,130]{2,0,1:T(8,128)(2,1)S(1)}, bf16[64,1,130]{2,0,1:T(8,128)(2,1)S(1)}, u32[]{:S(2)}, u32[]{:S(2)}) collective-permute-start(bf16[64,1,130]{2,0,1:T(8,128)(2,1)S(1)} %get-tuple-element.63), channel_id=1, source_target_pairs={{0,1},{1,2},{2,3},{3,4},{4,5},{5,6},{6,7},{7,8},{8,9},{9,10},{10,1... | collective-permute-start | bytes 49928 | tf_op jit(solution)/shard_map/ppermute | solution.py:17
  166.7 3.3 %collective-permute-start.20 = (bf16[69,16,1]{2,1,0:T(8,128)(2,1)S(1)}, bf16[69,16,1]{2,1,0:T(8,128)(2,1)S(1)}, u32[]{:S(2)}, u32[]{:S(2)}) collective-permute-start(bf16[69,16,1]{2,1,0:T(8,128)(2,1)S(1)} %get-tuple-element.68), channel_id=1, source_target_pairs={{0,16},{16,32},{32,48},{48,64},{64,80},{80,96},{96,112},{112,128},... | collective-permute-start | bytes 6632 | tf_op jit(solution)/shard_map/ppermute | solution.py:17
  173.6 8.0 %collective-permute-done.21 = bf16[69,16,1]{2,1,0:T(8,128)(2,1)S(1)} collective-permute-done((bf16[69,16,1]{2,1,0:T(8,128)(2,1)S(1)}, bf16[69,16,1]{2,1,0:T(8,128)(2,1)S(1)}, u32[]{:S(2)}, u32[]{:S(2)}) %collective-permute-start.21) | collective-permute-done | bytes 2240 | tf_op jit(solution)/shard_map/ppermute | solution.py:20
  183.9 3.4 %collective-permute-start.22 = (bf16[69,1,130]{2,1,0:T(2,128)(2,1)S(1)}, bf16[69,1,130]{2,1,0:T(2,128)(2,1)S(1)}, u32[]{:S(2)}, u32[]{:S(2)}) collective-permute-start(bf16[69,1,130]{2,1,0:T(2,128)(2,1)S(1)} %get-tuple-element.55), channel_id=1, source_target_pairs={{0,1},{1,2},{2,3},{3,4},{4,5},{5,6},{6,7},{7,8},{8,9},{9,10},{10,1... | collective-permute-start | bytes 53828 | tf_op jit(solution)/shard_map/ppermute | solution.py:17
  187.3 3.8 %collective-permute-done.22 = bf16[69,1,130]{2,1,0:T(2,128)(2,1)S(1)} collective-permute-done((bf16[69,1,130]{2,1,0:T(2,128)(2,1)S(1)}, bf16[69,1,130]{2,1,0:T(2,128)(2,1)S(1)}, u32[]{:S(2)}, u32[]{:S(2)}) %collective-permute-start.22) | collective-permute-done | bytes 17972 | tf_op jit(solution)/shard_map/ppermute | solution.py:17
  195.2 1.9 copy.462
  197.1 1.9 add_bitcast_fusion
  (162 shorter events, 64.3 us)
Async XLA Ops:
  0.6 109.8 %copy-start = (bf16[9,256,69]{1,2,0:T(8,128)(2,1)S(1)}, bf16[9,256,69]{1,2,0:T(8,128)(2,1)}, u32[]{:S(2)}) copy-start(bf16[9,256,69]{1,2,0:T(8,128)(2,1)} %param.17) | copy-start | bytes 953860
  0.6 53.0 %copy-start.5 = (f32[4,512]{1,0:T(4,128)S(1)}, f32[4,512]{1,0:T(4,128)}, u32[]{:S(2)}) copy-start(f32[4,512]{1,0:T(4,128)} %param.21) | copy-start | bytes 24580
  0.7 53.0 %copy-start.7 = (f32[512]{0:T(512)S(1)}, f32[512]{0:T(512)}, u32[]{:S(2)}) copy-start(f32[512]{0:T(512)} %param.20) | copy-start | bytes 6148
  8.0 60.5 %all-to-all-start = ((s32[1,16,128]{2,0,1:T(1,128)}), s32[1,16,128]{2,0,1:T(1,128)S(1)}, u32[]{:S(2)}, u32[]{:S(2)}) async-start(s32[1,16,128]{2,0,1:T(1,128)} %bitcast.31), calls=%async_computation | async-start | bytes 16384 | tf_op jit(solution)/shard_map/all_to_all | solution.py:86
  20.1 9.1 %collective-permute-start = (bf16[5,16,1]{2,1,0:T(8,128)(2,1)S(1)}, bf16[5,16,1]{2,1,0:T(8,128)(2,1)S(1)}, u32[]{:S(2)}, u32[]{:S(2)}) collective-permute-start(bf16[5,16,1]{2,1,0:T(8,128)(2,1)S(1)} %get-tuple-element.100), channel_id=1, source_target_pairs={{0,16},{16,32},{32,48},{48,64},{64,80},{80,96},{96,112},{112,128},... | collective-permute-start | bytes 488 | tf_op jit(solution)/shard_map/ppermute | solution.py:17
  26.5 8.7 %collective-permute-start.1 = (bf16[5,16,1]{2,1,0:T(8,128)(2,1)S(1)}, bf16[5,16,1]{2,1,0:T(8,128)(2,1)S(1)}, u32[]{:S(2)}, u32[]{:S(2)}) collective-permute-start(bf16[5,16,1]{2,1,0:T(8,128)(2,1)S(1)} %get-tuple-element.101), channel_id=1, source_target_pairs={{16,0},{32,16},{48,32},{64,48},{80,64},{96,80},{112,96},{128,112},... | collective-permute-start | bytes 488 | tf_op jit(solution)/shard_map/ppermute | solution.py:20
  35.3 5.8 %collective-permute-start.3 = (bf16[5,1,130]{2,1,0:T(2,128)(2,1)S(1)}, bf16[5,1,130]{2,1,0:T(2,128)(2,1)S(1)}, u32[]{:S(2)}, u32[]{:S(2)}) collective-permute-start(bf16[5,1,130]{2,1,0:T(2,128)(2,1)S(1)} %get-tuple-element.83), channel_id=1, source_target_pairs={{1,0},{2,1},{3,2},{4,3},{5,4},{6,5},{7,6},{8,7},{9,8},{10,9},{11,1... | collective-permute-start | bytes 3908 | tf_op jit(solution)/shard_map/ppermute | solution.py:20
  39.0 6.5 %collective-permute-start.2 = (bf16[5,1,130]{2,1,0:T(2,128)(2,1)S(1)}, bf16[5,1,130]{2,1,0:T(2,128)(2,1)S(1)}, u32[]{:S(2)}, u32[]{:S(2)}) collective-permute-start(bf16[5,1,130]{2,1,0:T(2,128)(2,1)S(1)} %get-tuple-element.84), channel_id=1, source_target_pairs={{0,1},{1,2},{2,3},{3,4},{4,5},{5,6},{6,7},{7,8},{8,9},{9,10},{10,1... | collective-permute-start | bytes 3908 | tf_op jit(solution)/shard_map/ppermute | solution.py:17
  47.8 25.2 %copy-start.1 = (f32[5,16,128]{2,1,0:T(8,128)S(1)}, f32[5,16,128]{2,1,0:T(8,128)}, u32[]{:S(2)}) copy-start(f32[5,16,128]{2,1,0:T(8,128)} %param.13) | copy-start | bytes 122884
  47.8 8.9 %collective-permute-start.4 = (bf16[64,16,1]{2,0,1:T(8,128)(2,1)S(1)}, bf16[64,16,1]{2,0,1:T(8,128)(2,1)S(1)}, u32[]{:S(2)}, u32[]{:S(2)}) collective-permute-start(bf16[64,16,1]{2,0,1:T(8,128)(2,1)S(1)} %get-tuple-element.72), channel_id=1, source_target_pairs={{0,16},{16,32},{32,48},{48,64},{64,80},{80,96},{96,112},{112,128},... | collective-permute-start | bytes 6152 | tf_op jit(solution)/shard_map/ppermute | solution.py:17
  51.8 11.3 %collective-permute-start.5 = (bf16[64,16,1]{2,0,1:T(8,128)(2,1)S(1)}, bf16[64,16,1]{2,0,1:T(8,128)(2,1)S(1)}, u32[]{:S(2)}, u32[]{:S(2)}) collective-permute-start(bf16[64,16,1]{2,0,1:T(8,128)(2,1)S(1)} %get-tuple-element.73), channel_id=1, source_target_pairs={{16,0},{32,16},{48,32},{64,48},{80,64},{96,80},{112,96},{128,112},... | collective-permute-start | bytes 6152 | tf_op jit(solution)/shard_map/ppermute | solution.py:20
  63.2 12.6 %collective-permute-start.7 = (bf16[64,1,130]{2,0,1:T(8,128)(2,1)S(1)}, bf16[64,1,130]{2,0,1:T(8,128)(2,1)S(1)}, u32[]{:S(2)}, u32[]{:S(2)}) collective-permute-start(bf16[64,1,130]{2,0,1:T(8,128)(2,1)S(1)} %get-tuple-element.66), channel_id=1, source_target_pairs={{1,0},{2,1},{3,2},{4,3},{5,4},{6,5},{7,6},{8,7},{9,8},{10,9},{11,1... | collective-permute-start | bytes 49928 | tf_op jit(solution)/shard_map/ppermute | solution.py:20
  65.1 10.7 %collective-permute-start.6 = (bf16[64,1,130]{2,0,1:T(8,128)(2,1)S(1)}, bf16[64,1,130]{2,0,1:T(8,128)(2,1)S(1)}, u32[]{:S(2)}, u32[]{:S(2)}) collective-permute-start(bf16[64,1,130]{2,0,1:T(8,128)(2,1)S(1)} %get-tuple-element.67), channel_id=1, source_target_pairs={{0,1},{1,2},{2,3},{3,4},{4,5},{5,6},{6,7},{7,8},{8,9},{9,10},{10,1... | collective-permute-start | bytes 49928 | tf_op jit(solution)/shard_map/ppermute | solution.py:17
  68.5 10.9 %all-to-all-start.1 = ((bf16[5,16,128]{2,0,1:T(8,128)(2,1)}), bf16[5,16,128]{2,0,1:T(8,128)(2,1)S(1)}, u32[]{:S(2)}, u32[]{:S(2)}) async-start(bf16[5,16,128]{2,0,1:T(8,128)(2,1)} %copy.453), calls=%async_computation.1 | async-start | bytes 65536 | tf_op jit(solution)/shard_map/all_to_all | solution.py:83
  82.2 7.3 %collective-permute-start.8 = (bf16[69,16,1]{2,1,0:T(8,128)(2,1)S(1)}, bf16[69,16,1]{2,1,0:T(8,128)(2,1)S(1)}, u32[]{:S(2)}, u32[]{:S(2)}) collective-permute-start(bf16[69,16,1]{2,1,0:T(8,128)(2,1)S(1)} %get-tuple-element.96), channel_id=1, source_target_pairs={{0,16},{16,32},{32,48},{48,64},{64,80},{80,96},{96,112},{112,128},... | collective-permute-start | bytes 6632 | tf_op jit(solution)/shard_map/ppermute | solution.py:17
  85.9 11.5 %collective-permute-start.9 = (bf16[69,16,1]{2,1,0:T(8,128)(2,1)S(1)}, bf16[69,16,1]{2,1,0:T(8,128)(2,1)S(1)}, u32[]{:S(2)}, u32[]{:S(2)}) collective-permute-start(bf16[69,16,1]{2,1,0:T(8,128)(2,1)S(1)} %get-tuple-element.97), channel_id=1, source_target_pairs={{16,0},{32,16},{48,32},{64,48},{80,64},{96,80},{112,96},{128,112},... | collective-permute-start | bytes 6632 | tf_op jit(solution)/shard_map/ppermute | solution.py:20
  97.9 5.5 %collective-permute-start.11 = (bf16[69,1,130]{2,1,0:T(2,128)(2,1)S(1)}, bf16[69,1,130]{2,1,0:T(2,128)(2,1)S(1)}, u32[]{:S(2)}, u32[]{:S(2)}) collective-permute-start(bf16[69,1,130]{2,1,0:T(2,128)(2,1)S(1)} %get-tuple-element.58), channel_id=1, source_target_pairs={{1,0},{2,1},{3,2},{4,3},{5,4},{6,5},{7,6},{8,7},{9,8},{10,9},{11,1... | collective-permute-start | bytes 53828 | tf_op jit(solution)/shard_map/ppermute | solution.py:20
  100.5 7.2 %collective-permute-start.10 = (bf16[69,1,130]{2,1,0:T(2,128)(2,1)S(1)}, bf16[69,1,130]{2,1,0:T(2,128)(2,1)S(1)}, u32[]{:S(2)}, u32[]{:S(2)}) collective-permute-start(bf16[69,1,130]{2,1,0:T(2,128)(2,1)S(1)} %get-tuple-element.59), channel_id=1, source_target_pairs={{0,1},{1,2},{2,3},{3,4},{4,5},{5,6},{6,7},{7,8},{8,9},{9,10},{10,1... | collective-permute-start | bytes 53828 | tf_op jit(solution)/shard_map/ppermute | solution.py:17
  116.7 9.1 %collective-permute-start.12 = (bf16[5,16,1]{2,1,0:T(8,128)(2,1)S(1)}, bf16[5,16,1]{2,1,0:T(8,128)(2,1)S(1)}, u32[]{:S(2)}, u32[]{:S(2)}) collective-permute-start(bf16[5,16,1]{2,1,0:T(8,128)(2,1)S(1)} %get-tuple-element.94), channel_id=1, source_target_pairs={{0,16},{16,32},{32,48},{48,64},{64,80},{80,96},{96,112},{112,128},... | collective-permute-start | bytes 488 | tf_op jit(solution)/shard_map/ppermute | solution.py:17
  121.1 8.7 %collective-permute-start.13 = (bf16[5,16,1]{2,1,0:T(8,128)(2,1)S(1)}, bf16[5,16,1]{2,1,0:T(8,128)(2,1)S(1)}, u32[]{:S(2)}, u32[]{:S(2)}) collective-permute-start(bf16[5,16,1]{2,1,0:T(8,128)(2,1)S(1)} %get-tuple-element.95), channel_id=1, source_target_pairs={{16,0},{32,16},{48,32},{64,48},{80,64},{96,80},{112,96},{128,112},... | collective-permute-start | bytes 488 | tf_op jit(solution)/shard_map/ppermute | solution.py:20
  124.2 14.8 %copy-start.3 = (bf16[9,64,5]{1,2,0:T(8,128)(2,1)S(1)}, bf16[9,64,5]{1,2,0:T(8,128)(2,1)}, u32[]{:S(2)}) copy-start(bf16[9,64,5]{1,2,0:T(8,128)(2,1)} %param.14) | copy-start | bytes 17284
  124.2 14.8 %copy-start.8 = (f32[64]{0:T(128)S(1)}, f32[64]{0:T(128)}, u32[]{:S(2)}) copy-start(f32[64]{0:T(128)} %param.15) | copy-start | bytes 772
  129.9 5.3 %collective-permute-start.15 = (bf16[5,1,130]{2,1,0:T(2,128)(2,1)S(1)}, bf16[5,1,130]{2,1,0:T(2,128)(2,1)S(1)}, u32[]{:S(2)}, u32[]{:S(2)}) collective-permute-start(bf16[5,1,130]{2,1,0:T(2,128)(2,1)S(1)} %get-tuple-element.76), channel_id=1, source_target_pairs={{1,0},{2,1},{3,2},{4,3},{5,4},{6,5},{7,6},{8,7},{9,8},{10,9},{11,1... | collective-permute-start | bytes 3908 | tf_op jit(solution)/shard_map/ppermute | solution.py:20
  131.8 6.5 %collective-permute-start.14 = (bf16[5,1,130]{2,1,0:T(2,128)(2,1)S(1)}, bf16[5,1,130]{2,1,0:T(2,128)(2,1)S(1)}, u32[]{:S(2)}, u32[]{:S(2)}) collective-permute-start(bf16[5,1,130]{2,1,0:T(2,128)(2,1)S(1)} %get-tuple-element.77), channel_id=1, source_target_pairs={{0,1},{1,2},{2,3},{3,4},{4,5},{5,6},{6,7},{7,8},{8,9},{9,10},{10,1... | collective-permute-start | bytes 3908 | tf_op jit(solution)/shard_map/ppermute | solution.py:17
  139.5 7.9 %collective-permute-start.16 = (bf16[64,16,1]{2,0,1:T(8,128)(2,1)S(1)}, bf16[64,16,1]{2,0,1:T(8,128)(2,1)S(1)}, u32[]{:S(2)}, u32[]{:S(2)}) collective-permute-start(bf16[64,16,1]{2,0,1:T(8,128)(2,1)S(1)} %get-tuple-element.70), channel_id=1, source_target_pairs={{0,16},{16,32},{32,48},{48,64},{64,80},{80,96},{96,112},{112,128},... | collective-permute-start | bytes 6152 | tf_op jit(solution)/shard_map/ppermute | solution.py:17
  144.0 11.3 %collective-permute-start.17 = (bf16[64,16,1]{2,0,1:T(8,128)(2,1)S(1)}, bf16[64,16,1]{2,0,1:T(8,128)(2,1)S(1)}, u32[]{:S(2)}, u32[]{:S(2)}) collective-permute-start(bf16[64,16,1]{2,0,1:T(8,128)(2,1)S(1)} %get-tuple-element.71), channel_id=1, source_target_pairs={{16,0},{32,16},{48,32},{64,48},{80,64},{96,80},{112,96},{128,112},... | collective-permute-start | bytes 6152 | tf_op jit(solution)/shard_map/ppermute | solution.py:20
  155.4 6.9 %collective-permute-start.19 = (bf16[64,1,130]{2,0,1:T(8,128)(2,1)S(1)}, bf16[64,1,130]{2,0,1:T(8,128)(2,1)S(1)}, u32[]{:S(2)}, u32[]{:S(2)}) collective-permute-start(bf16[64,1,130]{2,0,1:T(8,128)(2,1)S(1)} %get-tuple-element.62), channel_id=1, source_target_pairs={{1,0},{2,1},{3,2},{4,3},{5,4},{6,5},{7,6},{8,7},{9,8},{10,9},{11,1... | collective-permute-start | bytes 49928 | tf_op jit(solution)/shard_map/ppermute | solution.py:20
  157.4 6.8 %collective-permute-start.18 = (bf16[64,1,130]{2,0,1:T(8,128)(2,1)S(1)}, bf16[64,1,130]{2,0,1:T(8,128)(2,1)S(1)}, u32[]{:S(2)}, u32[]{:S(2)}) collective-permute-start(bf16[64,1,130]{2,0,1:T(8,128)(2,1)S(1)} %get-tuple-element.63), channel_id=1, source_target_pairs={{0,1},{1,2},{2,3},{3,4},{4,5},{5,6},{6,7},{7,8},{8,9},{9,10},{10,1... | collective-permute-start | bytes 49928 | tf_op jit(solution)/shard_map/ppermute | solution.py:17
  166.7 6.9 %collective-permute-start.20 = (bf16[69,16,1]{2,1,0:T(8,128)(2,1)S(1)}, bf16[69,16,1]{2,1,0:T(8,128)(2,1)S(1)}, u32[]{:S(2)}, u32[]{:S(2)}) collective-permute-start(bf16[69,16,1]{2,1,0:T(8,128)(2,1)S(1)} %get-tuple-element.68), channel_id=1, source_target_pairs={{0,16},{16,32},{32,48},{48,64},{64,80},{80,96},{96,112},{112,128},... | collective-permute-start | bytes 6632 | tf_op jit(solution)/shard_map/ppermute | solution.py:17
  170.0 11.5 %collective-permute-start.21 = (bf16[69,16,1]{2,1,0:T(8,128)(2,1)S(1)}, bf16[69,16,1]{2,1,0:T(8,128)(2,1)S(1)}, u32[]{:S(2)}, u32[]{:S(2)}) collective-permute-start(bf16[69,16,1]{2,1,0:T(8,128)(2,1)S(1)} %get-tuple-element.69), channel_id=1, source_target_pairs={{16,0},{32,16},{48,32},{64,48},{80,64},{96,80},{112,96},{128,112},... | collective-permute-start | bytes 6632 | tf_op jit(solution)/shard_map/ppermute | solution.py:20
  182.0 5.3 %collective-permute-start.23 = (bf16[69,1,130]{2,1,0:T(2,128)(2,1)S(1)}, bf16[69,1,130]{2,1,0:T(2,128)(2,1)S(1)}, u32[]{:S(2)}, u32[]{:S(2)}) collective-permute-start(bf16[69,1,130]{2,1,0:T(2,128)(2,1)S(1)} %get-tuple-element.54), channel_id=1, source_target_pairs={{1,0},{2,1},{3,2},{4,3},{5,4},{6,5},{7,6},{8,7},{9,8},{10,9},{11,1... | collective-permute-start | bytes 53828 | tf_op jit(solution)/shard_map/ppermute | solution.py:20
  183.9 7.2 %collective-permute-start.22 = (bf16[69,1,130]{2,1,0:T(2,128)(2,1)S(1)}, bf16[69,1,130]{2,1,0:T(2,128)(2,1)S(1)}, u32[]{:S(2)}, u32[]{:S(2)}) collective-permute-start(bf16[69,1,130]{2,1,0:T(2,128)(2,1)S(1)} %get-tuple-element.55), channel_id=1, source_target_pairs={{0,1},{1,2},{2,3},{3,4},{4,5},{5,6},{6,7},{7,8},{8,9},{9,10},{10,1... | collective-permute-start | bytes 53828 | tf_op jit(solution)/shard_map/ppermute | solution.py:17
  (3 other events, 4.0 us)
where the time goes:
time: 202 us; the launch traced here: 201 us
  starting transfers between devices  86 us (43%)
  waiting for transfers between devices  62.1 us (31%)
  other arithmetic  19 us (9%)
  local copies, waits for them, and re-layouts  16.4 us (8%)
  matrix products  16.1 us (8%)
    ppermute x12, starting transfers between devices, padded_2(): lax.ppermute(lax.slice_in_dim(block, block.shape[dim] - width, None, axis...  44.7 us
    ppermute x12, waiting for transfers between devices, padded_2(): lax.ppermute(lax.slice_in_dim(block, 0, width, axis=dim), axis, backward)  40.2 us
    ppermute x12, starting transfers between devices, padded_2(): lax.ppermute(lax.slice_in_dim(block, 0, width, axis=dim), axis, backward)  25.6 us
    ppermute x12, waiting for transfers between devices, padded_2(): lax.ppermute(lax.slice_in_dim(block, block.shape[dim] - width, None, axis...  20.7 us
    all_to_all x1, starting transfers between devices, on_device(): lax.all_to_all(sent_cells, 'lat', split_axis=1, concat_axis=1, tiled=True)  11.2 us
    dot_general x4, matrix products, on_device(): jnp.dot(row_tables[upper], flat_grid, precision=highest, preferred_elemen...  5.46 us
    dot_general x4, matrix products, on_device(): jnp.dot(row_tables[upper].T, spread, precision=highest, preferred_element...  5.31 us
    dot_general x6, matrix products, stencil(): jnp.einsum('koc,kcyx->oyx', weight, windows, preferred_element_type=jnp.f...  5.03 us
  transfers between devices with their start and end apart: 26, of which 15 were waited for; matrix products, arithmetic and copies ran while one was open for 9% of the time, Pallas kernels for 0%

commit v1 on v0

v1 whole, which is shorter than its diff:
```python
import jax
import jax.numpy as jnp
from jax import lax
from jax.experimental import pallas as pl
from jax.experimental.pallas import tpu as pltpu
from jax.sharding import PartitionSpec as P

DAYS = 5
ROWS = 16
COLS = 128
LANES = 128
HID = 64
TRACK = 512
HALO = 8
BASES = 25
CHUNK = 2048
FIRST = 7
TILES = 60
F32 = jnp.float32
BF16 = jnp.bfloat16


def nt_dot(left, right):
    return lax.dot_general(left, right, (((1,), (1,)), ((), ())), preferred_element_type=F32)


def lane_roll(value, shift):
    return pltpu.roll(value, shift % value.shape[1], 1)


def day_rows(low_ref, mid_ref, high_ref, row):
    if row < 0:
        picked = low_ref[pl.ds(row + HALO, DAYS, stride=HALO), :]
    elif row < ROWS:
        picked = mid_ref[pl.ds(row, DAYS, stride=ROWS), :]
    else:
        picked = high_ref[pl.ds(row - ROWS, DAYS, stride=HALO), :]
    return jnp.concatenate([picked, jnp.zeros((8 - DAYS, LANES), F32)], axis=0)


def adjoint_terms(sums_ref, base, here, above):
    low = pl.ds(5 * base, 8)
    high = pl.ds(LANES + 5 * base, 8)
    here_right = lane_roll(here, -1)
    above_right = lane_roll(above, -1)
    s01 = sums_ref[1, low, :]
    s02 = sums_ref[2, low, :]
    s03 = sums_ref[3, low, :]
    s12 = sums_ref[2, high, :]
    s13 = sums_ref[3, high, :]
    s23 = sums_ref[6, low, :]
    g0 = sums_ref[0, low, :] * here + s01 * here_right + s02 * above + s03 * above_right - sums_ref[4, low, :]
    g1 = s01 * here + sums_ref[1, high, :] * here_right + s12 * above + s13 * above_right - sums_ref[4, high, :]
    g2 = s02 * here + s12 * here_right + sums_ref[5, low, :] * above + s23 * above_right - sums_ref[7, low, :]
    g3 = s03 * here + s13 * here_right + s23 * above + sums_ref[6, high, :] * above_right - sums_ref[7, high, :]
    return g0 + lane_roll(g1, 1), g2 + lane_roll(g3, 1)


def build_kernel(
    lat_ref, track_ref, mid_ref, low_ref, high_ref, sums_ref, adjoint_ref, east_ref, west_ref, rw_ref, cw_ref, ce_ref, edge_ref
):
    base_row = (lat_ref[0] * ROWS - 5).astype(F32)
    entry = lax.broadcasted_iota(jnp.int32, (LANES, TRACK), 0).astype(F32)
    sums_ref[...] = jnp.zeros_like(sums_ref)
    edge_ref[...] = jnp.zeros_like(edge_ref)

    def chunk_step(chunk, carry):
        for half in range(2):
            both = track_ref[pl.ds(pl.multiple_of(chunk * 32 + half * 16, 16), 16), :].astype(F32)
            for part in range(2):
                block = both[8 * part : 8 * part + 8]
                at = (2 * half + part) * TRACK
                time = block[5:6]
                offset = block[6:7] - base_row
                column = block[7:8]
                inside = (offset >= 0.0) & (offset < float(BASES))
                key = jnp.where(inside, offset * 5.0 + time, -1.0)
                row_hit = entry == key
                col_hit = entry == column
                for k in range(4):
                    rw_ref[128 * k : 128 * k + 128, at : at + TRACK] = jnp.where(
                        row_hit, block[1 + k : 2 + k], 0.0
                    ).astype(BF16)
                for k in range(5):
                    source = (1 + k) % 5
                    cw_ref[128 * k : 128 * k + 128, at : at + TRACK] = jnp.where(
                        col_hit, block[source : source + 1], 0.0
                    ).astype(BF16)
                ce_ref[:, at : at + TRACK] = jnp.concatenate(
                    [
                        jnp.where(column == float(COLS - 2), block, 0.0),
                        jnp.where(column == 0.0, block, 0.0),
                    ],
                    axis=0,
                ).astype(BF16)
        first = nt_dot(rw_ref[0:256, :], cw_ref[...])
        for k in range(5):
            sums_ref[k] += first[:, 128 * k : 128 * k + 128]
        second = nt_dot(rw_ref[256:512, :], cw_ref[256:640, :])
        for k in range(3):
            sums_ref[5 + k] += second[:, 128 * k : 128 * k + 128]
        edge_ref[...] += nt_dot(ce_ref[...], rw_ref[...])
        return carry

    lax.fori_loop(0, track_ref.shape[0] * TRACK // (8 * CHUNK), chunk_step, 0)

    lane_group = lax.broadcasted_iota(jnp.int32, (8, LANES), 1) // 8

    def pack(slot, row, east, west):
        return (
            jnp.where(lane_group == slot, lane_roll(row, 8 * slot + 8), east),
            jnp.where(lane_group == slot, lane_roll(row, 8 * slot), west),
        )

    zero = jnp.zeros((8, LANES), F32)
    for part in range(2):
        east, west = zero, zero
        for slot in range(16):
            row = part * 16 + slot - 6
            if row < ROWS + 6:
                east, west = pack(slot, day_rows(low_ref, mid_ref, high_ref, row), east, west)
        east_ref[8 * part : 8 * part + 8, :] = east
        west_ref[8 * part : 8 * part + 8, :] = west
    packed = [[zero, zero], [zero, zero]]
    here = day_rows(low_ref, mid_ref, high_ref, -5)
    carried = zero
    for base in range(BASES):
        above = day_rows(low_ref, mid_ref, high_ref, base - 4)
        now, later = adjoint_terms(sums_ref, base, here, above)
        if base > 0:
            total = carried + now
            adjoint_ref[base - 1] = total
            part, slot = divmod(base - 1, 16)
            packed[part] = list(pack(slot, total, *packed[part]))
        carried = later
        here = above
    for part in range(2):
        east_ref[16 + 8 * part : 24 + 8 * part, :] = packed[part][0]
        west_ref[16 + 8 * part : 24 + 8 * part, :] = packed[part][1]
    east_ref[32:40, :] = edge_ref[0:8, 128:256]
    east_ref[40:48, :] = edge_ref[0:8, 384:512]
    west_ref[32:40, :] = edge_ref[8:16, 0:128]
    west_ref[40:48, :] = edge_ref[8:16, 256:384]


def solve_kernel(
    lat_ref,
    mid_ref,
    low_ref,
    high_ref,
    sums_ref,
    adjoint_ref,
    fromw_ref,
    frome_ref,
    w_in_ref,
    w_out_ref,
    w_gate_ref,
    w_inc_ref,
    est_out_ref,
    cell_out_ref,
    est_ref,
    grad_ref,
    minus_ref,
    plus_ref,
    latent_ref,
    spread_ref,
    cell_ref,
    hidden_ref,
    hid16_ref,
    edge_ref,
    *,
    lat_count,
):
    lat = lat_ref[0]
    lane = lax.broadcasted_iota(jnp.int32, (8, LANES), 1)
    zero = jnp.zeros((8, LANES), F32)

    def tile(index, count=1):
        return slice(index * LANES, (index + count) * LANES)

    def inside(first_tile, count):
        place = lax.broadcasted_iota(jnp.int32, (1, count * LANES), 1) + (first_tile * LANES + 64)
        row = lax.shift_right_logical(place, 8) - FIRST + lat * ROWS
        return (row >= 0) & (row < lat_count * ROWS)

    def unpack(ref, first, row_slot, east):
        part, slot = divmod(row_slot, 16)
        value = ref[first + 8 * part : first + 8 * part + 8, :]
        return lane_roll(value, -8 * slot if east else -8 * slot - 8)

    def side(first, here_slot, next_slot, count):
        right = unpack(frome_ref, first, here_slot, True) if 0 <= here_slot < count else zero
        left = unpack(fromw_ref, first, next_slot, False) if 0 <= next_slot < count else zero
        return jnp.where(lane < 8, right, jnp.where(lane >= 120, left, 0.0))

    est_ref[:, 0:LANES] = zero
    est_ref[:, tile(58, 2)] = jnp.zeros((8, 2 * LANES), F32)
    for block in range(0, 29):
        row = block - FIRST
        if block >= 1:
            est_ref[:, tile(2 * block)] = day_rows(low_ref, mid_ref, high_ref, row)
        est_ref[:, tile(2 * block + 1)] = side(0, row + 6, row + 7, 28)

    ones = jnp.where(lax.broadcasted_iota(jnp.int32, (8, 256), 0) < 3, 1.0, 0.0).astype(F32)

    def shifted(ref, first_tile, count):
        value = ref[:, tile(first_tile, count)]
        minus_ref[:, tile(first_tile, count)] = lane_roll(value, 1)
        plus_ref[:, tile(first_tile, count)] = lane_roll(value, -1)

    def windows(ref, tiles):
        pieces = []
        for a in (-2, 0, 2):
            for source in (minus_ref, ref, plus_ref):
                pieces.append(jnp.concatenate([source[:, tile(t + a)] for t in tiles], axis=1))
        return jnp.concatenate(pieces + [ones], axis=0).astype(BF16)

    def prior(first_row, last_row):
        low_tile = 2 * (first_row - 1 + FIRST) - 1
        high_tile = 2 * (last_row + 1 + FIRST) + 2
        shifted(est_ref, low_tile - 2, high_tile - low_tile + 5)
        for t in range(low_tile, high_tile, 2):
            value = jnp.dot(w_in_ref[...], windows(est_ref, (t, t + 1)), preferred_element_type=F32)
            value = jnp.maximum(value, 0.0)
            if t + 2 > 2 * (ROWS + FIRST) - 2 or t < 2 * FIRST:
                value = jnp.where(inside(t, 2), value, 0.0)
            latent_ref[:, tile(t, 2)] = value.astype(BF16)
            spread_ref[:, tile(t, 2)] = jnp.dot(w_out_ref[...], latent_ref[:, tile(t, 2)], preferred_element_type=F32)
        out_tile = low_tile + 2
        count = 2 * (last_row + FIRST) + 2 - out_tile
        columns = []
        for b in range(3):
            total = None
            for a in range(3):
                k = 8 * (3 * a + b)
                piece = spread_ref[k : k + 8, tile(out_tile + 2 * a - 2, count)]
                total = piece if total is None else total + piece
            columns.append(total)
        grad_ref[:, tile(out_tile, count)] = -(columns[1] + lane_roll(columns[0], 1) + lane_roll(columns[2], -1))

    prior(-4, 19)
    for t in range(5, 54):
        block = t // 2
        row = block - FIRST
        if t % 2 == 0:
            extra = adjoint_ref[row + 4]
        else:
            extra = side(16, row + 4, row + 5, 24)
        total = est_ref[:, tile(t)] + grad_ref[:, tile(t)] + extra
        if row < 0 or row >= ROWS - 1:
            total = jnp.where(inside(t, 1), total, 0.0)
        grad_ref[:, tile(t)] = total
    grad_ref[:, tile(54)] = zero
    shifted(grad_ref, 5, 50)
    for t in range(7, 53, 2):
        sums = jnp.dot(w_gate_ref[HID:, 0:80], windows(grad_ref, (t, t + 1)), preferred_element_type=F32)
        gate_in = 0.5 * jnp.tanh(sums[0:HID]) + 0.5
        gate_out = 0.5 * jnp.tanh(sums[HID : 2 * HID]) + 0.5
        cell = gate_in * jnp.tanh(sums[2 * HID : 3 * HID])
        hidden = gate_out * jnp.tanh(cell)
        if t + 2 > 2 * (ROWS + FIRST) - 2 or t < 2 * FIRST:
            hidden = jnp.where(inside(t, 2), hidden, 0.0)
        cell_ref[:, tile(t, 2)] = cell
        hidden_ref[:, tile(t, 2)] = hidden
        update = jnp.dot(w_inc_ref[...], hidden.astype(BF16), preferred_element_type=F32)
        est_ref[:, tile(t, 2)] -= update[0:8]

    for group in range(0, HID, 16):
        value = hidden_ref[group : group + 16, tile(11, 37)]
        hid16_ref[0, group : group + 16, tile(11, 37)] = lane_roll(value, 1).astype(BF16)
        hid16_ref[1, group : group + 16, tile(11, 37)] = value.astype(BF16)
        hid16_ref[2, group : group + 16, tile(11, 37)] = lane_roll(value, -1).astype(BF16)

    prior(-1, 16)
    edges = jnp.concatenate(
        [fromw_ref[32:48, :], frome_ref[32:48, :], jnp.zeros((LANES - 32, LANES), F32)], axis=0
    )
    edge_ref[...] = edges.T
    carried = zero
    carried_w = zero
    carried_e = zero
    side_w = {}
    side_e = {}
    for row in range(-2, 17):
        base = row + 5
        block = row + FIRST
        now, later = adjoint_terms(sums_ref, base, est_ref[:, tile(2 * block)], est_ref[:, tile(2 * block + 2)])
        if row > -2:
            grad_ref[:, tile(2 * block)] += est_ref[:, tile(2 * block)] + carried + now
        carried = later
        factors = edge_ref[pl.ds(5 * base, 8), :]

        def edge_term(first, e0, e1, e2, e3):
            def factor(j):
                return factors[:, first + j : first + j + 1]

            return factor(1) * e0 + factor(2) * e1 + factor(3) * e2 + factor(4) * e3 - factor(0)

        here = est_ref[:, tile(2 * block - 1)]
        above = est_ref[:, tile(2 * block + 1)]
        far_here, far_above = lane_roll(here, 1), lane_roll(above, 1)
        side_w[row] = carried_w + edge_term(0, far_here, here, far_above, above)
        carried_w = edge_term(8, far_here, here, far_above, above)
        here = above
        above = est_ref[:, tile(2 * block + 3)]
        far_here, far_above = lane_roll(here, -1), lane_roll(above, -1)
        side_e[row] = carried_e + edge_term(16, here, far_here, above, far_above)
        carried_e = edge_term(24, here, far_here, above, far_above)
    for row in range(-2, 17):
        block = row + FIRST
        t = 2 * block + 1
        right = side_e[row] if row > -2 else zero
        left = side_w[row + 1] if row < 16 else zero
        grad_ref[:, tile(t)] += est_ref[:, tile(t)] + jnp.where(lane < 64, right, left)
    for t in (11, 12, 13, 45, 46, 47):
        grad_ref[:, tile(t)] = jnp.where(inside(t, 1), grad_ref[:, tile(t)], 0.0)
    shifted(grad_ref, 11, 37)
    for row in range(0, ROWS, 2):
        tiles = (2 * (row + FIRST), 2 * (row + FIRST) + 2)
        pieces = [windows(grad_ref, tiles)]
        for a in (-2, 0, 2):
            for b in range(3):
                pieces.append(jnp.concatenate([hid16_ref[b, :, tile(t + a)] for t in tiles], axis=1))
        sums = jnp.dot(w_gate_ref[...], jnp.concatenate(pieces, axis=0), preferred_element_type=F32)
        old = jnp.concatenate([cell_ref[:, tile(t)] for t in tiles], axis=1)
        forget = 0.5 * jnp.tanh(sums[0:HID]) + 0.5
        gate_in = 0.5 * jnp.tanh(sums[HID : 2 * HID]) + 0.5
        gate_out = 0.5 * jnp.tanh(sums[2 * HID : 3 * HID]) + 0.5
        cell = forget * old + gate_in * jnp.tanh(sums[3 * HID :])
        hidden = gate_out * jnp.tanh(cell)
        update = jnp.dot(w_inc_ref[...], hidden.astype(BF16), preferred_element_type=F32)
        for k in range(2):
            cell_out_ref[pl.ds(row + k, HID, stride=ROWS), :] = cell[:, tile(k)]
            final = est_ref[:, tile(tiles[k])] - update[0:8, tile(k)]
            est_out_ref[pl.ds(row + k, DAYS, stride=ROWS), :] = final[0:DAYS]


def bias_pieces(bias):
    high = lax.reduce_precision(bias, 8, 7)
    middle = lax.reduce_precision(bias - high, 8, 7)
    low = bias - high - middle
    pieces = jnp.stack([high, middle, low], axis=1).astype(BF16)
    return jnp.pad(pieces, ((0, 0), (0, 5)))


def by_offset(weight):
    padded = jnp.pad(weight, ((0, 0), (0, 0), (0, 8 - DAYS)))
    return jnp.transpose(padded, (1, 0, 2)).reshape(weight.shape[1], 72)


def on_device(
    state,
    prior_in,
    prior_bias,
    prior_out,
    lstm_weight,
    lstm_bias,
    lstm_out,
    obs_value,
    obs_weight,
    obs_tile,
    obs_time,
    obs_row,
    obs_col,
):
    lat_count = lax.axis_size("lat")
    lon_count = lax.axis_size("lon")
    keys = jnp.stack([obs_time, obs_tile[:, 0] * ROWS + obs_row, obs_col]).astype(F32)
    track = jnp.concatenate([obs_value[None], obs_weight, keys], axis=0).astype(BF16)
    gathered = lax.all_gather(track, "lat", axis=0, tiled=True)

    up = [(i, i + 1) for i in range(lat_count - 1)]
    down = [(i + 1, i) for i in range(lat_count - 1)]
    low = lax.ppermute(state[:, ROWS - HALO :], "lat", up).reshape(DAYS * HALO, LANES)
    high = lax.ppermute(state[:, :HALO], "lat", down).reshape(DAYS * HALO, LANES)
    mid = state.reshape(DAYS * ROWS, LANES)
    lat = lax.axis_index("lat").astype(jnp.int32).reshape(1)

    w_in = jnp.concatenate([by_offset(prior_in), bias_pieces(prior_bias)], axis=1)
    w_out = jnp.pad(
        jnp.pad(prior_out, ((0, 0), (0, 8 - DAYS), (0, 0))).reshape(72, HID), ((0, 8), (0, 0))
    )
    half = jnp.concatenate([jnp.full((3 * HID,), 0.5, F32), jnp.ones((HID,), F32)])
    gates = jnp.concatenate(
        [lstm_weight[:, HID : 2 * HID], lstm_weight[:, :HID], lstm_weight[:, 2 * HID :]], axis=1
    ) * half.astype(BF16)[None, :, None]
    gate_bias = jnp.concatenate([lstm_bias[HID : 2 * HID], lstm_bias[:HID], lstm_bias[2 * HID :]]) * half
    w_gate = jnp.concatenate(
        [
            by_offset(gates[:, :, :DAYS]),
            bias_pieces(gate_bias),
            jnp.transpose(gates[:, :, DAYS:], (1, 0, 2)).reshape(4 * HID, 9 * HID),
        ],
        axis=1,
    )
    w_inc = jnp.pad(lstm_out, ((0, 16 - DAYS), (0, 0)))

    smem = pl.BlockSpec(memory_space=pltpu.SMEM)
    vmem = pl.BlockSpec(memory_space=pltpu.VMEM)
    sums, adjoint, to_east, to_west = pl.pallas_call(
        build_kernel,
        out_shape=(
            jax.ShapeDtypeStruct((8, 256, LANES), F32),
            jax.ShapeDtypeStruct((24, 8, LANES), F32),
            jax.ShapeDtypeStruct((48, LANES), F32),
            jax.ShapeDtypeStruct((48, LANES), F32),
        ),
        in_specs=[smem, vmem, vmem, vmem, vmem],
        out_specs=(vmem, vmem, vmem, vmem),
        scratch_shapes=[
            pltpu.VMEM((512, CHUNK), BF16),
            pltpu.VMEM((640, CHUNK), BF16),
            pltpu.VMEM((16, CHUNK), BF16),
            pltpu.VMEM((16, 512), F32),
        ],
        compiler_params=pltpu.CompilerParams(vmem_limit_bytes=32 * 1024 * 1024),
        name="build",
    )(lat, gathered, mid, low, high)

    east = [(i, (i + 1) % lon_count) for i in range(lon_count)]
    west = [(target, source) for source, target in east]
    from_west = lax.ppermute(to_east, "lon", east)
    from_east = lax.ppermute(to_west, "lon", west)

    def solve(*refs):
        solve_kernel(*refs, lat_count=lat_count)

    width = TILES * LANES
    estimate, cell_state = pl.pallas_call(
        solve,
        out_shape=(
            jax.ShapeDtypeStruct((DAYS * ROWS, LANES), F32),
            jax.ShapeDtypeStruct((HID * ROWS, LANES), F32),
        ),
        in_specs=[smem] + [vmem] * 11,
        out_specs=(vmem, vmem),
        scratch_shapes=[
            pltpu.VMEM((8, width), F32),
            pltpu.VMEM((8, width), F32),
            pltpu.VMEM((8, width), F32),
            pltpu.VMEM((8, width), F32),
            pltpu.VMEM((HID, width), BF16),
            pltpu.VMEM((80, width), F32),
            pltpu.VMEM((HID, width), F32),
            pltpu.VMEM((HID, width), F32),
            pltpu.VMEM((3, HID, width), BF16),
            pltpu.VMEM((LANES, LANES), F32),
        ],
        compiler_params=pltpu.CompilerParams(vmem_limit_bytes=32 * 1024 * 1024),
        name="solve",
    )(lat, mid, low, high, sums, adjoint, from_west, from_east, w_in, w_out, w_gate, w_inc)
    return (
        estimate.reshape(DAYS, ROWS, LANES),
        cell_state.reshape(HID, ROWS, LANES),
    )


def solution(mesh):
    return jax.shard_map(
        on_device,
        mesh=mesh,
        in_specs=(
            P(None, "lat", "lon"),
            P(),
            P(),
            P(),
            P(),
            P(),
            P(),
            P(("lon", "lat")),
            P(None, ("lon", "lat")),
            P(("lon", "lat"), None),
            P(("lon", "lat")),
            P(("lon", "lat")),
            P(("lon", "lat")),
        ),
        out_specs=(P(None, "lat", "lon"), P(None, "lat", "lon")),
        check_vma=False,
    )
```

time: 202 us -> 91.8 us (0.45)
  starting transfers between devices: 86 us -> 28 us
  waiting for transfers between devices: 62.1 us -> 6.72 us
  blocking collectives: 0 us -> 26.8 us
  Pallas kernels: 0 us -> 21.4 us
  other arithmetic: 19 us -> 0.71 us
  matrix products: 16.1 us -> 0 us
  local copies, waits for them, and re-layouts: 16.4 us -> 6.7 us
    ppermute x24 -> x4, waiting for transfers between devices: 60.9 us -> 6.72 us  [the longest x1 6.71 us: on_device(): from_east = lax.ppermute(to_west, 'lon', west)]
    ppermute x24 -> x4, starting transfers between devices: 70.2 us -> 28 us  [the longest x1 13.3 us: on_device(): from_west = lax.ppermute(to_east, 'lon', east)]
    all_gather x0 -> x1, blocking collectives: none -> 26.8 us  [on_device(): gathered = lax.all_gather(track, 'lat', axis=0, tiled=True)]
    pallas_call x0 -> x2, Pallas kernels: none -> 21.4 us  [the longest x1 12.7 us: on_device(): pl.pallas_call(solve, out_shape=(jax.ShapeDtypeStruct((DAYS * ROWS, LANES...]
    dot_general x16 -> x0, matrix products: 16.1 us -> none  [the longest x4 5.46 us: on_device(): jnp.dot(row_tables[upper], flat_grid, precision=highest, preferred_elemen...]
    all_to_all x2 -> x0, starting transfers between devices: 15.8 us -> none  [the longest x1 11.2 us: on_device(): lax.all_to_all(sent_cells, 'lat', split_axis=1, concat_axis=1, tiled=True)]
    scatter x2 -> x0, local copies, waits for them, and re-layouts: 4.98 us -> none  [the longest x1 3.01 us: on_device(): sent_cells = jnp.zeros((lat_count * CAP,), jnp.int32).at[position].set(fl...]
    add x4 -> x1, other arithmetic: 4.58 us -> 0.01 us  [on_device(): obs_tile[:, 0] * ROWS + obs_row]
  transfers between devices with their start and end apart: 26 -> 4, of which waited for: 15 -> 1; matrix products, arithmetic and copies ran while one was open for 9% -> 3% of each run, Pallas kernels for 0% -> 0%
where the time goes in v1:
time: 91.8 us; the launch traced here: 91.3 us
  starting transfers between devices  28 us (31%)
  blocking collectives  26.8 us (29%)
  Pallas kernels  21.4 us (23%)
  waiting for transfers between devices  6.72 us (7%)
  local copies, waits for them, and re-layouts  6.7 us (7%)
  between operations  0.92 us (1%)
    all_gather x1, blocking collectives, on_device(): gathered = lax.all_gather(track, 'lat', axis=0, tiled=True)  26.8 us
    ppermute x1, starting transfers between devices, on_device(): from_west = lax.ppermute(to_east, 'lon', east)  13.3 us
    pallas_call x1, Pallas kernels, on_device(): pl.pallas_call(solve, out_shape=(jax.ShapeDtypeStruct((DAYS * ROWS, LANES...  12.7 us
    ppermute x1, starting transfers between devices, on_device(): lax.ppermute(state[:, :HALO], 'lat', down).reshape(DAYS * HALO, LANES)  10.9 us
    pallas_call x1, Pallas kernels, on_device(): pl.pallas_call(build_kernel, out_shape=(jax.ShapeDtypeStruct((8, 256, LAN...  8.73 us
    ppermute x1, waiting for transfers between devices, on_device(): from_east = lax.ppermute(to_west, 'lon', west)  6.71 us
    unnamed x30, local copies, waits for them, and re-layouts  2.98 us
    ppermute x1, starting transfers between devices, on_device(): from_east = lax.ppermute(to_west, 'lon', west)  1.92 us
  transfers between devices with their start and end apart: 4, of which 1 were waited for; matrix products, arithmetic and copies ran while one was open for 3% of the time, Pallas kernels for 0%

profile of v1, /device:TPU:31, one launch (start us, length us, event | category | flops | bytes accessed | tf_op | source)
XLA Modules:
  0.0 91.3 jit_solution(11727115335052815408)
XLA Ops:
  0.6 0.8 fusion.14
  1.4 10.9 %collective-permute-start.1 = (f32[5,8,128]{2,1,0:T(8,128)S(1)}, f32[5,8,128]{2,1,0:T(8,128)S(1)}, u32[]{:S(2)}, u32[]{:S(2)}) collective-permute-start(f32[5,8,128]{2,1,0:T(8,128)S(1)} %get-tuple-element.18), channel_id=1, source_target_pairs={{1,0},{2,1},{3,2},{4,3},{5,4},{6,5},{7,6},{8,7},{9,8},{10,9},{11,1... | collective-permute-start | bytes 61448 | tf_op jit(solution)/shard_map/ppermute | solution.py:375
  12.4 1.9 %collective-permute-start = (f32[5,8,128]{2,1,0:T(8,128)S(1)}, f32[5,8,128]{2,1,0:T(8,128)S(1)}, u32[]{:S(2)}, u32[]{:S(2)}) collective-permute-start(f32[5,8,128]{2,1,0:T(8,128)S(1)} %get-tuple-element.19), channel_id=1, source_target_pairs={{0,1},{1,2},{2,3},{3,4},{4,5},{5,6},{6,7},{7,8},{8,9},{9,10},{10,1... | collective-permute-start | bytes 61448 | tf_op jit(solution)/shard_map/ppermute | solution.py:374
  14.3 0.7 slice_bitcast_fusion
  15.0 0.8 slice_bitcast_fusion.2
  15.8 0.0 copy-start.11
  15.9 0.1 fusion.13
  16.0 0.5 copy-done.8
  16.6 0.1 reduce-precision_convert_fusion.1
  16.7 0.1 copy.35
  16.9 0.5 slice-done
  17.4 0.1 copy-done.14
  17.6 0.2 maximum_multiply_fusion
  17.8 0.1 slice.42
  17.8 0.6 copy-done.12
  18.4 0.1 fusion.4
  18.5 0.1 copy.36
  18.6 0.2 copy.37
  18.8 0.5 copy-done.5
  19.3 0.7 copy-done.7
  20.0 0.0 copy-done.6
  20.0 0.2 fusion.3.refs_10_
  20.3 26.8 %all_gather.3.track_ref = bf16[128,512]{1,0:T(8,128)(2,1)S(1)} all-gather(bf16[8,512]{1,0:T(8,128)(2,1)S(1)} %pad_maximum_fusion), channel_id=1, replica_groups=mesh['lon'=32,'lat'=16] {'lat'}, dimensions={0}, use_global_device_ids=true | all-gather | bytes 139264 | tf_op jit(solution)/shard_map/all_gather | solution.py:370
  47.1 0.1 copy.33
  47.2 0.1 copy.34
  47.3 0.6 copy-done
  47.8 8.7 %build.1 = (f32[8,256,128]{2,1,0:T(8,128)S(1)}, f32[24,8,128]{2,1,0:T(8,128)S(1)}, f32[48,128]{1,0:T(8,128)S(1)}, f32[48,128]{1,0:T(8,128)S(1)}) custom-call(s32[1]{0:T(128)} %bitcast.lat_ref.refs_0_, bf16[128,512]{1,0:T(8,128)(2,1)S(1)} %all_gather.3.track_ref, f32[80,128]{1,0:T(8,128)S(1)} %bitcast.35, f32[40,128]{1,0:T(8,128)S(1)} %bitcast.39, ...), custom_call_target="tpu_custom_call" | custom-call | tf_op jit(solution)/shard_map/build/pallas_call | solution.py:400
  56.6 13.3 %collective-permute-start.2 = (f32[48,128]{1,0:T(8,128)S(1)}, f32[48,128]{1,0:T(8,128)S(1)}, u32[]{:S(2)}, u32[]{:S(2)}) collective-permute-start(f32[48,128]{1,0:T(8,128)S(1)} %get-tuple-element.10), channel_id=1, source_target_pairs={{0,16},{16,32},{32,48},{48,64},{64,80},{80,96},{96,112},{112,128},... | collective-permute-start | bytes 73736 | tf_op jit(solution)/shard_map/ppermute | solution.py:422
  69.9 1.9 %collective-permute-start.3 = (f32[48,128]{1,0:T(8,128)S(1)}, f32[48,128]{1,0:T(8,128)S(1)}, u32[]{:S(2)}, u32[]{:S(2)}) collective-permute-start(f32[48,128]{1,0:T(8,128)S(1)} %get-tuple-element.11), channel_id=1, source_target_pairs={{16,0},{32,16},{48,32},{64,48},{80,64},{96,80},{112,96},{128,112},... | collective-permute-start | bytes 73736 | tf_op jit(solution)/shard_map/ppermute | solution.py:423
  71.8 0.1 fusion.6.refs_8_
  71.9 6.7 %collective-permute-done.3.refs_7_ = f32[48,128]{1,0:T(8,128)S(1)} collective-permute-done((f32[48,128]{1,0:T(8,128)S(1)}, f32[48,128]{1,0:T(8,128)S(1)}, u32[]{:S(2)}, u32[]{:S(2)}) %collective-permute-start.3) | collective-permute-done | bytes 24608 | tf_op jit(solution)/shard_map/ppermute | solution.py:423
  78.6 12.7 %solve.1 = (f32[80,128]{1,0:T(8,128)}, f32[1024,128]{1,0:T(8,128)}) custom-call(s32[1]{0:T(128)} %bitcast.lat_ref.refs_0_, f32[80,128]{1,0:T(8,128)S(1)} %bitcast.36, f32[40,128]{1,0:T(8,128)S(1)} %bitcast.40, f32[40,128]{1,0:T(8,128)S(1)} %bitcast.38, f32[8,256,128]{2,1,0:T(8,128)S(1)} %get-tuple-element.8.refs_4_, ...), custom_call_target="tpu_custom_call" | custom-call | tf_op jit(solution)/shard_map/solve/pallas_call | solution.py:429
  (41 shorter events, 0.2 us)
Async XLA Ops:
  0.6 15.2 %copy-start.1 = (bf16[9,256,69]{1,2,0:T(8,128)(2,1)S(1)}, bf16[9,256,69]{1,2,0:T(8,128)(2,1)}, u32[]{:S(2)}) copy-start(bf16[9,256,69]{1,2,0:T(8,128)(2,1)} %param.17) | copy-start | bytes 953860
  1.4 45.8 %collective-permute-start.1 = (f32[5,8,128]{2,1,0:T(8,128)S(1)}, f32[5,8,128]{2,1,0:T(8,128)S(1)}, u32[]{:S(2)}, u32[]{:S(2)}) collective-permute-start(f32[5,8,128]{2,1,0:T(8,128)S(1)} %get-tuple-element.18), channel_id=1, source_target_pairs={{1,0},{2,1},{3,2},{4,3},{5,4},{6,5},{7,6},{8,7},{9,8},{10,9},{11,1... | collective-permute-start | bytes 61448 | tf_op jit(solution)/shard_map/ppermute | solution.py:375
  12.4 34.9 %collective-permute-start = (f32[5,8,128]{2,1,0:T(8,128)S(1)}, f32[5,8,128]{2,1,0:T(8,128)S(1)}, u32[]{:S(2)}, u32[]{:S(2)}) collective-permute-start(f32[5,8,128]{2,1,0:T(8,128)S(1)} %get-tuple-element.19), channel_id=1, source_target_pairs={{0,1},{1,2},{2,3},{3,4},{4,5},{5,6},{6,7},{7,8},{8,9},{9,10},{10,1... | collective-permute-start | bytes 61448 | tf_op jit(solution)/shard_map/ppermute | solution.py:374
  15.8 0.7 copy-start.8
  15.8 0.7 copy-start.13
  15.8 0.7 copy-start.9
  15.8 0.7 copy-start.11
  15.8 0.8 copy-start.4
  15.8 0.8 copy-start.2
  15.9 0.8 copy-start.3
  16.5 0.9 %slice-start = ((bf16[9,256,69]{1,2,0:T(8,128)(2,1)}), bf16[9,128,69]{1,2,0:T(8,128)(2,1)S(1)}, s32[]{:S(2)}) async-start(bf16[9,256,69]{1,2,0:T(8,128)(2,1)} %param.17), calls=%async_computation | async-start | bytes 331776 | tf_op jit(solution)/shard_map/slice | solution.py:385
  16.9 0.7 copy-start.14
  17.7 0.7 copy-start.12
  18.6 0.7 copy-start.5
  19.3 0.7 copy-start.7
  19.3 0.7 copy-start.6
  47.1 0.8 copy-start
  56.6 15.3 %collective-permute-start.2 = (f32[48,128]{1,0:T(8,128)S(1)}, f32[48,128]{1,0:T(8,128)S(1)}, u32[]{:S(2)}, u32[]{:S(2)}) collective-permute-start(f32[48,128]{1,0:T(8,128)S(1)} %get-tuple-element.10), channel_id=1, source_target_pairs={{0,16},{16,32},{32,48},{48,64},{64,80},{80,96},{96,112},{112,128},... | collective-permute-start | bytes 73736 | tf_op jit(solution)/shard_map/ppermute | solution.py:422
  69.9 2.0 %copy-start.10 = (bf16[5,64]{1,0:T(8,128)(2,1)S(1)}, bf16[5,64]{1,0:T(8,128)(2,1)}, u32[]{:S(2)}) copy-start(bf16[5,64]{1,0:T(8,128)(2,1)} %param.19) | copy-start | bytes 1924
  69.9 8.8 %collective-permute-start.3 = (f32[48,128]{1,0:T(8,128)S(1)}, f32[48,128]{1,0:T(8,128)S(1)}, u32[]{:S(2)}, u32[]{:S(2)}) collective-permute-start(f32[48,128]{1,0:T(8,128)S(1)} %get-tuple-element.11), channel_id=1, source_target_pairs={{16,0},{32,16},{48,32},{64,48},{80,64},{96,80},{112,96},{128,112},... | collective-permute-start | bytes 73736 | tf_op jit(solution)/shard_map/ppermute | solution.py:423

commit v2 on v0

v2 whole, which is shorter than its diff:
```python
import jax
import jax.numpy as jnp
from jax import lax
from jax.experimental import pallas as pl
from jax.experimental.pallas import tpu as pltpu
from jax.sharding import PartitionSpec as P

DAYS = 5
ROWS = 16
COLS = 128
LANES = 128
HID = 64
TRACK = 512
HALO = 8
BASES = 25
CHUNK = 2048
FIRST = 7
STRIP = 30
TILES = 37
GROUP = 4
F32 = jnp.float32
BF16 = jnp.bfloat16


def nt_dot(left, right):
    return lax.dot_general(left, right, (((1,), (1,)), ((), ())), preferred_element_type=F32)


def lane_roll(value, shift):
    return pltpu.roll(value, shift % value.shape[1], 1)


def strip_place(row):
    return (row + 6) // 4, (row + 6) % 4 * 32


def day_rows(near_ref, mid_ref, far_ref, even, row):
    if 0 <= row < ROWS:
        picked = mid_ref[pl.ds(row, DAYS, stride=ROWS), :]
    else:
        place = pl.ds(row + HALO if row < 0 else row - ROWS, DAYS, stride=HALO)
        near, far = near_ref[place, :], far_ref[place, :]
        picked = jnp.where(even, far, near) if row < 0 else jnp.where(even, near, far)
    return jnp.concatenate([picked, jnp.zeros((8 - DAYS, LANES), F32)], axis=0)


def adjoint_terms(sums_ref, base, here, above):
    low = pl.ds(5 * base, 8)
    high = pl.ds(LANES + 5 * base, 8)
    here_right = lane_roll(here, -1)
    above_right = lane_roll(above, -1)
    s01 = sums_ref[1, low, :]
    s02 = sums_ref[2, low, :]
    s03 = sums_ref[3, low, :]
    s12 = sums_ref[2, high, :]
    s13 = sums_ref[3, high, :]
    s23 = sums_ref[6, low, :]
    g0 = sums_ref[0, low, :] * here + s01 * here_right + s02 * above + s03 * above_right - sums_ref[4, low, :]
    g1 = s01 * here + sums_ref[1, high, :] * here_right + s12 * above + s13 * above_right - sums_ref[4, high, :]
    g2 = s02 * here + s12 * here_right + sums_ref[5, low, :] * above + s23 * above_right - sums_ref[7, low, :]
    g3 = s03 * here + s13 * here_right + s23 * above + sums_ref[6, high, :] * above_right - sums_ref[7, high, :]
    return g0 + lane_roll(g1, 1), g2 + lane_roll(g3, 1)


def track_kernel(value_ref, weight_ref, tile_ref, time_ref, row_ref, col_ref, out_ref):
    latitude = tile_ref[...] * ROWS + row_ref[...]
    keys = [time_ref[...].astype(F32), latitude.astype(F32), col_ref[...].astype(F32)]
    block = jnp.concatenate([value_ref[...], weight_ref[...]] + keys, axis=0)
    twice = jnp.concatenate([block, block], axis=0).astype(BF16)
    for k in range(out_ref.shape[0] // 16):
        out_ref[16 * k : 16 * k + 16, :] = twice


def prepare_kernel(gate_ref, gate_bias_ref, in_ref, in_bias_ref, out_ref, inc_ref, w_gate_ref, w_in_ref, w_out_ref, w_inc_ref):
    def rows_of(ref, k):
        return jnp.concatenate([ref[k].astype(F32)[0:DAYS], jnp.zeros((8 - DAYS, ref.shape[2]), F32)], axis=0)

    def bias_rows(bias):
        high = bias.astype(BF16).astype(F32)
        middle = (bias - high).astype(BF16).astype(F32)
        low = bias - high - middle
        return jnp.concatenate([high, middle, low, jnp.zeros((5, bias.shape[1]), F32)], axis=0)

    pieces = [rows_of(gate_ref, k) for k in range(9)] + [bias_rows(gate_bias_ref[...])]
    pieces += [gate_ref[k].astype(F32)[DAYS:] for k in range(9)]
    whole = jnp.concatenate(pieces + [jnp.zeros((768 - 656, 4 * HID), F32)], axis=0)
    for k in range(6):
        block = whole[128 * k : 128 * k + 128]
        first = lane_roll(block[:, 0:128], HID) * 0.5
        second = block[:, 128:256]
        lane = lax.broadcasted_iota(jnp.int32, (128, 128), 1)
        second = jnp.where(lane < HID, 0.5 * second, second)
        w_gate_ref[0:128, 128 * k : 128 * k + 128] = first.T.astype(BF16)
        w_gate_ref[128:256, 128 * k : 128 * k + 128] = second.T.astype(BF16)
    narrow = jnp.concatenate([rows_of(in_ref, k) for k in range(9)] + [bias_rows(in_bias_ref[...])], axis=0)
    narrow = jnp.concatenate([narrow, jnp.zeros((48, HID), F32)], axis=0)
    narrow = jnp.concatenate([narrow, jnp.zeros((128, 128 - HID), F32)], axis=1)
    w_in_ref[...] = narrow.T[0:HID].astype(BF16)
    spread = [rows_of(out_ref, k) for k in range(9)]
    w_out_ref[...] = jnp.concatenate(spread + [jnp.zeros((8, HID), F32)], axis=0).astype(BF16)
    w_inc_ref[...] = jnp.concatenate(
        [inc_ref[...].astype(F32), jnp.zeros((16 - DAYS, HID), F32)], axis=0
    ).astype(BF16)


EAST_FIELDS = ((4, 1), (1, 0), (1, 1), (2, 1), (3, 1), (7, 1), (3, 0), (6, 0), (6, 1))
WEST_FIELDS = ((4, 0), (0, 0), (1, 0), (2, 0), (3, 0), (7, 0), (2, 1), (5, 0), (6, 0))
EAST_LANES = ((0, 1, 2, 3, 4), (5, 6, 4, 7, 8))
WEST_LANES = ((0, 1, 2, 3, 4), (5, 3, 6, 7, 8))


def build_kernel(
    place_ref, track_ref, mid_ref, near_ref, far_ref, sums_ref, adjoint_ref, to_near_ref, to_far_ref, rw_ref, cw_ref
):
    base_row = (place_ref[0] * ROWS - 5).astype(F32)
    even_lat = place_ref[0] % 2 == 0
    even_lon = place_ref[1] % 2 == 0
    entry = lax.broadcasted_iota(jnp.int32, (LANES, TRACK), 0).astype(F32).astype(BF16)
    nothing = jnp.zeros((LANES, TRACK), BF16)

    def spread(row):
        part = jnp.broadcast_to(row, (16, TRACK)).astype(BF16)
        return jnp.concatenate([part] * 8, axis=0)

    per_chunk = CHUNK // TRACK
    chunks = track_ref.shape[0] * TRACK // (8 * CHUNK)
    for chunk in range(chunks):
        slot = chunk % 2
        for pair in range(per_chunk // 2):
            first_row = chunk * per_chunk * 8 + pair * 16
            both = track_ref[first_row : first_row + 16, :].astype(F32)
            for part in range(2):
                block = both[8 * part : 8 * part + 8]
                at = (2 * pair + part) * TRACK
                offset = block[6:7] - base_row
                within = (offset >= 0.0) & (offset < float(BASES))
                row_hit = entry == spread(jnp.where(within, offset * 5.0 + block[5:6], -1.0))
                col_hit = entry == spread(block[7:8])
                for k in range(5):
                    source = (1 + k) % 5
                    value = spread(block[source : source + 1])
                    if k < 4:
                        rw_ref[slot, 128 * k : 128 * k + 128, at : at + TRACK] = jnp.where(row_hit, value, nothing)
                    cw_ref[slot, 128 * k : 128 * k + 128, at : at + TRACK] = jnp.where(col_hit, value, nothing)
        first = nt_dot(rw_ref[slot, 0:256, :], cw_ref[slot])
        second = nt_dot(rw_ref[slot, 256:512, :], cw_ref[slot, 256:640, :])
        for k in range(8):
            total = first[:, 128 * k : 128 * k + 128] if k < 5 else second[:, 128 * k - 640 : 128 * k - 512]
            sums_ref[k] = total if chunk == 0 else sums_ref[k] + total

    lane = lax.broadcasted_iota(jnp.int32, (8, LANES), 1)
    zero = jnp.zeros((8, LANES), F32)
    east, west = zero, zero
    carried = zero
    for row in range(-6, ROWS + 6):
        part, place = strip_place(row)
        here = day_rows(near_ref, mid_ref, far_ref, even_lat, row)
        picked = lane // 8 == place // 8
        east = jnp.where(picked, lane_roll(here, place - 120), east)
        west = jnp.where(picked, lane_roll(here, place), west)
        if -5 <= row <= 19:
            above = day_rows(near_ref, mid_ref, far_ref, even_lat, row + 1)
            now, later = adjoint_terms(sums_ref, row + 5, here, above)
            if row > -5:
                total = carried + now
                adjoint_ref[row + 4] = total
                picked = lane // 8 == place // 8 + 1
                east = jnp.where(picked, lane_roll(total, place + 8 - 120), east)
                west = jnp.where(picked, lane_roll(total, place + 8), west)
            carried = later
        if -2 <= row <= ROWS:
            for k in range(9):
                target = place + 16 + k
                array, half = EAST_FIELDS[k]
                piece = sums_ref[array, pl.ds(LANES * half + 5 * (row + 5), 8), :]
                east = jnp.where(lane == target, lane_roll(piece, target - (COLS - 2)), east)
                array, half = WEST_FIELDS[k]
                piece = sums_ref[array, pl.ds(LANES * half + 5 * (row + 5), 8), :]
                west = jnp.where(lane == target, lane_roll(piece, target), west)
        if place == 96:
            to_near_ref[8 * part : 8 * part + 8, :] = jnp.where(even_lon, east, west)
            to_far_ref[8 * part : 8 * part + 8, :] = jnp.where(even_lon, west, east)
            east, west = zero, zero


def solve_kernel(
    place_ref,
    mid_ref,
    near_ref,
    far_ref,
    sums_ref,
    adjoint_ref,
    own_near_ref,
    own_far_ref,
    from_near_ref,
    from_far_ref,
    w_in_ref,
    w_out_ref,
    w_gate_ref,
    w_inc_ref,
    est_out_ref,
    cell_out_ref,
    est_ref,
    grad_ref,
    minus_ref,
    plus_ref,
    mask_ref,
    window_ref,
    spread_ref,
    cell_ref,
    hidden_ref,
    hid_minus_ref,
    hid_plus_ref,
    *,
    lat_count,
):
    lat = place_ref[0]
    even_lat = lat % 2 == 0
    even_lon = place_ref[1] % 2 == 0
    lane = lax.broadcasted_iota(jnp.int32, (8, LANES), 1)
    zero = jnp.zeros((8, LANES), F32)
    strips = slice(STRIP * LANES, TILES * LANES)
    strip_width = (TILES - STRIP) * LANES
    strip_lane = lax.broadcasted_iota(jnp.int32, (8, strip_width), 1)

    def tile(index, count=1):
        return slice(index * LANES, (index + count) * LANES)

    def at(row):
        return tile(row + FIRST)

    def within(row):
        row = row + lat * ROWS
        return (row >= 0) & (row < lat_count * ROWS)

    def left(main, strip, row):
        part, place = strip_place(row)
        edge = lane_roll(strip[:, tile(part)], -(place + 7))
        return jnp.where(lane[: main.shape[0]] == 0, edge, lane_roll(main, 1))

    def right(main, strip, row):
        part, place = strip_place(row)
        edge = lane_roll(strip[:, tile(part)], 127 - (place + 24))
        return jnp.where(lane[: main.shape[0]] == 127, edge, lane_roll(main, -1))

    est_ref[:, at(-7)] = zero
    est_ref[:, at(22)] = zero
    for row in range(-6, 22):
        est_ref[:, at(row)] = day_rows(near_ref, mid_ref, far_ref, even_lat, row)
    quarter = (lane % 32) // 8
    from_west, from_east, adjoint_strip = [], [], []
    for part in range(TILES - STRIP):
        rows = slice(8 * part, 8 * part + 8)
        own_east = jnp.where(even_lon, own_near_ref[rows, :], own_far_ref[rows, :])
        own_west = jnp.where(even_lon, own_far_ref[rows, :], own_near_ref[rows, :])
        west = jnp.where(even_lon, from_far_ref[rows, :], from_near_ref[rows, :])
        east = jnp.where(even_lon, from_near_ref[rows, :], from_far_ref[rows, :])
        from_west.append(west)
        from_east.append(east)

        def join(first, second, third, fourth):
            return jnp.where(
                quarter < 2, jnp.where(quarter == 0, first, second), jnp.where(quarter == 2, third, fourth)
            )

        est_ref[:, tile(STRIP + part)] = join(west, lane_roll(own_west, 8), lane_roll(own_east, 16), lane_roll(east, 24))
        adjoint_strip.append(join(lane_roll(west, -8), own_west, lane_roll(own_east, 8), lane_roll(east, 16)))
    from_west = jnp.concatenate(from_west, axis=1)
    from_east = jnp.concatenate(from_east, axis=1)
    adjoint_strip = jnp.concatenate(adjoint_strip, axis=1)
    for row in range(-7, 23):
        mask_ref[:, at(row)] = jnp.where(within(row), jnp.ones((8, LANES), F32), 0.0)
    mask_ref[:, strips] = jnp.where(within(strip_lane // 32 - 6), 1.0, 0.0)

    ones = jnp.where(lax.broadcasted_iota(jnp.int32, (8, LANES), 0) < 3, 1.0, 0.0).astype(F32)

    def windows(ref, first_row, last_row, with_strips):
        strip = ref[:, strips]
        for row in range(first_row - 1, last_row + 2):
            main = ref[:, at(row)]
            minus_ref[:, at(row)] = left(main, strip, row)
            plus_ref[:, at(row)] = right(main, strip, row)
        for row in range(first_row, last_row + 1):
            pieces = [source[:, at(row + a)] for a in (-1, 0, 1) for source in (minus_ref, ref, plus_ref)]
            window_ref[:, at(row)] = jnp.concatenate(pieces + [ones], axis=0).astype(BF16)
        if with_strips:
            pieces = []
            shifts = (lane_roll(strip, 1), strip, lane_roll(strip, -1))
            for a in (-1, 0, 1):
                pieces += [lane_roll(value, -32 * a) if a else value for value in shifts]
            pieces.append(jnp.concatenate([ones] * (TILES - STRIP), axis=1))
            window_ref[:, strips] = jnp.concatenate(pieces, axis=0).astype(BF16)

    def pieces_of(first_row, last_row):
        runs = [(first_row + FIRST, last_row + 1 + FIRST), (STRIP, TILES)]
        return [tile(t, min(GROUP, end - t)) for start, end in runs for t in range(start, end, GROUP)]

    def gradient(first_row, last_row):
        windows(est_ref, first_row - 1, last_row + 1, True)
        for where in pieces_of(first_row - 1, last_row + 1):
            value = jnp.dot(w_in_ref[:, 0:80], window_ref[:, where], preferred_element_type=F32)
            value = jnp.maximum(value, 0.0) * mask_ref[0:1, where]
            spread_ref[:, where] = jnp.dot(w_out_ref[...], value.astype(BF16), preferred_element_type=F32)
        totals = []
        for b in range(3):
            total = None
            for a in range(3):
                k = 8 * (3 * a + b)
                piece = spread_ref[k : k + 8, strips]
                piece = lane_roll(piece, 32 - 32 * a) if a != 1 else piece
                total = piece if total is None else total + piece
            totals.append(total)
        grad_ref[:, strips] = est_ref[:, strips] - (totals[1] + lane_roll(totals[0], 1) + lane_roll(totals[2], -1))
        for row in range(first_row, last_row + 1):
            columns = []
            for b in range(3):
                terms = [spread_ref[8 * (3 * a + b) : 8 * (3 * a + b) + 8, at(row + a - 1)] for a in range(3)]
                columns.append(terms[0] + terms[1] + terms[2])
            term = columns[1] + left(columns[0], totals[0], row) + right(columns[2], totals[2], row)
            grad_ref[:, at(row)] = est_ref[:, at(row)] - term

    gradient(-4, 19)
    for row in range(-4, 20):
        total = grad_ref[:, at(row)] + adjoint_ref[row + 4]
        grad_ref[:, at(row)] = total if 0 <= row < ROWS else total * mask_ref[:, at(row)]
    grad_ref[:, strips] = (grad_ref[:, strips] + adjoint_strip) * mask_ref[:, strips]
    windows(grad_ref, -3, 18, True)
    for where in pieces_of(-3, 18):
        sums = jnp.dot(w_gate_ref[HID:, 0:80], window_ref[:, where], preferred_element_type=F32)
        gate_in = 0.5 * jnp.tanh(sums[0:HID]) + 0.5
        gate_out = 0.5 * jnp.tanh(sums[HID : 2 * HID]) + 0.5
        cell = gate_in * jnp.tanh(sums[2 * HID : 3 * HID])
        hidden = (gate_out * jnp.tanh(cell) * mask_ref[0:1, where]).astype(BF16)
        cell_ref[:, where] = cell
        hidden_ref[:, where] = hidden
        update = jnp.dot(w_inc_ref[...], hidden, preferred_element_type=F32)
        est_ref[:, where] -= update[0:8]

    lane64 = lax.broadcasted_iota(jnp.int32, (HID, LANES), 1)
    for row in range(-1, ROWS + 1):
        part, place = strip_place(row)
        main = hidden_ref[:, at(row)].astype(F32)
        strip = hidden_ref[:, tile(STRIP + part)].astype(F32)
        hid_minus_ref[:, at(row)] = jnp.where(
            lane64 == 0, lane_roll(strip, -(place + 7)), lane_roll(main, 1)
        ).astype(BF16)
        hid_plus_ref[:, at(row)] = jnp.where(
            lane64 == 127, lane_roll(strip, 127 - (place + 24)), lane_roll(main, -1)
        ).astype(BF16)
    gradient(-1, 16)
    carried = zero
    for row in range(-2, ROWS + 1):
        now, later = adjoint_terms(sums_ref, row + 5, est_ref[:, at(row)], est_ref[:, at(row + 1)])
        if row > -2:
            total = grad_ref[:, at(row)] + carried + now
            grad_ref[:, at(row)] = total if 0 <= row < ROWS else total * mask_ref[:, at(row)]
        carried = later
    here = est_ref[:, strips]
    above = lane_roll(here, -32)

    def edge_term(source, lane_at, lanes, e0, e1, e2, e3):
        d, f0, f1, f2, f3 = [lane_roll(source, lane_at - (16 + k)) for k in lanes]
        return f0 * e0 + f1 * e1 + f2 * e2 + f3 * e3 - d

    west = (lane_roll(here, 1), here, lane_roll(above, 1), above)
    east = (here, lane_roll(here, -1), above, lane_roll(above, -1))
    extra_w = edge_term(from_west, 7, EAST_LANES[0], *west) + lane_roll(
        edge_term(from_west, 7, EAST_LANES[1], *west), 32
    )
    extra_e = edge_term(from_east, 24, WEST_LANES[0], *east) + lane_roll(
        edge_term(from_east, 24, WEST_LANES[1], *east), 32
    )
    grad_ref[:, strips] = (
        grad_ref[:, strips] + jnp.where(strip_lane % 32 < 16, extra_w, extra_e)
    ) * mask_ref[:, strips]
    windows(grad_ref, 0, ROWS - 1, False)
    for row in range(0, ROWS, 2):
        pieces = [window_ref[:, tile(row + FIRST, 2)]]
        for a in (-1, 0, 1):
            for source in (hid_minus_ref, hidden_ref, hid_plus_ref):
                pieces.append(source[:, tile(row + a + FIRST, 2)])
        sums = jnp.dot(w_gate_ref[:, 0:656], jnp.concatenate(pieces, axis=0), preferred_element_type=F32)
        old = cell_ref[:, tile(row + FIRST, 2)]
        forget = 0.5 * jnp.tanh(sums[0:HID]) + 0.5
        gate_in = 0.5 * jnp.tanh(sums[HID : 2 * HID]) + 0.5
        gate_out = 0.5 * jnp.tanh(sums[2 * HID : 3 * HID]) + 0.5
        cell = forget * old + gate_in * jnp.tanh(sums[3 * HID :])
        hidden = gate_out * jnp.tanh(cell)
        update = jnp.dot(w_inc_ref[...], hidden.astype(BF16), preferred_element_type=F32)
        for k in range(2):
            cell_out_ref[pl.ds(row + k, HID, stride=ROWS), :] = cell[:, tile(k)]
            final = est_ref[:, at(row + k)] - update[0:8, tile(k)]
            est_out_ref[pl.ds(row + k, DAYS, stride=ROWS), :] = final[0:DAYS]


def swap(value, axis, first, count, periodic):
    last = count if periodic else count - 1
    pairs = [(i, (i + 1) % count) for i in range(first, last, 2)]
    return lax.ppermute(value, axis, pairs + [(target, source) for source, target in pairs])


def on_device(
    state,
    prior_in,
    prior_bias,
    prior_out,
    lstm_weight,
    lstm_bias,
    lstm_out,
    obs_value,
    obs_weight,
    obs_tile,
    obs_time,
    obs_row,
    obs_col,
):
    lat_count = lax.axis_size("lat")
    lon_count = lax.axis_size("lon")
    lat = lax.axis_index("lat").astype(jnp.int32)
    lon = lax.axis_index("lon").astype(jnp.int32)
    place = jnp.stack([lat, lon])
    upper, lower = state[:, ROWS - HALO :], state[:, :HALO]
    even_lat = lat % 2 == 0
    far = swap(jnp.where(even_lat, lower, upper), "lat", 1, lat_count, False).reshape(DAYS * HALO, LANES)
    near = swap(jnp.where(even_lat, upper, lower), "lat", 0, lat_count, False).reshape(DAYS * HALO, LANES)
    mid = state.reshape(DAYS * ROWS, LANES)

    smem = pl.BlockSpec(memory_space=pltpu.SMEM)
    vmem = pl.BlockSpec(memory_space=pltpu.VMEM)
    track = pl.pallas_call(
        track_kernel,
        out_shape=jax.ShapeDtypeStruct((lat_count * 8, TRACK), BF16),
        in_specs=[vmem] * 6,
        out_specs=vmem,
        cost_estimate=pl.CostEstimate(flops=100_000, bytes_accessed=150_000, transcendentals=0),
        name="track",
    )(
        obs_value.reshape(1, TRACK),
        obs_weight,
        obs_tile.reshape(1, TRACK),
        obs_time.reshape(1, TRACK),
        obs_row.reshape(1, TRACK),
        obs_col.reshape(1, TRACK),
    )
    track, near, far = lax.optimization_barrier((track, near, far))
    gathered = lax.all_to_all(
        track.reshape(lat_count, 8, TRACK), "lat", split_axis=0, concat_axis=0, tiled=True
    ).reshape(lat_count * 8, TRACK)
    w_gate, w_in, w_out, w_inc = pl.pallas_call(
        prepare_kernel,
        out_shape=(
            jax.ShapeDtypeStruct((4 * HID, 768), BF16),
            jax.ShapeDtypeStruct((HID, LANES), BF16),
            jax.ShapeDtypeStruct((80, HID), BF16),
            jax.ShapeDtypeStruct((16, HID), BF16),
        ),
        in_specs=[vmem] * 6,
        out_specs=(vmem,) * 4,
        compiler_params=pltpu.CompilerParams(vmem_limit_bytes=16 * 1024 * 1024),
        cost_estimate=pl.CostEstimate(flops=2_000_000, bytes_accessed=1_500_000, transcendentals=0),
        name="prepare",
    )(
        jnp.transpose(lstm_weight, (0, 2, 1)),
        lstm_bias.reshape(1, 4 * HID),
        jnp.transpose(prior_in, (0, 2, 1)),
        prior_bias.reshape(1, HID),
        prior_out,
        lstm_out,
    )
    sums, adjoint, to_near, to_far = pl.pallas_call(
        build_kernel,
        out_shape=(
            jax.ShapeDtypeStruct((8, 256, LANES), F32),
            jax.ShapeDtypeStruct((24, 8, LANES), F32),
            jax.ShapeDtypeStruct((56, LANES), F32),
            jax.ShapeDtypeStruct((56, LANES), F32),
        ),
        in_specs=[smem, vmem, vmem, vmem, vmem],
        out_specs=(vmem, vmem, vmem, vmem),
        scratch_shapes=[
            pltpu.VMEM((2, 512, CHUNK), BF16),
            pltpu.VMEM((2, 640, CHUNK), BF16),
        ],
        compiler_params=pltpu.CompilerParams(vmem_limit_bytes=32 * 1024 * 1024),
        cost_estimate=pl.CostEstimate(flops=4_000_000_000, bytes_accessed=1_500_000, transcendentals=0),
        name="build",
    )(place, gathered, mid, near, far)

    from_far = swap(to_far, "lon", 1, lon_count, True)
    from_near = swap(to_near, "lon", 0, lon_count, True)

    def solve(*refs):
        solve_kernel(*refs, lat_count=lat_count)

    width = TILES * LANES
    estimate, cell_state = pl.pallas_call(
        solve,
        out_shape=(
            jax.ShapeDtypeStruct((DAYS * ROWS, LANES), F32),
            jax.ShapeDtypeStruct((HID * ROWS, LANES), F32),
        ),
        in_specs=[smem] + [vmem] * 13,
        out_specs=(vmem, vmem),
        scratch_shapes=[
            pltpu.VMEM((8, width), F32),
            pltpu.VMEM((8, width), F32),
            pltpu.VMEM((8, width), F32),
            pltpu.VMEM((8, width), F32),
            pltpu.VMEM((8, width), F32),
            pltpu.VMEM((80, width), BF16),
            pltpu.VMEM((80, width), F32),
            pltpu.VMEM((HID, width), F32),
            pltpu.VMEM((HID, width), BF16),
            pltpu.VMEM((HID, width), BF16),
            pltpu.VMEM((HID, width), BF16),
        ],
        compiler_params=pltpu.CompilerParams(vmem_limit_bytes=32 * 1024 * 1024),
        name="solve",
    )(place, mid, near, far, sums, adjoint, to_near, to_far, from_near, from_far, w_in, w_out, w_gate, w_inc)
    return (
        estimate.reshape(DAYS, ROWS, LANES),
        cell_state.reshape(HID, ROWS, LANES),
    )


def solution(mesh):
    return jax.shard_map(
        on_device,
        mesh=mesh,
        in_specs=(
            P(None, "lat", "lon"),
            P(),
            P(),
            P(),
            P(),
            P(),
            P(),
            P(("lon", "lat")),
            P(None, ("lon", "lat")),
            P(("lon", "lat"), None),
            P(("lon", "lat")),
            P(("lon", "lat")),
            P(("lon", "lat")),
        ),
        out_specs=(P(None, "lat", "lon"), P(None, "lat", "lon")),
        check_vma=False,
    )
```

time: 202 us -> 57.4 us (0.28)
  the two profiles are of different devices: /device:TPU:31 before, /device:TPU:29 now
where the time goes in v2:
time: 57.4 us; the launch traced here: 56.9 us
  starting transfers between devices  27 us (47%)
  Pallas kernels  17.1 us (30%)
  waiting for transfers between devices  10.6 us (18%)
  other arithmetic  0.83 us (1%)
  between operations  0.77 us (1%)
  local copies, waits for them, and re-layouts  0.66 us (1%)
    ppermute x4, starting transfers between devices, swap(): lax.ppermute(value, axis, pairs + [(target, source) for source, target in...  18 us
    all_to_all x1, starting transfers between devices, on_device(): lax.all_to_all(track.reshape(lat_count, 8, TRACK), 'lat', split_axis=0, c...  9.05 us
    pallas_call x1, Pallas kernels, on_device(): pl.pallas_call(solve, out_shape=(jax.ShapeDtypeStruct((DAYS * ROWS, LANES...  8.92 us
    all_to_all x1, waiting for transfers between devices, on_device(): lax.all_to_all(track.reshape(lat_count, 8, TRACK), 'lat', split_axis=0, c...  7.35 us
    pallas_call x1, Pallas kernels, on_device(): pl.pallas_call(build_kernel, out_shape=(jax.ShapeDtypeStruct((8, 256, LAN...  6.41 us
    ppermute x4, waiting for transfers between devices, swap(): lax.ppermute(value, axis, pairs + [(target, source) for source, target in...  3.24 us
    pallas_call x1, Pallas kernels, on_device(): pl.pallas_call(track_kernel, out_shape=jax.ShapeDtypeStruct((lat_count *...  1.44 us
  transfers between devices with their start and end apart: 5, of which 2 were waited for; matrix products, arithmetic and copies ran while one was open for 0% of the time, Pallas kernels for 3%

profile of v2, /device:TPU:29, one launch (start us, length us, event | category | flops | bytes accessed | tf_op | source)
XLA Modules:
  0.0 56.9 jit_solution(11027964941576816693)
XLA Ops:
  0.6 0.8 %slice_select_fusion = (f32[5,8,128]{2,1,0:T(8,128)S(1)}, f32[5,8,128]{2,1,0:T(8,128)S(1)}) fusion(f32[5,16,128]{2,1,0:T(8,128)} %param.13, pred[]{:T(512)S(6)} %eq.5), kind=kLoop, calls=%fused_computation | loop fusion | flops 10240 | bytes 81921 | tf_op jit(solution)/shard_map/jit(_where)/select_n | solution.py:424
  1.4 0.7 %collective-permute-start.1 = (f32[5,8,128]{2,1,0:T(8,128)S(1)}, f32[5,8,128]{2,1,0:T(8,128)S(1)}, u32[]{:S(2)}, u32[]{:S(2)}) collective-permute-start(f32[5,8,128]{2,1,0:T(8,128)S(1)} %get-tuple-element.28), channel_id=1, source_target_pairs={{1,2},{3,4},{5,6},{7,8},{9,10},{11,12},{13,14},{2,1},{4,3},{6,5},{... | collective-permute-start | bytes 61448 | tf_op jit(solution)/shard_map/ppermute | solution.py:399
  2.1 7.3 %collective-permute-start = (f32[5,8,128]{2,1,0:T(8,128)S(1)}, f32[5,8,128]{2,1,0:T(8,128)S(1)}, u32[]{:S(2)}, u32[]{:S(2)}) collective-permute-start(f32[5,8,128]{2,1,0:T(8,128)S(1)} %get-tuple-element.29), channel_id=1, source_target_pairs={{0,1},{2,3},{4,5},{6,7},{8,9},{10,11},{12,13},{14,15},{1,0},{3,2},... | collective-permute-start | bytes 61448 | tf_op jit(solution)/shard_map/ppermute | solution.py:399
  9.4 1.4 %track.1 = bf16[128,512]{1,0:T(8,128)(2,1)} custom-call(f32[1,512]{1,0:T(1,128)} %bitcast.30, f32[4,512]{1,0:T(4,128)} %weight_ref.1, s32[1,512]{1,0:T(1,128)} %bitcast.31, s32[1,512]{1,0:T(1,128)} %bitcast.32, s32[1,512]{1,0:T(1,128)} %bitcast.33, s32[1,512]{1,0:T(1,128)} %bitcast.34), custom_call_target="tpu_custom_call" | custom-call | flops 100000 | bytes 150000 | tf_op jit(solution)/shard_map/track/pallas_call | solution.py:430
  10.8 0.0 collective-permute-done.1
  10.8 0.0 collective-permute-done
  10.8 0.0 copy-start.1
  10.9 9.0 %all-to-all-start = ((bf16[16,8,512]{2,1,0:T(8,128)(2,1)}), bf16[16,8,512]{2,1,0:T(8,128)(2,1)S(1)}, u32[]{:S(2)}, u32[]{:S(2)}) async-start(bf16[16,8,512]{2,1,0:T(8,128)(2,1)} %bitcast.29), calls=%async_computation | async-start | bytes 262144 | tf_op jit(solution)/shard_map/all_to_all | solution.py:446
  19.9 0.1 pad_add_fusion.place_ref.refs_0_
  20.0 7.3 %all-to-all-done = bf16[16,8,512]{2,1,0:T(8,128)(2,1)S(1)} async-done(((bf16[16,8,512]{2,1,0:T(8,128)(2,1)}), bf16[16,8,512]{2,1,0:T(8,128)(2,1)S(1)}, u32[]{:S(2)}, u32[]{:S(2)}) %all-to-all-start) | async-done | bytes 131104 | tf_op jit(solution)/shard_map/all_to_all | solution.py:446
  27.3 0.0 copy-done.1
  27.3 0.0 copy-start
  27.3 0.0 copy-start.2
  27.3 0.0 copy-start.3
  27.4 6.4 %build.1 = (f32[8,256,128]{2,1,0:T(8,128)S(1)}, f32[24,8,128]{2,1,0:T(8,128)S(1)}, f32[56,128]{1,0:T(8,128)S(1)}, f32[56,128]{1,0:T(8,128)S(1)}) custom-call(s32[2]{0:T(128)S(1)} %pad_add_fusion.place_ref.refs_0_, bf16[128,512]{1,0:T(8,128)(2,1)S(1)} %bitcast.21, f32[80,128]{1,0:T(8,128)S(1)} %bitcast.19, f32[40,128]{1,0:T(8,128)S(1)} %bitcast.24, ...), custom_call_target="tpu_custom_call" | custom-call | flops 4000000000 | bytes 1500000 | tf_op jit(solution)/shard_map/build/pallas_call | solution.py:470
  33.8 5.4 %collective-permute-start.2 = (f32[56,128]{1,0:T(8,128)S(1)}, f32[56,128]{1,0:T(8,128)S(1)}, u32[]{:S(2)}, u32[]{:S(2)}) collective-permute-start(f32[56,128]{1,0:T(8,128)S(1)} %get-tuple-element.20.refs_6_), channel_id=1, source_target_pairs={{0,16},{32,48},{64,80},{96,112},{128,144},{160,176},{192,208},{224... | collective-permute-start | bytes 86024 | tf_op jit(solution)/shard_map/ppermute | solution.py:399
  39.2 4.6 %collective-permute-start.3 = (f32[56,128]{1,0:T(8,128)S(1)}, f32[56,128]{1,0:T(8,128)S(1)}, u32[]{:S(2)}, u32[]{:S(2)}) collective-permute-start(f32[56,128]{1,0:T(8,128)S(1)} %get-tuple-element.21.refs_7_), channel_id=1, source_target_pairs={{16,32},{48,64},{80,96},{112,128},{144,160},{176,192},{208,224},{2... | collective-permute-start | bytes 86024 | tf_op jit(solution)/shard_map/ppermute | solution.py:399
  43.8 0.0 copy-start.4
  43.8 0.0 copy-start.5
  43.8 0.0 copy-start.6
  43.8 0.0 copy-done
  43.8 0.0 copy-done.2
  43.8 0.0 copy-done.3
  43.8 0.6 %copy-done.4 = bf16[5,64]{1,0:T(8,128)(2,1)S(1)} copy-done((bf16[5,64]{1,0:T(8,128)(2,1)S(1)}, bf16[5,64]{1,0:T(8,128)(2,1)}, u32[]{:S(2)}) %copy-start.4) | copy-done | bytes 664
  44.5 0.0 copy-done.5
  44.5 0.0 copy-done.6
  44.5 0.3 prepare.1
  44.8 0.0 collective-permute-done.2.refs_8_
  44.8 3.2 %collective-permute-done.3.refs_9_ = f32[56,128]{1,0:T(8,128)S(1)} collective-permute-done((f32[56,128]{1,0:T(8,128)S(1)}, f32[56,128]{1,0:T(8,128)S(1)}, u32[]{:S(2)}, u32[]{:S(2)}) %collective-permute-start.3) | collective-permute-done | bytes 28704 | tf_op jit(solution)/shard_map/ppermute | solution.py:399
  48.0 8.9 %solve.1 = (f32[80,128]{1,0:T(8,128)}, f32[1024,128]{1,0:T(8,128)}) custom-call(s32[2]{0:T(128)S(1)} %pad_add_fusion.place_ref.refs_0_, f32[80,128]{1,0:T(8,128)S(1)} %bitcast.20, f32[40,128]{1,0:T(8,128)S(1)} %bitcast.25, f32[40,128]{1,0:T(8,128)S(1)} %bitcast.23, f32[8,256,128]{2,1,0:T(8,128)S(1)} %get-tuple-element.18.refs_4_, ...), custom_call_target="tpu_custom_call" | custom-call | tf_op jit(solution)/shard_map/solve/pallas_call | solution.py:496
Async XLA Ops:
  1.4 9.4 %collective-permute-start.1 = (f32[5,8,128]{2,1,0:T(8,128)S(1)}, f32[5,8,128]{2,1,0:T(8,128)S(1)}, u32[]{:S(2)}, u32[]{:S(2)}) collective-permute-start(f32[5,8,128]{2,1,0:T(8,128)S(1)} %get-tuple-element.28), channel_id=1, source_target_pairs={{1,2},{3,4},{5,6},{7,8},{9,10},{11,12},{13,14},{2,1},{4,3},{6,5},{... | collective-permute-start | bytes 61448 | tf_op jit(solution)/shard_map/ppermute | solution.py:399
  2.1 8.8 %collective-permute-start = (f32[5,8,128]{2,1,0:T(8,128)S(1)}, f32[5,8,128]{2,1,0:T(8,128)S(1)}, u32[]{:S(2)}, u32[]{:S(2)}) collective-permute-start(f32[5,8,128]{2,1,0:T(8,128)S(1)} %get-tuple-element.29), channel_id=1, source_target_pairs={{0,1},{2,3},{4,5},{6,7},{8,9},{10,11},{12,13},{14,15},{1,0},{3,2},... | collective-permute-start | bytes 61448 | tf_op jit(solution)/shard_map/ppermute | solution.py:399
  10.8 16.5 %copy-start.1 = (f32[5,16,128]{2,1,0:T(8,128)S(1)}, f32[5,16,128]{2,1,0:T(8,128)}, u32[]{:S(2)}) copy-start(f32[5,16,128]{2,1,0:T(8,128)} %param.13) | copy-start | bytes 122884
  10.9 16.5 %all-to-all-start = ((bf16[16,8,512]{2,1,0:T(8,128)(2,1)}), bf16[16,8,512]{2,1,0:T(8,128)(2,1)S(1)}, u32[]{:S(2)}, u32[]{:S(2)}) async-start(bf16[16,8,512]{2,1,0:T(8,128)(2,1)} %bitcast.29), calls=%async_computation | async-start | bytes 262144 | tf_op jit(solution)/shard_map/all_to_all | solution.py:446
  27.3 16.5 %copy-start = (bf16[9,256,69]{1,2,0:T(8,128)(2,1)S(1)}, bf16[9,256,69]{1,2,0:T(8,128)(2,1)}, u32[]{:S(2)}) copy-start(bf16[9,256,69]{1,2,0:T(8,128)(2,1)} %param.17) | copy-start | bytes 953860
  27.3 16.5 %copy-start.2 = (bf16[9,64,5]{1,2,0:T(8,128)(2,1)S(1)}, bf16[9,64,5]{1,2,0:T(8,128)(2,1)}, u32[]{:S(2)}) copy-start(bf16[9,64,5]{1,2,0:T(8,128)(2,1)} %param.14) | copy-start | bytes 17284
  27.3 16.5 %copy-start.3 = (bf16[9,5,64]{2,1,0:T(8,128)(2,1)S(1)}, bf16[9,5,64]{2,1,0:T(8,128)(2,1)}, u32[]{:S(2)}) copy-start(bf16[9,5,64]{2,1,0:T(8,128)(2,1)} %out_ref.1) | copy-start | bytes 17284
  33.8 11.0 %collective-permute-start.2 = (f32[56,128]{1,0:T(8,128)S(1)}, f32[56,128]{1,0:T(8,128)S(1)}, u32[]{:S(2)}, u32[]{:S(2)}) collective-permute-start(f32[56,128]{1,0:T(8,128)S(1)} %get-tuple-element.20.refs_6_), channel_id=1, source_target_pairs={{0,16},{32,48},{64,80},{96,112},{128,144},{160,176},{192,208},{224... | collective-permute-start | bytes 86024 | tf_op jit(solution)/shard_map/ppermute | solution.py:399
  39.2 8.8 %collective-permute-start.3 = (f32[56,128]{1,0:T(8,128)S(1)}, f32[56,128]{1,0:T(8,128)S(1)}, u32[]{:S(2)}, u32[]{:S(2)}) collective-permute-start(f32[56,128]{1,0:T(8,128)S(1)} %get-tuple-element.21.refs_7_), channel_id=1, source_target_pairs={{16,32},{48,64},{80,96},{112,128},{144,160},{176,192},{208,224},{2... | collective-permute-start | bytes 86024 | tf_op jit(solution)/shard_map/ppermute | solution.py:399
  43.8 0.7 %copy-start.4 = (bf16[5,64]{1,0:T(8,128)(2,1)S(1)}, bf16[5,64]{1,0:T(8,128)(2,1)}, u32[]{:S(2)}) copy-start(bf16[5,64]{1,0:T(8,128)(2,1)} %inc_ref.1) | copy-start | bytes 1924
  43.8 0.7 %copy-start.5 = (f32[256]{0:T(256)S(1)}, f32[256]{0:T(256)}, u32[]{:S(2)}) copy-start(f32[256]{0:T(256)} %param.18) | copy-start | bytes 3076
  43.8 0.7 %copy-start.6 = (f32[64]{0:T(128)S(1)}, f32[64]{0:T(128)}, u32[]{:S(2)}) copy-start(f32[64]{0:T(128)} %param.15) | copy-start | bytes 772

commit v3 on v2

--- a/solution.py
+++ b/solution.py
@@ -62,13 +62,21 @@
     return g0 + lane_roll(g1, 1), g2 + lane_roll(g3, 1)
 
 
-def track_kernel(value_ref, weight_ref, tile_ref, time_ref, row_ref, col_ref, out_ref):
+def track_kernel(
+    place_ref, value_ref, weight_ref, tile_ref, time_ref, row_ref, col_ref, state_ref, out_ref, to_near_ref, to_far_ref
+):
     latitude = tile_ref[...] * ROWS + row_ref[...]
     keys = [time_ref[...].astype(F32), latitude.astype(F32), col_ref[...].astype(F32)]
     block = jnp.concatenate([value_ref[...], weight_ref[...]] + keys, axis=0)
     twice = jnp.concatenate([block, block], axis=0).astype(BF16)
     for k in range(out_ref.shape[0] // 16):
         out_ref[16 * k : 16 * k + 16, :] = twice
+    even = place_ref[0] % 2 == 0
+    for day in range(DAYS):
+        lower = state_ref[ROWS * day : ROWS * day + HALO, :]
+        upper = state_ref[ROWS * (day + 1) - HALO : ROWS * (day + 1), :]
+        to_near_ref[HALO * day : HALO * day + HALO, :] = jnp.where(even, upper, lower)
+        to_far_ref[HALO * day : HALO * day + HALO, :] = jnp.where(even, lower, upper)
 
 
 def prepare_kernel(gate_ref, gate_bias_ref, in_ref, in_bias_ref, out_ref, inc_ref, w_gate_ref, w_in_ref, w_out_ref, w_inc_ref):
@@ -110,7 +118,7 @@
 
 
 def build_kernel(
-    place_ref, track_ref, mid_ref, near_ref, far_ref, sums_ref, adjoint_ref, to_near_ref, to_far_ref, rw_ref, cw_ref
+    place_ref, track_ref, mid_ref, near_ref, far_ref, sums_ref, adjoint_ref, to_far_ref, to_near_ref, rw_ref, cw_ref
 ):
     base_row = (place_ref[0] * ROWS - 5).astype(F32)
     even_lat = place_ref[0] % 2 == 0
@@ -183,6 +191,61 @@
             east, west = zero, zero
 
 
+def row_mask(place_ref, lat_count, row):
+    row = row + place_ref[0] * ROWS
+    return (row >= 0) & (row < lat_count * ROWS)
+
+
+def tile(index, count=1):
+    return slice(index * LANES, (index + count) * LANES)
+
+
+def at(row):
+    return tile(row + FIRST)
+
+
+def ones_rows():
+    return jnp.where(lax.broadcasted_iota(jnp.int32, (8, LANES), 0) < 3, 1.0, 0.0).astype(F32)
+
+
+def spread_terms(spread_ref, row):
+    columns = []
+    for b in range(3):
+        terms = [spread_ref[8 * (3 * a + b) : 8 * (3 * a + b) + 8, at(row + a - 1)] for a in range(3)]
+        columns.append(terms[0] + terms[1] + terms[2])
+    return columns
+
+
+def first_kernel(
+    place_ref, mid_ref, near_ref, far_ref, w_in_ref, w_out_ref, out_ref, est_ref, minus_ref, plus_ref, window_ref, spread_ref, *, lat_count
+):
+    even_lat = place_ref[0] % 2 == 0
+    for row in range(-6, 22):
+        value = day_rows(near_ref, mid_ref, far_ref, even_lat, row)
+        est_ref[:, at(row)] = value
+        minus_ref[:, at(row)] = lane_roll(value, 1)
+        plus_ref[:, at(row)] = lane_roll(value, -1)
+    ones = ones_rows()
+    for row in range(-5, 21):
+        pieces = [source[:, at(row + a)] for a in (-1, 0, 1) for source in (minus_ref, est_ref, plus_ref)]
+        window_ref[:, at(row)] = jnp.concatenate(pieces + [ones], axis=0).astype(BF16)
+    groups = [(-5, 5), (0, 4), (4, 4), (8, 4), (12, 4), (16, 5)]
+    for row, count in groups:
+        where = tile(row + FIRST, count)
+        value = jnp.dot(w_in_ref[:, 0:80], window_ref[:, where], preferred_element_type=F32)
+        value = jnp.maximum(value, 0.0)
+        if row < 0 or row >= ROWS:
+            flags = [
+                jnp.where(row_mask(place_ref, lat_count, row + k), jnp.ones((1, LANES), F32), 0.0) for k in range(count)
+            ]
+            value = value * jnp.concatenate(flags, axis=1)
+        spread_ref[:, where] = jnp.dot(w_out_ref[...], value.astype(BF16), preferred_element_type=F32)
+    for row in range(-4, 20):
+        columns = spread_terms(spread_ref, row)
+        term = columns[1] + lane_roll(columns[0], 1) + lane_roll(columns[2], -1)
+        out_ref[row + 4] = est_ref[:, at(row)] - term
+
+
 def solve_kernel(
     place_ref,
     mid_ref,
@@ -190,10 +253,11 @@
     far_ref,
     sums_ref,
     adjoint_ref,
+    first_ref,
+    own_far_ref,
     own_near_ref,
-    own_far_ref,
+    from_far_ref,
     from_near_ref,
-    from_far_ref,
     w_in_ref,
     w_out_ref,
     w_gate_ref,
@@ -223,15 +287,8 @@
     strip_width = (TILES - STRIP) * LANES
     strip_lane = lax.broadcasted_iota(jnp.int32, (8, strip_width), 1)
 
-    def tile(index, count=1):
-        return slice(index * LANES, (index + count) * LANES)
-
-    def at(row):
-        return tile(row + FIRST)
-
     def within(row):
-        row = row + lat * ROWS
-        return (row >= 0) & (row < lat_count * ROWS)
+        return row_mask(place_ref, lat_count, row)
 
     def left(main, strip, row):
         part, place = strip_place(row)
@@ -272,11 +329,11 @@
         mask_ref[:, at(row)] = jnp.where(within(row), jnp.ones((8, LANES), F32), 0.0)
     mask_ref[:, strips] = jnp.where(within(strip_lane // 32 - 6), 1.0, 0.0)
 
-    ones = jnp.where(lax.broadcasted_iota(jnp.int32, (8, LANES), 0) < 3, 1.0, 0.0).astype(F32)
+    ones = ones_rows()
 
     def windows(ref, first_row, last_row, with_strips):
         strip = ref[:, strips]
-        for row in range(first_row - 1, last_row + 2):
+        for row in range(first_row - 1, last_row + 2) if first_row <= last_row else ():
             main = ref[:, at(row)]
             minus_ref[:, at(row)] = left(main, strip, row)
             plus_ref[:, at(row)] = right(main, strip, row)
@@ -295,9 +352,9 @@
         runs = [(first_row + FIRST, last_row + 1 + FIRST), (STRIP, TILES)]
         return [tile(t, min(GROUP, end - t)) for start, end in runs for t in range(start, end, GROUP)]
 
-    def gradient(first_row, last_row):
-        windows(est_ref, first_row - 1, last_row + 1, True)
-        for where in pieces_of(first_row - 1, last_row + 1):
+    def gradient(first_row, last_row, low, high):
+        windows(est_ref, low, high, True)
+        for where in pieces_of(low, high):
             value = jnp.dot(w_in_ref[:, 0:80], window_ref[:, where], preferred_element_type=F32)
             value = jnp.maximum(value, 0.0) * mask_ref[0:1, where]
             spread_ref[:, where] = jnp.dot(w_out_ref[...], value.astype(BF16), preferred_element_type=F32)
@@ -310,20 +367,26 @@
                 piece = lane_roll(piece, 32 - 32 * a) if a != 1 else piece
                 total = piece if total is None else total + piece
             totals.append(total)
-        grad_ref[:, strips] = est_ref[:, strips] - (totals[1] + lane_roll(totals[0], 1) + lane_roll(totals[2], -1))
+        strip = est_ref[:, strips] - (totals[1] + lane_roll(totals[0], 1) + lane_roll(totals[2], -1))
+        grad_ref[:, strips] = strip
         for row in range(first_row, last_row + 1):
-            columns = []
-            for b in range(3):
-                terms = [spread_ref[8 * (3 * a + b) : 8 * (3 * a + b) + 8, at(row + a - 1)] for a in range(3)]
-                columns.append(terms[0] + terms[1] + terms[2])
+            columns = spread_terms(spread_ref, row)
             term = columns[1] + left(columns[0], totals[0], row) + right(columns[2], totals[2], row)
             grad_ref[:, at(row)] = est_ref[:, at(row)] - term
-
-    gradient(-4, 19)
+        return strip
+
+    strip = gradient(0, -1, 0, -1)
     for row in range(-4, 20):
-        total = grad_ref[:, at(row)] + adjoint_ref[row + 4]
+        part, place = strip_place(row)
+        edges = strip[:, tile(part)]
+        total = jnp.where(
+            lane < 2,
+            lane_roll(edges, -(place + 8)),
+            jnp.where(lane >= 126, lane_roll(edges, 126 - (place + 22)), first_ref[row + 4]),
+        )
+        total = total + adjoint_ref[row + 4]
         grad_ref[:, at(row)] = total if 0 <= row < ROWS else total * mask_ref[:, at(row)]
-    grad_ref[:, strips] = (grad_ref[:, strips] + adjoint_strip) * mask_ref[:, strips]
+    grad_ref[:, strips] = (strip + adjoint_strip) * mask_ref[:, strips]
     windows(grad_ref, -3, 18, True)
     for where in pieces_of(-3, 18):
         sums = jnp.dot(w_gate_ref[HID:, 0:80], window_ref[:, where], preferred_element_type=F32)
@@ -347,7 +410,7 @@
         hid_plus_ref[:, at(row)] = jnp.where(
             lane64 == 127, lane_roll(strip, 127 - (place + 24)), lane_roll(main, -1)
         ).astype(BF16)
-    gradient(-1, 16)
+    gradient(-1, 16, -2, 17)
     carried = zero
     for row in range(-2, ROWS + 1):
         now, later = adjoint_terms(sums_ref, row + 5, est_ref[:, at(row)], est_ref[:, at(row + 1)])
@@ -419,33 +482,36 @@
     lat = lax.axis_index("lat").astype(jnp.int32)
     lon = lax.axis_index("lon").astype(jnp.int32)
     place = jnp.stack([lat, lon])
-    upper, lower = state[:, ROWS - HALO :], state[:, :HALO]
-    even_lat = lat % 2 == 0
-    far = swap(jnp.where(even_lat, lower, upper), "lat", 1, lat_count, False).reshape(DAYS * HALO, LANES)
-    near = swap(jnp.where(even_lat, upper, lower), "lat", 0, lat_count, False).reshape(DAYS * HALO, LANES)
     mid = state.reshape(DAYS * ROWS, LANES)
 
     smem = pl.BlockSpec(memory_space=pltpu.SMEM)
     vmem = pl.BlockSpec(memory_space=pltpu.VMEM)
-    track = pl.pallas_call(
+    track, lat_near, lat_far = pl.pallas_call(
         track_kernel,
-        out_shape=jax.ShapeDtypeStruct((lat_count * 8, TRACK), BF16),
-        in_specs=[vmem] * 6,
-        out_specs=vmem,
+        out_shape=(
+            jax.ShapeDtypeStruct((lat_count * 8, TRACK), BF16),
+            jax.ShapeDtypeStruct((DAYS * HALO, LANES), F32),
+            jax.ShapeDtypeStruct((DAYS * HALO, LANES), F32),
+        ),
+        in_specs=[smem] + [vmem] * 7,
+        out_specs=(vmem, vmem, vmem),
         cost_estimate=pl.CostEstimate(flops=100_000, bytes_accessed=150_000, transcendentals=0),
         name="track",
     )(
+        place,
         obs_value.reshape(1, TRACK),
         obs_weight,
         obs_tile.reshape(1, TRACK),
         obs_time.reshape(1, TRACK),
         obs_row.reshape(1, TRACK),
         obs_col.reshape(1, TRACK),
+        mid,
     )
-    track, near, far = lax.optimization_barrier((track, near, far))
     gathered = lax.all_to_all(
         track.reshape(lat_count, 8, TRACK), "lat", split_axis=0, concat_axis=0, tiled=True
     ).reshape(lat_count * 8, TRACK)
+    far = swap(lat_far, "lat", 1, lat_count, False)
+    near = swap(lat_near, "lat", 0, lat_count, False)
     w_gate, w_in, w_out, w_inc = pl.pallas_call(
         prepare_kernel,
         out_shape=(
@@ -467,7 +533,29 @@
         prior_out,
         lstm_out,
     )
-    sums, adjoint, to_near, to_far = pl.pallas_call(
+    width = TILES * LANES
+    main_width = STRIP * LANES
+
+    def first(*refs):
+        first_kernel(*refs, lat_count=lat_count)
+
+    started = pl.pallas_call(
+        first,
+        out_shape=jax.ShapeDtypeStruct((24, 8, LANES), F32),
+        in_specs=[smem] + [vmem] * 5,
+        out_specs=vmem,
+        scratch_shapes=[
+            pltpu.VMEM((8, main_width), F32),
+            pltpu.VMEM((8, main_width), F32),
+            pltpu.VMEM((8, main_width), F32),
+            pltpu.VMEM((80, main_width), BF16),
+            pltpu.VMEM((80, main_width), F32),
+        ],
+        compiler_params=pltpu.CompilerParams(vmem_limit_bytes=16 * 1024 * 1024),
+        cost_estimate=pl.CostEstimate(flops=2_000_000_000, bytes_accessed=500_000, transcendentals=0),
+        name="first",
+    )(place, mid, near, far, w_in, w_out)
+    sums, adjoint, to_far, to_near = pl.pallas_call(
         build_kernel,
         out_shape=(
             jax.ShapeDtypeStruct((8, 256, LANES), F32),
@@ -492,14 +580,13 @@
     def solve(*refs):
         solve_kernel(*refs, lat_count=lat_count)
 
-    width = TILES * LANES
     estimate, cell_state = pl.pallas_call(
         solve,
         out_shape=(
             jax.ShapeDtypeStruct((DAYS * ROWS, LANES), F32),
             jax.ShapeDtypeStruct((HID * ROWS, LANES), F32),
         ),
-        in_specs=[smem] + [vmem] * 13,
+        in_specs=[smem] + [vmem] * 14,
         out_specs=(vmem, vmem),
         scratch_shapes=[
             pltpu.VMEM((8, width), F32),
@@ -516,7 +603,7 @@
         ],
         compiler_params=pltpu.CompilerParams(vmem_limit_bytes=32 * 1024 * 1024),
         name="solve",
-    )(place, mid, near, far, sums, adjoint, to_near, to_far, from_near, from_far, w_in, w_out, w_gate, w_inc)
+    )(place, mid, near, far, sums, adjoint, started, to_far, to_near, from_far, from_near, w_in, w_out, w_gate, w_inc)
     return (
         estimate.reshape(DAYS, ROWS, LANES),
         cell_state.reshape(HID, ROWS, LANES),

time: 57.4 us -> 50.8 us (0.89)
  the two profiles are of different devices: /device:TPU:29 before, /device:TPU:31 now
where the time goes in v3:
time: 50.8 us; the launch traced here: 50.3 us
  starting transfers between devices  28.5 us (56%)
  Pallas kernels  18.2 us (36%)
  local copies, waits for them, and re-layouts  1.39 us (3%)
  waiting for transfers between devices  0.8 us (2%)
  between operations  0.75 us (1%)
  other arithmetic  0.66 us (1%)
    ppermute x4, starting transfers between devices, swap(): lax.ppermute(value, axis, pairs + [(target, source) for source, target in...  17.1 us
    all_to_all x1, starting transfers between devices, on_device(): lax.all_to_all(track.reshape(lat_count, 8, TRACK), 'lat', split_axis=0, c...  11.4 us
    pallas_call x1, Pallas kernels, on_device(): pl.pallas_call(solve, out_shape=(jax.ShapeDtypeStruct((DAYS * ROWS, LANES...  8.07 us
    pallas_call x1, Pallas kernels, on_device(): pl.pallas_call(build_kernel, out_shape=(jax.ShapeDtypeStruct((8, 256, LAN...  6.47 us
    pallas_call x1, Pallas kernels, on_device(): pl.pallas_call(first, out_shape=jax.ShapeDtypeStruct((24, 8, LANES), F32)...  1.82 us
    pallas_call x1, Pallas kernels, on_device(): pl.pallas_call(track_kernel, out_shape=(jax.ShapeDtypeStruct((lat_count *...  1.56 us
    unnamed x16, local copies, waits for them, and re-layouts  1.39 us
  transfers between devices with their start and end apart: 5, of which 1 were waited for; matrix products, arithmetic and copies ran while one was open for 0% of the time, Pallas kernels for 4%

profile of v3, /device:TPU:31, one launch (start us, length us, event | category | flops | bytes accessed | tf_op | source)
XLA Modules:
  0.0 50.3 jit_solution(18345411353731897941)
XLA Ops:
  0.6 0.0 copy-start
  0.6 0.7 %pad_add_fusion.place_ref.refs_0_ = s32[2]{0:T(128)} fusion(s32[1]{0:T(128)} %bitcast.1, s32[1]{0:T(128)} %bitcast), kind=kLoop, calls=%fused_computation | loop fusion | flops 2 | bytes 16 | tf_op jit(solution)/shard_map/stack | solution.py:484
  1.3 1.6 %track.1 = (bf16[128,512]{1,0:T(8,128)(2,1)}, f32[40,128]{1,0:T(8,128)}, f32[40,128]{1,0:T(8,128)}) custom-call(s32[2]{0:T(128)} %pad_add_fusion.place_ref.refs_0_, f32[1,512]{1,0:T(1,128)} %bitcast.26, f32[4,512]{1,0:T(4,128)} %weight_ref.1, s32[1,512]{1,0:T(1,128)} %bitcast.27, s32[1,512]{1,0:T(1,128)} %bitcast.28, s32[1,512]{1,0:T(1,128)} %bitcast.29, ...), custom_call_target="tpu_custom_call" | custom-call | flops 100000 | bytes 150000 | tf_op jit(solution)/shard_map/track/pallas_call | solution.py:489
  2.9 0.0 copy-start.2
  2.9 11.4 %all-to-all-start = ((bf16[16,8,512]{2,1,0:T(8,128)(2,1)}), bf16[16,8,512]{2,1,0:T(8,128)(2,1)S(1)}, u32[]{:S(2)}, u32[]{:S(2)}) async-start(bf16[16,8,512]{2,1,0:T(8,128)(2,1)} %bitcast.25), calls=%async_computation | async-start | bytes 262144 | tf_op jit(solution)/shard_map/all_to_all | solution.py:510
  14.2 3.1 %collective-permute-start = (f32[40,128]{1,0:T(8,128)}, f32[40,128]{1,0:T(8,128)S(1)}, u32[]{:S(2)}, u32[]{:S(2)}) collective-permute-start(f32[40,128]{1,0:T(8,128)} %get-tuple-element.15), channel_id=1, source_target_pairs={{0,1},{2,3},{4,5},{6,7},{8,9},{10,11},{12,13},{14,15},{1,0},{3,2},... | collective-permute-start | bytes 61448 | tf_op jit(solution)/shard_map/ppermute | solution.py:462
  17.3 4.3 %collective-permute-start.1 = (f32[40,128]{1,0:T(8,128)}, f32[40,128]{1,0:T(8,128)S(1)}, u32[]{:S(2)}, u32[]{:S(2)}) collective-permute-start(f32[40,128]{1,0:T(8,128)} %get-tuple-element.16), channel_id=1, source_target_pairs={{1,2},{3,4},{5,6},{7,8},{9,10},{11,12},{13,14},{2,1},{4,3},{6,5},{... | collective-permute-start | bytes 61448 | tf_op jit(solution)/shard_map/ppermute | solution.py:462
  21.6 0.0 copy-start.4
  21.6 0.0 copy-start.6
  21.7 0.0 copy-start.7
  21.7 0.0 copy-done
  21.7 0.0 copy-done.2
  21.7 0.6 %copy-done.4 = bf16[5,64]{1,0:T(8,128)(2,1)S(1)} copy-done((bf16[5,64]{1,0:T(8,128)(2,1)S(1)}, bf16[5,64]{1,0:T(8,128)(2,1)}, u32[]{:S(2)}) %copy-start.4) | copy-done | bytes 664
  22.3 0.0 copy-done.6
  22.3 0.0 copy-done.7
  22.3 0.0 copy-start.3
  22.3 0.7 %copy-done.3 = bf16[9,5,64]{2,1,0:T(8,128)(2,1)S(1)} copy-done((bf16[9,5,64]{2,1,0:T(8,128)(2,1)S(1)}, bf16[9,5,64]{2,1,0:T(8,128)(2,1)}, u32[]{:S(2)}) %copy-start.3) | copy-done | bytes 5784
  23.1 0.0 copy-start.1
  23.1 0.3 prepare.1
  23.4 0.0 copy-start.5
  23.4 0.0 collective-permute-done.near_ref.refs_2_
  23.4 0.8 %collective-permute-done.1.far_ref.refs_3_ = f32[40,128]{1,0:T(8,128)S(1)} collective-permute-done((f32[40,128]{1,0:T(8,128)}, f32[40,128]{1,0:T(8,128)S(1)}, u32[]{:S(2)}, u32[]{:S(2)}) %collective-permute-start.1) | collective-permute-done | bytes 20512 | tf_op jit(solution)/shard_map/ppermute | solution.py:462
  24.2 0.0 all-to-all-done
  24.2 0.0 copy-done.1
  24.2 0.0 copy-done.5
  24.2 6.5 %build.1 = (f32[8,256,128]{2,1,0:T(8,128)S(1)}, f32[24,8,128]{2,1,0:T(8,128)S(1)}, f32[56,128]{1,0:T(8,128)S(1)}, f32[56,128]{1,0:T(8,128)S(1)}) custom-call(s32[2]{0:T(128)S(1)} %copy-done.5, bf16[128,512]{1,0:T(8,128)(2,1)S(1)} %bitcast.21, f32[80,128]{1,0:T(8,128)S(1)} %bitcast.18, f32[40,128]{1,0:T(8,128)S(1)} %collective-permute-done.near_ref.refs_2_, ...), custom_call_target="tpu_custom_call" | custom-call | flops 4000000000 | bytes 1500000 | tf_op jit(solution)/shard_map/build/pallas_call | solution.py:558
  30.7 7.8 %collective-permute-start.2 = (f32[56,128]{1,0:T(8,128)S(1)}, f32[56,128]{1,0:T(8,128)S(1)}, u32[]{:S(2)}, u32[]{:S(2)}) collective-permute-start(f32[56,128]{1,0:T(8,128)S(1)} %get-tuple-element.22.refs_7_), channel_id=1, source_target_pairs={{16,32},{48,64},{80,96},{112,128},{144,160},{176,192},{208,224},{2... | collective-permute-start | bytes 86024 | tf_op jit(solution)/shard_map/ppermute | solution.py:462
  38.5 1.9 %collective-permute-start.3 = (f32[56,128]{1,0:T(8,128)S(1)}, f32[56,128]{1,0:T(8,128)S(1)}, u32[]{:S(2)}, u32[]{:S(2)}) collective-permute-start(f32[56,128]{1,0:T(8,128)S(1)} %get-tuple-element.23.refs_8_), channel_id=1, source_target_pairs={{0,16},{32,48},{64,80},{96,112},{128,144},{160,176},{192,208},{224... | collective-permute-start | bytes 86024 | tf_op jit(solution)/shard_map/ppermute | solution.py:462
  40.4 1.8 %first.1.refs_6_ = f32[24,8,128]{2,1,0:T(8,128)S(1)} custom-call(s32[2]{0:T(128)S(1)} %copy-done.5, f32[80,128]{1,0:T(8,128)S(1)} %bitcast.19, f32[40,128]{1,0:T(8,128)S(1)} %collective-permute-done.near_ref.refs_2_, f32[40,128]{1,0:T(8,128)S(1)} %collective-permute-done.1.far_ref.refs_3_, bf16[64,128]{1,0:T(8,128)(2,1)S(1)} %get-tuple-element.20.refs_4_.refs_11_, ...), custom_call_target="tpu_custom_call" | custom-call | flops 2000000000 | bytes 500000 | tf_op jit(solution)/shard_map/first/pallas_call | solution.py:542
  42.2 0.0 collective-permute-done.2.refs_9_
  42.2 0.0 collective-permute-done.3.refs_10_
  42.2 8.1 %solve.1 = (f32[80,128]{1,0:T(8,128)}, f32[1024,128]{1,0:T(8,128)}) custom-call(s32[2]{0:T(128)S(1)} %copy-done.5, f32[80,128]{1,0:T(8,128)S(1)} %bitcast.20, f32[40,128]{1,0:T(8,128)S(1)} %collective-permute-done.near_ref.refs_2_, f32[40,128]{1,0:T(8,128)S(1)} %collective-permute-done.1.far_ref.refs_3_, f32[8,256,128]{2,1,0:T(8,128)S(1)} %get-tuple-element.18.refs_4_, ...), custom_call_target="tpu_custom_call" | custom-call | tf_op jit(solution)/shard_map/solve/pallas_call | solution.py:583
Async XLA Ops:
  0.6 21.0 %copy-start = (bf16[9,256,69]{1,2,0:T(8,128)(2,1)S(1)}, bf16[9,256,69]{1,2,0:T(8,128)(2,1)}, u32[]{:S(2)}) copy-start(bf16[9,256,69]{1,2,0:T(8,128)(2,1)} %param.17) | copy-start | bytes 953860
  2.9 18.8 %copy-start.2 = (bf16[9,64,5]{1,2,0:T(8,128)(2,1)S(1)}, bf16[9,64,5]{1,2,0:T(8,128)(2,1)}, u32[]{:S(2)}) copy-start(bf16[9,64,5]{1,2,0:T(8,128)(2,1)} %param.14) | copy-start | bytes 17284
  2.9 21.3 %all-to-all-start = ((bf16[16,8,512]{2,1,0:T(8,128)(2,1)}), bf16[16,8,512]{2,1,0:T(8,128)(2,1)S(1)}, u32[]{:S(2)}, u32[]{:S(2)}) async-start(bf16[16,8,512]{2,1,0:T(8,128)(2,1)} %bitcast.25), calls=%async_computation | async-start | bytes 262144 | tf_op jit(solution)/shard_map/all_to_all | solution.py:510
  14.2 9.1 %collective-permute-start = (f32[40,128]{1,0:T(8,128)}, f32[40,128]{1,0:T(8,128)S(1)}, u32[]{:S(2)}, u32[]{:S(2)}) collective-permute-start(f32[40,128]{1,0:T(8,128)} %get-tuple-element.15), channel_id=1, source_target_pairs={{0,1},{2,3},{4,5},{6,7},{8,9},{10,11},{12,13},{14,15},{1,0},{3,2},... | collective-permute-start | bytes 61448 | tf_op jit(solution)/shard_map/ppermute | solution.py:462
  17.3 6.8 %collective-permute-start.1 = (f32[40,128]{1,0:T(8,128)}, f32[40,128]{1,0:T(8,128)S(1)}, u32[]{:S(2)}, u32[]{:S(2)}) collective-permute-start(f32[40,128]{1,0:T(8,128)} %get-tuple-element.16), channel_id=1, source_target_pairs={{1,2},{3,4},{5,6},{7,8},{9,10},{11,12},{13,14},{2,1},{4,3},{6,5},{... | collective-permute-start | bytes 61448 | tf_op jit(solution)/shard_map/ppermute | solution.py:462
  21.6 0.7 %copy-start.4 = (bf16[5,64]{1,0:T(8,128)(2,1)S(1)}, bf16[5,64]{1,0:T(8,128)(2,1)}, u32[]{:S(2)}) copy-start(bf16[5,64]{1,0:T(8,128)(2,1)} %inc_ref.1) | copy-start | bytes 1924
  21.6 0.7 %copy-start.6 = (f32[256]{0:T(256)S(1)}, f32[256]{0:T(256)}, u32[]{:S(2)}) copy-start(f32[256]{0:T(256)} %param.18) | copy-start | bytes 3076
  21.7 0.7 %copy-start.7 = (f32[64]{0:T(128)S(1)}, f32[64]{0:T(128)}, u32[]{:S(2)}) copy-start(f32[64]{0:T(128)} %param.15) | copy-start | bytes 772
  22.3 0.7 %copy-start.3 = (bf16[9,5,64]{2,1,0:T(8,128)(2,1)S(1)}, bf16[9,5,64]{2,1,0:T(8,128)(2,1)}, u32[]{:S(2)}) copy-start(bf16[9,5,64]{2,1,0:T(8,128)(2,1)} %out_ref.1) | copy-start | bytes 17284
  23.1 1.1 %copy-start.1 = (f32[5,16,128]{2,1,0:T(8,128)S(1)}, f32[5,16,128]{2,1,0:T(8,128)}, u32[]{:S(2)}) copy-start(f32[5,16,128]{2,1,0:T(8,128)} %param.13) | copy-start | bytes 122884
  23.4 0.8 %copy-start.5 = (s32[2]{0:T(128)S(1)}, s32[2]{0:T(128)}, u32[]{:S(2)}) copy-start(s32[2]{0:T(128)} %pad_add_fusion.place_ref.refs_0_) | copy-start | bytes 28
  30.7 11.6 %collective-permute-start.2 = (f32[56,128]{1,0:T(8,128)S(1)}, f32[56,128]{1,0:T(8,128)S(1)}, u32[]{:S(2)}, u32[]{:S(2)}) collective-permute-start(f32[56,128]{1,0:T(8,128)S(1)} %get-tuple-element.22.refs_7_), channel_id=1, source_target_pairs={{16,32},{48,64},{80,96},{112,128},{144,160},{176,192},{208,224},{2... | collective-permute-start | bytes 86024 | tf_op jit(solution)/shard_map/ppermute | solution.py:462
  38.5 3.8 %collective-permute-start.3 = (f32[56,128]{1,0:T(8,128)S(1)}, f32[56,128]{1,0:T(8,128)S(1)}, u32[]{:S(2)}, u32[]{:S(2)}) collective-permute-start(f32[56,128]{1,0:T(8,128)S(1)} %get-tuple-element.23.refs_8_), channel_id=1, source_target_pairs={{0,16},{32,48},{64,80},{96,112},{128,144},{160,176},{192,208},{224... | collective-permute-start | bytes 86024 | tf_op jit(solution)/shard_map/ppermute | solution.py:462

commit v4 on v3

--- a/solution.py
+++ b/solution.py
@@ -63,7 +63,7 @@
 
 
 def track_kernel(
-    place_ref, value_ref, weight_ref, tile_ref, time_ref, row_ref, col_ref, state_ref, out_ref, to_near_ref, to_far_ref
+    value_ref, weight_ref, tile_ref, time_ref, row_ref, col_ref, state_ref, out_ref, to_near_ref, to_far_ref
 ):
     latitude = tile_ref[...] * ROWS + row_ref[...]
     keys = [time_ref[...].astype(F32), latitude.astype(F32), col_ref[...].astype(F32)]
@@ -71,7 +71,7 @@
     twice = jnp.concatenate([block, block], axis=0).astype(BF16)
     for k in range(out_ref.shape[0] // 16):
         out_ref[16 * k : 16 * k + 16, :] = twice
-    even = place_ref[0] % 2 == 0
+    even = lax.axis_index("lat") % 2 == 0
     for day in range(DAYS):
         lower = state_ref[ROWS * day : ROWS * day + HALO, :]
         upper = state_ref[ROWS * (day + 1) - HALO : ROWS * (day + 1), :]
@@ -117,12 +117,17 @@
 WEST_LANES = ((0, 1, 2, 3, 4), (5, 3, 6, 7, 8))
 
 
-def build_kernel(
-    place_ref, track_ref, mid_ref, near_ref, far_ref, sums_ref, adjoint_ref, to_far_ref, to_near_ref, rw_ref, cw_ref
-):
-    base_row = (place_ref[0] * ROWS - 5).astype(F32)
-    even_lat = place_ref[0] % 2 == 0
-    even_lon = place_ref[1] % 2 == 0
+PRODUCTS = (
+    ((0, 512), (384, 640), {(0, 0): (3, 1), (1, 0): (3, 0), (2, 0): (6, 0), (3, 0): (6, 1), (0, 1): (4, 1), (1, 1): (4, 0), (2, 1): (7, 0), (3, 1): (7, 1)}),
+    ((0, 256), (128, 384), {(0, 0): (2, 1), (1, 0): (2, 0), (0, 1): (1, 1), (1, 1): (1, 0)}),
+    ((128, 384), (0, 256), {(0, 0): (0, 0), (1, 1): (5, 0)}),
+)
+ROW_WEIGHTS = (1, 0, 2, 3)
+COL_WEIGHTS = (0, 2, 1, 3, -1)
+
+
+def sums_kernel(track_ref, sums_ref, rw_ref, cw_ref):
+    base_row = (lax.axis_index("lat") * ROWS - 5).astype(F32)
     entry = lax.broadcasted_iota(jnp.int32, (LANES, TRACK), 0).astype(F32).astype(BF16)
     nothing = jnp.zeros((LANES, TRACK), BF16)
 
@@ -139,23 +144,29 @@
             both = track_ref[first_row : first_row + 16, :].astype(F32)
             for part in range(2):
                 block = both[8 * part : 8 * part + 8]
-                at = (2 * pair + part) * TRACK
+                start = (2 * pair + part) * TRACK
                 offset = block[6:7] - base_row
                 within = (offset >= 0.0) & (offset < float(BASES))
                 row_hit = entry == spread(jnp.where(within, offset * 5.0 + block[5:6], -1.0))
                 col_hit = entry == spread(block[7:8])
-                for k in range(5):
-                    source = (1 + k) % 5
+                for source in range(5):
                     value = spread(block[source : source + 1])
-                    if k < 4:
-                        rw_ref[slot, 128 * k : 128 * k + 128, at : at + TRACK] = jnp.where(row_hit, value, nothing)
-                    cw_ref[slot, 128 * k : 128 * k + 128, at : at + TRACK] = jnp.where(col_hit, value, nothing)
-        first = nt_dot(rw_ref[slot, 0:256, :], cw_ref[slot])
-        second = nt_dot(rw_ref[slot, 256:512, :], cw_ref[slot, 256:640, :])
-        for k in range(8):
-            total = first[:, 128 * k : 128 * k + 128] if k < 5 else second[:, 128 * k - 640 : 128 * k - 512]
-            sums_ref[k] = total if chunk == 0 else sums_ref[k] + total
-
+                    if source > 0:
+                        k = ROW_WEIGHTS.index(source - 1)
+                        rw_ref[slot, 128 * k : 128 * k + 128, start : start + TRACK] = jnp.where(row_hit, value, nothing)
+                    k = COL_WEIGHTS.index(source - 1)
+                    cw_ref[slot, 128 * k : 128 * k + 128, start : start + TRACK] = jnp.where(col_hit, value, nothing)
+        for (row0, row1), (col0, col1), blocks in PRODUCTS:
+            product = nt_dot(rw_ref[slot, row0:row1, :], cw_ref[slot, col0:col1, :])
+            for (i, j), (array, half) in blocks.items():
+                total = product[128 * i : 128 * i + 128, 128 * j : 128 * j + 128]
+                rows = slice(LANES * half, LANES * half + LANES)
+                sums_ref[array, rows, :] = total if chunk == 0 else sums_ref[array, rows, :] + total
+
+
+def edges_kernel(mid_ref, near_ref, far_ref, sums_ref, adjoint_ref, to_far_ref, to_near_ref):
+    even_lat = lax.axis_index("lat") % 2 == 0
+    even_lon = lax.axis_index("lon") % 2 == 0
     lane = lax.broadcasted_iota(jnp.int32, (8, LANES), 1)
     zero = jnp.zeros((8, LANES), F32)
     east, west = zero, zero
@@ -191,8 +202,8 @@
             east, west = zero, zero
 
 
-def row_mask(place_ref, lat_count, row):
-    row = row + place_ref[0] * ROWS
+def row_mask(lat_count, row):
+    row = row + lax.axis_index("lat") * ROWS
     return (row >= 0) & (row < lat_count * ROWS)
 
 
@@ -217,9 +228,9 @@
 
 
 def first_kernel(
-    place_ref, mid_ref, near_ref, far_ref, w_in_ref, w_out_ref, out_ref, est_ref, minus_ref, plus_ref, window_ref, spread_ref, *, lat_count
+    mid_ref, near_ref, far_ref, w_in_ref, w_out_ref, out_ref, est_ref, minus_ref, plus_ref, window_ref, spread_ref, *, lat_count
 ):
-    even_lat = place_ref[0] % 2 == 0
+    even_lat = lax.axis_index("lat") % 2 == 0
     for row in range(-6, 22):
         value = day_rows(near_ref, mid_ref, far_ref, even_lat, row)
         est_ref[:, at(row)] = value
@@ -236,7 +247,7 @@
         value = jnp.maximum(value, 0.0)
         if row < 0 or row >= ROWS:
             flags = [
-                jnp.where(row_mask(place_ref, lat_count, row + k), jnp.ones((1, LANES), F32), 0.0) for k in range(count)
+                jnp.where(row_mask(lat_count, row + k), jnp.ones((1, LANES), F32), 0.0) for k in range(count)
             ]
             value = value * jnp.concatenate(flags, axis=1)
         spread_ref[:, where] = jnp.dot(w_out_ref[...], value.astype(BF16), preferred_element_type=F32)
@@ -247,7 +258,6 @@
 
 
 def solve_kernel(
-    place_ref,
     mid_ref,
     near_ref,
     far_ref,
@@ -278,9 +288,8 @@
     *,
     lat_count,
 ):
-    lat = place_ref[0]
-    even_lat = lat % 2 == 0
-    even_lon = place_ref[1] % 2 == 0
+    even_lat = lax.axis_index("lat") % 2 == 0
+    even_lon = lax.axis_index("lon") % 2 == 0
     lane = lax.broadcasted_iota(jnp.int32, (8, LANES), 1)
     zero = jnp.zeros((8, LANES), F32)
     strips = slice(STRIP * LANES, TILES * LANES)
@@ -288,7 +297,7 @@
     strip_lane = lax.broadcasted_iota(jnp.int32, (8, strip_width), 1)
 
     def within(row):
-        return row_mask(place_ref, lat_count, row)
+        return row_mask(lat_count, row)
 
     def left(main, strip, row):
         part, place = strip_place(row)
@@ -479,12 +488,8 @@
 ):
     lat_count = lax.axis_size("lat")
     lon_count = lax.axis_size("lon")
-    lat = lax.axis_index("lat").astype(jnp.int32)
-    lon = lax.axis_index("lon").astype(jnp.int32)
-    place = jnp.stack([lat, lon])
     mid = state.reshape(DAYS * ROWS, LANES)
 
-    smem = pl.BlockSpec(memory_space=pltpu.SMEM)
     vmem = pl.BlockSpec(memory_space=pltpu.VMEM)
     track, lat_near, lat_far = pl.pallas_call(
         track_kernel,
@@ -493,12 +498,11 @@
             jax.ShapeDtypeStruct((DAYS * HALO, LANES), F32),
             jax.ShapeDtypeStruct((DAYS * HALO, LANES), F32),
         ),
-        in_specs=[smem] + [vmem] * 7,
+        in_specs=[vmem] * 7,
         out_specs=(vmem, vmem, vmem),
         cost_estimate=pl.CostEstimate(flops=100_000, bytes_accessed=150_000, transcendentals=0),
         name="track",
     )(
-        place,
         obs_value.reshape(1, TRACK),
         obs_weight,
         obs_tile.reshape(1, TRACK),
@@ -542,7 +546,7 @@
     started = pl.pallas_call(
         first,
         out_shape=jax.ShapeDtypeStruct((24, 8, LANES), F32),
-        in_specs=[smem] + [vmem] * 5,
+        in_specs=[vmem] * 5,
         out_specs=vmem,
         scratch_shapes=[
             pltpu.VMEM((8, main_width), F32),
@@ -554,25 +558,33 @@
         compiler_params=pltpu.CompilerParams(vmem_limit_bytes=16 * 1024 * 1024),
         cost_estimate=pl.CostEstimate(flops=2_000_000_000, bytes_accessed=500_000, transcendentals=0),
         name="first",
-    )(place, mid, near, far, w_in, w_out)
-    sums, adjoint, to_far, to_near = pl.pallas_call(
-        build_kernel,
-        out_shape=(
-            jax.ShapeDtypeStruct((8, 256, LANES), F32),
-            jax.ShapeDtypeStruct((24, 8, LANES), F32),
-            jax.ShapeDtypeStruct((56, LANES), F32),
-            jax.ShapeDtypeStruct((56, LANES), F32),
-        ),
-        in_specs=[smem, vmem, vmem, vmem, vmem],
-        out_specs=(vmem, vmem, vmem, vmem),
+    )(mid, near, far, w_in, w_out)
+    sums = pl.pallas_call(
+        sums_kernel,
+        out_shape=jax.ShapeDtypeStruct((8, 256, LANES), F32),
+        in_specs=[vmem],
+        out_specs=vmem,
         scratch_shapes=[
             pltpu.VMEM((2, 512, CHUNK), BF16),
             pltpu.VMEM((2, 640, CHUNK), BF16),
         ],
         compiler_params=pltpu.CompilerParams(vmem_limit_bytes=32 * 1024 * 1024),
         cost_estimate=pl.CostEstimate(flops=4_000_000_000, bytes_accessed=1_500_000, transcendentals=0),
-        name="build",
-    )(place, gathered, mid, near, far)
+        name="sums",
+    )(gathered)
+    adjoint, to_far, to_near = pl.pallas_call(
+        edges_kernel,
+        out_shape=(
+            jax.ShapeDtypeStruct((24, 8, LANES), F32),
+            jax.ShapeDtypeStruct((56, LANES), F32),
+            jax.ShapeDtypeStruct((56, LANES), F32),
+        ),
+        in_specs=[vmem] * 4,
+        out_specs=(vmem, vmem, vmem),
+        compiler_params=pltpu.CompilerParams(vmem_limit_bytes=16 * 1024 * 1024),
+        cost_estimate=pl.CostEstimate(flops=1_000_000, bytes_accessed=1_500_000, transcendentals=0),
+        name="edges",
+    )(mid, near, far, sums)
 
     from_far = swap(to_far, "lon", 1, lon_count, True)
     from_near = swap(to_near, "lon", 0, lon_count, True)
@@ -586,7 +598,7 @@
             jax.ShapeDtypeStruct((DAYS * ROWS, LANES), F32),
             jax.ShapeDtypeStruct((HID * ROWS, LANES), F32),
         ),
-        in_specs=[smem] + [vmem] * 14,
+        in_specs=[vmem] * 14,
         out_specs=(vmem, vmem),
         scratch_shapes=[
             pltpu.VMEM((8, width), F32),
@@ -603,7 +615,7 @@
         ],
         compiler_params=pltpu.CompilerParams(vmem_limit_bytes=32 * 1024 * 1024),
         name="solve",
-    )(place, mid, near, far, sums, adjoint, started, to_far, to_near, from_far, from_near, w_in, w_out, w_gate, w_inc)
+    )(mid, near, far, sums, adjoint, started, to_far, to_near, from_far, from_near, w_in, w_out, w_gate, w_inc)
     return (
         estimate.reshape(DAYS, ROWS, LANES),
         cell_state.reshape(HID, ROWS, LANES),

time: 50.8 us -> 48.6 us (0.957)
  the two profiles are of different devices: /device:TPU:31 before, /device:TPU:3 now
where the time goes in v4:
time: 48.6 us; the launch traced here: 48.2 us
  starting transfers between devices  27.6 us (57%)
  Pallas kernels  17.7 us (36%)
  local copies, waits for them, and re-layouts  2.12 us (4%)
  between operations  0.77 us (2%)
    ppermute x4, starting transfers between devices, swap(): lax.ppermute(value, axis, pairs + [(target, source) for source, target in...  16.3 us
    all_to_all x1, starting transfers between devices, on_device(): lax.all_to_all(track.reshape(lat_count, 8, TRACK), 'lat', split_axis=0, c...  11.2 us
    pallas_call x1, Pallas kernels, on_device(): pl.pallas_call(solve, out_shape=(jax.ShapeDtypeStruct((DAYS * ROWS, LANES...  7.52 us
    pallas_call x1, Pallas kernels, on_device(): pl.pallas_call(sums_kernel, out_shape=jax.ShapeDtypeStruct((8, 256, LANES...  4.52 us
    pallas_call x1, Pallas kernels, on_device(): pl.pallas_call(edges_kernel, out_shape=(jax.ShapeDtypeStruct((24, 8, LANE...  2.48 us
    unnamed x14, local copies, waits for them, and re-layouts  2.12 us
    pallas_call x1, Pallas kernels, on_device(): pl.pallas_call(track_kernel, out_shape=(jax.ShapeDtypeStruct((lat_count *...  1.6 us
    pallas_call x1, Pallas kernels, on_device(): pl.pallas_call(first, out_shape=jax.ShapeDtypeStruct((24, 8, LANES), F32)...  1.28 us
  transfers between devices with their start and end apart: 5, of which 0 were waited for; matrix products, arithmetic and copies ran while one was open for 0% of the time, Pallas kernels for 13%

profile of v4, /device:TPU:3, one launch (start us, length us, event | category | flops | bytes accessed | tf_op | source)
XLA Modules:
  0.0 48.2 jit_solution(14951805671056292340)
XLA Ops:
  0.6 0.0 copy-start.1
  0.6 1.6 %track.1 = (bf16[128,512]{1,0:T(8,128)(2,1)}, f32[40,128]{1,0:T(8,128)}, f32[40,128]{1,0:T(8,128)}) custom-call(f32[1,512]{1,0:T(1,128)} %bitcast.24, f32[4,512]{1,0:T(4,128)} %weight_ref.1, s32[1,512]{1,0:T(1,128)} %bitcast.25, s32[1,512]{1,0:T(1,128)} %bitcast.26, s32[1,512]{1,0:T(1,128)} %bitcast.27, s32[1,512]{1,0:T(1,128)} %bitcast.28, f32[80,128]{1,0:T(8,128)} %bitcast.14), custom_call_target="tpu_custom_call" | custom-call | flops 100000 | bytes 150000 | tf_op jit(solution)/shard_map/track/pallas_call | solution.py:494
  2.2 11.2 %all-to-all-start = ((bf16[16,8,512]{2,1,0:T(8,128)(2,1)}), bf16[16,8,512]{2,1,0:T(8,128)(2,1)S(1)}, u32[]{:S(2)}, u32[]{:S(2)}) async-start(bf16[16,8,512]{2,1,0:T(8,128)(2,1)} %bitcast.23), calls=%async_computation | async-start | bytes 262144 | tf_op jit(solution)/shard_map/all_to_all | solution.py:514
  13.5 3.1 %collective-permute-start = (f32[40,128]{1,0:T(8,128)}, f32[40,128]{1,0:T(8,128)S(1)}, u32[]{:S(2)}, u32[]{:S(2)}) collective-permute-start(f32[40,128]{1,0:T(8,128)} %get-tuple-element.14), channel_id=1, source_target_pairs={{0,1},{2,3},{4,5},{6,7},{8,9},{10,11},{12,13},{14,15},{1,0},{3,2},... | collective-permute-start | bytes 61448 | tf_op jit(solution)/shard_map/ppermute | solution.py:471
  16.6 4.3 %collective-permute-start.1 = (f32[40,128]{1,0:T(8,128)}, f32[40,128]{1,0:T(8,128)S(1)}, u32[]{:S(2)}, u32[]{:S(2)}) collective-permute-start(f32[40,128]{1,0:T(8,128)} %get-tuple-element.15), channel_id=1, source_target_pairs={{1,2},{3,4},{5,6},{7,8},{9,10},{11,12},{13,14},{2,1},{4,3},{6,5},{... | collective-permute-start | bytes 61448 | tf_op jit(solution)/shard_map/ppermute | solution.py:471
  20.9 0.0 copy-start.4
  20.9 0.0 copy-start.5
  20.9 0.0 copy-start.6
  20.9 0.0 copy-done.1
  20.9 0.6 %copy-done.4 = bf16[5,64]{1,0:T(8,128)(2,1)S(1)} copy-done((bf16[5,64]{1,0:T(8,128)(2,1)S(1)}, bf16[5,64]{1,0:T(8,128)(2,1)}, u32[]{:S(2)}) %copy-start.4) | copy-done | bytes 664
  21.6 0.0 copy-done.5
  21.6 0.0 copy-done.6
  21.6 0.0 copy-start.2
  21.6 0.7 %copy-done.2 = bf16[9,64,5]{1,2,0:T(8,128)(2,1)S(1)} copy-done((bf16[9,64,5]{1,2,0:T(8,128)(2,1)S(1)}, bf16[9,64,5]{1,2,0:T(8,128)(2,1)}, u32[]{:S(2)}) %copy-start.2) | copy-done | bytes 5784
  22.3 0.0 copy-start.3
  22.3 0.7 %copy-done.3 = bf16[9,5,64]{2,1,0:T(8,128)(2,1)S(1)} copy-done((bf16[9,5,64]{2,1,0:T(8,128)(2,1)S(1)}, bf16[9,5,64]{2,1,0:T(8,128)(2,1)}, u32[]{:S(2)}) %copy-start.3) | copy-done | bytes 5784
  23.0 0.3 prepare.1
  23.3 0.0 all-to-all-done
  23.3 0.0 copy-start
  23.3 4.5 %sums.1.sums_ref.refs_3_ = f32[8,256,128]{2,1,0:T(8,128)S(1)} custom-call(bf16[128,512]{1,0:T(8,128)(2,1)S(1)} %bitcast.19), custom_call_target="tpu_custom_call" | custom-call | flops 4000000000 | bytes 1500000 | tf_op jit(solution)/shard_map/sums/pallas_call | solution.py:562
  27.9 0.0 collective-permute-done.near_ref.refs_1_
  27.9 0.0 collective-permute-done.1.far_ref.refs_2_
  27.9 0.0 copy-done
  27.9 2.5 %edges.1 = (f32[24,8,128]{2,1,0:T(8,128)S(1)}, f32[56,128]{1,0:T(8,128)S(1)}, f32[56,128]{1,0:T(8,128)S(1)}) custom-call(f32[80,128]{1,0:T(8,128)S(1)} %bitcast.15, f32[40,128]{1,0:T(8,128)S(1)} %collective-permute-done.near_ref.refs_1_, f32[40,128]{1,0:T(8,128)S(1)} %collective-permute-done.1.far_ref.refs_2_, f32[8,256,128]{2,1,0:T(8,128)S(1)} %sums.1.sums_ref.refs_3_), custom_call_target="tpu_custom_call" | custom-call | flops 1000000 | bytes 1500000 | tf_op jit(solution)/shard_map/edges/pallas_call | solution.py:575
  30.4 5.4 %collective-permute-start.2 = (f32[56,128]{1,0:T(8,128)S(1)}, f32[56,128]{1,0:T(8,128)S(1)}, u32[]{:S(2)}, u32[]{:S(2)}) collective-permute-start(f32[56,128]{1,0:T(8,128)S(1)} %get-tuple-element.20.refs_6_), channel_id=1, source_target_pairs={{16,32},{48,64},{80,96},{112,128},{144,160},{176,192},{208,224},{2... | collective-permute-start | bytes 86024 | tf_op jit(solution)/shard_map/ppermute | solution.py:471
  35.8 3.5 %collective-permute-start.3 = (f32[56,128]{1,0:T(8,128)S(1)}, f32[56,128]{1,0:T(8,128)S(1)}, u32[]{:S(2)}, u32[]{:S(2)}) collective-permute-start(f32[56,128]{1,0:T(8,128)S(1)} %get-tuple-element.21.refs_7_), channel_id=1, source_target_pairs={{0,16},{32,48},{64,80},{96,112},{128,144},{160,176},{192,208},{224... | collective-permute-start | bytes 86024 | tf_op jit(solution)/shard_map/ppermute | solution.py:471
  39.3 1.3 %first.1.refs_5_ = f32[24,8,128]{2,1,0:T(8,128)S(1)} custom-call(f32[80,128]{1,0:T(8,128)S(1)} %bitcast.16, f32[40,128]{1,0:T(8,128)S(1)} %collective-permute-done.near_ref.refs_1_, f32[40,128]{1,0:T(8,128)S(1)} %collective-permute-done.1.far_ref.refs_2_, bf16[64,128]{1,0:T(8,128)(2,1)S(1)} %get-tuple-element.18.refs_3_.refs_10_, ...), custom_call_target="tpu_custom_call" | custom-call | flops 2000000000 | bytes 500000 | tf_op jit(solution)/shard_map/first/pallas_call | solution.py:546
  40.6 0.0 collective-permute-done.2.refs_8_
  40.6 0.0 collective-permute-done.3.refs_9_
  40.6 7.5 %solve.1 = (f32[80,128]{1,0:T(8,128)}, f32[1024,128]{1,0:T(8,128)}) custom-call(f32[80,128]{1,0:T(8,128)S(1)} %bitcast.17, f32[40,128]{1,0:T(8,128)S(1)} %collective-permute-done.near_ref.refs_1_, f32[40,128]{1,0:T(8,128)S(1)} %collective-permute-done.1.far_ref.refs_2_, f32[8,256,128]{2,1,0:T(8,128)S(1)} %sums.1.sums_ref.refs_3_, ...), custom_call_target="tpu_custom_call" | custom-call | tf_op jit(solution)/shard_map/solve/pallas_call | solution.py:595
Async XLA Ops:
  0.6 20.3 %copy-start.1 = (bf16[9,256,69]{1,2,0:T(8,128)(2,1)S(1)}, bf16[9,256,69]{1,2,0:T(8,128)(2,1)}, u32[]{:S(2)}) copy-start(bf16[9,256,69]{1,2,0:T(8,128)(2,1)} %param.17) | copy-start | bytes 953860
  2.2 21.1 %all-to-all-start = ((bf16[16,8,512]{2,1,0:T(8,128)(2,1)}), bf16[16,8,512]{2,1,0:T(8,128)(2,1)S(1)}, u32[]{:S(2)}, u32[]{:S(2)}) async-start(bf16[16,8,512]{2,1,0:T(8,128)(2,1)} %bitcast.23), calls=%async_computation | async-start | bytes 262144 | tf_op jit(solution)/shard_map/all_to_all | solution.py:514
  13.5 14.4 %collective-permute-start = (f32[40,128]{1,0:T(8,128)}, f32[40,128]{1,0:T(8,128)S(1)}, u32[]{:S(2)}, u32[]{:S(2)}) collective-permute-start(f32[40,128]{1,0:T(8,128)} %get-tuple-element.14), channel_id=1, source_target_pairs={{0,1},{2,3},{4,5},{6,7},{8,9},{10,11},{12,13},{14,15},{1,0},{3,2},... | collective-permute-start | bytes 61448 | tf_op jit(solution)/shard_map/ppermute | solution.py:471
  16.6 11.3 %collective-permute-start.1 = (f32[40,128]{1,0:T(8,128)}, f32[40,128]{1,0:T(8,128)S(1)}, u32[]{:S(2)}, u32[]{:S(2)}) collective-permute-start(f32[40,128]{1,0:T(8,128)} %get-tuple-element.15), channel_id=1, source_target_pairs={{1,2},{3,4},{5,6},{7,8},{9,10},{11,12},{13,14},{2,1},{4,3},{6,5},{... | collective-permute-start | bytes 61448 | tf_op jit(solution)/shard_map/ppermute | solution.py:471
  20.9 0.7 %copy-start.4 = (bf16[5,64]{1,0:T(8,128)(2,1)S(1)}, bf16[5,64]{1,0:T(8,128)(2,1)}, u32[]{:S(2)}) copy-start(bf16[5,64]{1,0:T(8,128)(2,1)} %inc_ref.1) | copy-start | bytes 1924
  20.9 0.7 %copy-start.5 = (f32[256]{0:T(256)S(1)}, f32[256]{0:T(256)}, u32[]{:S(2)}) copy-start(f32[256]{0:T(256)} %param.18) | copy-start | bytes 3076
  20.9 0.7 %copy-start.6 = (f32[64]{0:T(128)S(1)}, f32[64]{0:T(128)}, u32[]{:S(2)}) copy-start(f32[64]{0:T(128)} %param.15) | copy-start | bytes 772
  21.6 0.7 %copy-start.2 = (bf16[9,64,5]{1,2,0:T(8,128)(2,1)S(1)}, bf16[9,64,5]{1,2,0:T(8,128)(2,1)}, u32[]{:S(2)}) copy-start(bf16[9,64,5]{1,2,0:T(8,128)(2,1)} %param.14) | copy-start | bytes 17284
  22.3 0.7 %copy-start.3 = (bf16[9,5,64]{2,1,0:T(8,128)(2,1)S(1)}, bf16[9,5,64]{2,1,0:T(8,128)(2,1)}, u32[]{:S(2)}) copy-start(bf16[9,5,64]{2,1,0:T(8,128)(2,1)} %out_ref.1) | copy-start | bytes 17284
  23.3 4.6 %copy-start = (f32[5,16,128]{2,1,0:T(8,128)S(1)}, f32[5,16,128]{2,1,0:T(8,128)}, u32[]{:S(2)}) copy-start(f32[5,16,128]{2,1,0:T(8,128)} %param.13) | copy-start | bytes 122884
  30.4 10.3 %collective-permute-start.2 = (f32[56,128]{1,0:T(8,128)S(1)}, f32[56,128]{1,0:T(8,128)S(1)}, u32[]{:S(2)}, u32[]{:S(2)}) collective-permute-start(f32[56,128]{1,0:T(8,128)S(1)} %get-tuple-element.20.refs_6_), channel_id=1, source_target_pairs={{16,32},{48,64},{80,96},{112,128},{144,160},{176,192},{208,224},{2... | collective-permute-start | bytes 86024 | tf_op jit(solution)/shard_map/ppermute | solution.py:471
  35.8 4.8 %collective-permute-start.3 = (f32[56,128]{1,0:T(8,128)S(1)}, f32[56,128]{1,0:T(8,128)S(1)}, u32[]{:S(2)}, u32[]{:S(2)}) collective-permute-start(f32[56,128]{1,0:T(8,128)S(1)} %get-tuple-element.21.refs_7_), channel_id=1, source_target_pairs={{0,16},{32,48},{64,80},{96,112},{128,144},{160,176},{192,208},{224... | collective-permute-start | bytes 86024 | tf_op jit(solution)/shard_map/ppermute | solution.py:471

commit v5 on v4

--- a/solution.py
+++ b/solution.py
@@ -11,6 +11,8 @@
 LANES = 128
 HID = 64
 TRACK = 512
+SENT = 384
+ALWAYS = 256
 HALO = 8
 BASES = 25
 CHUNK = 2048
@@ -44,22 +46,31 @@
     return jnp.concatenate([picked, jnp.zeros((8 - DAYS, LANES), F32)], axis=0)
 
 
-def adjoint_terms(sums_ref, base, here, above):
-    low = pl.ds(5 * base, 8)
-    high = pl.ds(LANES + 5 * base, 8)
+PLACES = {
+    "00": (0, 0), "01": (1, 0), "02": (2, 0), "03": (3, 0), "d0": (4, 0), "11": (1, 1), "12": (2, 1), "13": (3, 1), "d1": (4, 1),
+    "22": (5, 0), "23": (6, 0), "d2": (7, 0), "33": (6, 1), "d3": (7, 1),
+}
+
+
+def base_sums(sums_ref, row):
+    first = 5 * (row + 5)
+    return {name: sums_ref[array, pl.ds(LANES * half + first, 8), :] for name, (array, half) in PLACES.items()}
+
+
+def adjoint_terms(s, here, above):
     here_right = lane_roll(here, -1)
     above_right = lane_roll(above, -1)
-    s01 = sums_ref[1, low, :]
-    s02 = sums_ref[2, low, :]
-    s03 = sums_ref[3, low, :]
-    s12 = sums_ref[2, high, :]
-    s13 = sums_ref[3, high, :]
-    s23 = sums_ref[6, low, :]
-    g0 = sums_ref[0, low, :] * here + s01 * here_right + s02 * above + s03 * above_right - sums_ref[4, low, :]
-    g1 = s01 * here + sums_ref[1, high, :] * here_right + s12 * above + s13 * above_right - sums_ref[4, high, :]
-    g2 = s02 * here + s12 * here_right + sums_ref[5, low, :] * above + s23 * above_right - sums_ref[7, low, :]
-    g3 = s03 * here + s13 * here_right + s23 * above + sums_ref[6, high, :] * above_right - sums_ref[7, high, :]
+    g0 = s["00"] * here + s["01"] * here_right + s["02"] * above + s["03"] * above_right - s["d0"]
+    g1 = s["01"] * here + s["11"] * here_right + s["12"] * above + s["13"] * above_right - s["d1"]
+    g2 = s["02"] * here + s["12"] * here_right + s["22"] * above + s["23"] * above_right - s["d2"]
+    g3 = s["03"] * here + s["13"] * here_right + s["23"] * above + s["33"] * above_right - s["d3"]
     return g0 + lane_roll(g1, 1), g2 + lane_roll(g3, 1)
+
+
+def edge_factors(now, before):
+    east = (now["d1"] + before["d3"], now["11"] + before["33"], now["01"] + before["23"], now["13"], now["12"], now["03"])
+    west = (now["d0"] + before["d2"], now["00"] + before["22"], now["01"] + before["23"], now["02"], now["03"], now["12"])
+    return east, west
 
 
 def track_kernel(
@@ -68,9 +79,20 @@
     latitude = tile_ref[...] * ROWS + row_ref[...]
     keys = [time_ref[...].astype(F32), latitude.astype(F32), col_ref[...].astype(F32)]
     block = jnp.concatenate([value_ref[...], weight_ref[...]] + keys, axis=0)
-    twice = jnp.concatenate([block, block], axis=0).astype(BF16)
-    for k in range(out_ref.shape[0] // 16):
-        out_ref[16 * k : 16 * k + 16, :] = twice
+    count = out_ref.shape[0] // 8
+    number = lax.broadcasted_iota(jnp.int32, (1, TRACK), 1).astype(F32)
+    key = block[6:7] * float(TRACK) + number
+    key_down = jnp.broadcast_to(key, (LANES, TRACK)).T[:, 0:1]
+    rank = jnp.sum(jnp.where(key_down < key, 1.0, 0.0), axis=0, keepdims=True)
+    target = lax.broadcasted_iota(jnp.int32, (TRACK, TRACK), 0).astype(F32)
+    chosen = jnp.where(target == rank, 1.0, 0.0).astype(BF16)
+    ordered = nt_dot(jnp.concatenate([block, block], axis=0).astype(BF16), chosen)[0:8]
+    for pair in range(count // 2):
+        turned = []
+        for k in (2 * pair, 2 * pair + 1):
+            skipped = jnp.sum(jnp.where(block[6:7] < float(ROWS * k - 5), 1, 0))
+            turned.append(pltpu.roll(ordered, jnp.where(skipped == 0, 0, TRACK - skipped), 1)[:, 0:SENT])
+        out_ref[16 * pair : 16 * pair + 16, :] = jnp.concatenate(turned, axis=0).astype(BF16)
     even = lax.axis_index("lat") % 2 == 0
     for day in range(DAYS):
         lower = state_ref[ROWS * day : ROWS * day + HALO, :]
@@ -111,12 +133,6 @@
     ).astype(BF16)
 
 
-EAST_FIELDS = ((4, 1), (1, 0), (1, 1), (2, 1), (3, 1), (7, 1), (3, 0), (6, 0), (6, 1))
-WEST_FIELDS = ((4, 0), (0, 0), (1, 0), (2, 0), (3, 0), (7, 0), (2, 1), (5, 0), (6, 0))
-EAST_LANES = ((0, 1, 2, 3, 4), (5, 6, 4, 7, 8))
-WEST_LANES = ((0, 1, 2, 3, 4), (5, 3, 6, 7, 8))
-
-
 PRODUCTS = (
     ((0, 512), (384, 640), {(0, 0): (3, 1), (1, 0): (3, 0), (2, 0): (6, 0), (3, 0): (6, 1), (0, 1): (4, 1), (1, 1): (4, 0), (2, 1): (7, 0), (3, 1): (7, 1)}),
     ((0, 256), (128, 384), {(0, 0): (2, 1), (1, 0): (2, 0), (0, 1): (1, 1), (1, 1): (1, 0)}),
@@ -128,23 +144,23 @@
 
 def sums_kernel(track_ref, sums_ref, rw_ref, cw_ref):
     base_row = (lax.axis_index("lat") * ROWS - 5).astype(F32)
-    entry = lax.broadcasted_iota(jnp.int32, (LANES, TRACK), 0).astype(F32).astype(BF16)
-    nothing = jnp.zeros((LANES, TRACK), BF16)
-
-    def spread(row):
-        part = jnp.broadcast_to(row, (16, TRACK)).astype(BF16)
-        return jnp.concatenate([part] * 8, axis=0)
-
-    per_chunk = CHUNK // TRACK
-    chunks = track_ref.shape[0] * TRACK // (8 * CHUNK)
-    for chunk in range(chunks):
+
+    def accumulate(chunk, lanes, sources, fresh):
         slot = chunk % 2
-        for pair in range(per_chunk // 2):
-            first_row = chunk * per_chunk * 8 + pair * 16
-            both = track_ref[first_row : first_row + 16, :].astype(F32)
+        width = lanes.stop - lanes.start
+        filled = 2 * len(sources) * width
+        entry = lax.broadcasted_iota(jnp.int32, (LANES, width), 0).astype(F32).astype(BF16)
+        nothing = jnp.zeros((LANES, width), BF16)
+
+        def spread(row):
+            part = jnp.broadcast_to(row, (16, width)).astype(BF16)
+            return jnp.concatenate([part] * 8, axis=0)
+
+        for index, pair in enumerate(sources):
+            both = track_ref[16 * pair : 16 * pair + 16, lanes].astype(F32)
             for part in range(2):
                 block = both[8 * part : 8 * part + 8]
-                start = (2 * pair + part) * TRACK
+                start = (2 * index + part) * width
                 offset = block[6:7] - base_row
                 within = (offset >= 0.0) & (offset < float(BASES))
                 row_hit = entry == spread(jnp.where(within, offset * 5.0 + block[5:6], -1.0))
@@ -153,15 +169,28 @@
                     value = spread(block[source : source + 1])
                     if source > 0:
                         k = ROW_WEIGHTS.index(source - 1)
-                        rw_ref[slot, 128 * k : 128 * k + 128, start : start + TRACK] = jnp.where(row_hit, value, nothing)
+                        rw_ref[slot, 128 * k : 128 * k + 128, start : start + width] = jnp.where(row_hit, value, nothing)
                     k = COL_WEIGHTS.index(source - 1)
-                    cw_ref[slot, 128 * k : 128 * k + 128, start : start + TRACK] = jnp.where(col_hit, value, nothing)
+                    cw_ref[slot, 128 * k : 128 * k + 128, start : start + width] = jnp.where(col_hit, value, nothing)
         for (row0, row1), (col0, col1), blocks in PRODUCTS:
-            product = nt_dot(rw_ref[slot, row0:row1, :], cw_ref[slot, col0:col1, :])
+            product = nt_dot(rw_ref[slot, row0:row1, 0:filled], cw_ref[slot, col0:col1, 0:filled])
             for (i, j), (array, half) in blocks.items():
                 total = product[128 * i : 128 * i + 128, 128 * j : 128 * j + 128]
                 rows = slice(LANES * half, LANES * half + LANES)
-                sums_ref[array, rows, :] = total if chunk == 0 else sums_ref[array, rows, :] + total
+                sums_ref[array, rows, :] = total if fresh else sums_ref[array, rows, :] + total
+
+    pairs = track_ref.shape[0] // 16
+    size = CHUNK // (2 * ALWAYS)
+    for chunk, first in enumerate(range(0, pairs, size)):
+        accumulate(chunk, slice(0, ALWAYS), range(first, min(first + size, pairs)), chunk == 0)
+    rest = track_ref[:, ALWAYS:SENT].astype(F32) - base_row
+    row_kind = lax.broadcasted_iota(jnp.int32, rest.shape, 0) % 8
+    needed = jnp.max(jnp.where((row_kind == 6) & (rest >= 0.0) & (rest < float(BASES)), 1.0, 0.0))
+
+    @pl.when(needed > 0.0)
+    def _():
+        for first in range(0, pairs, 2 * size):
+            accumulate(0, slice(ALWAYS, SENT), range(first, min(first + 2 * size, pairs)), False)
 
 
 def edges_kernel(mid_ref, near_ref, far_ref, sums_ref, adjoint_ref, to_far_ref, to_near_ref):
@@ -179,23 +208,21 @@
         west = jnp.where(picked, lane_roll(here, place), west)
         if -5 <= row <= 19:
             above = day_rows(near_ref, mid_ref, far_ref, even_lat, row + 1)
-            now, later = adjoint_terms(sums_ref, row + 5, here, above)
+            sums = base_sums(sums_ref, row)
+            now, later = adjoint_terms(sums, here, above)
             if row > -5:
                 total = carried + now
                 adjoint_ref[row + 4] = total
                 picked = lane // 8 == place // 8 + 1
                 east = jnp.where(picked, lane_roll(total, place + 8 - 120), east)
                 west = jnp.where(picked, lane_roll(total, place + 8), west)
+            if -2 <= row <= ROWS:
+                for k, (last, first) in enumerate(zip(*edge_factors(sums, before))):
+                    target = place + 16 + k
+                    east = jnp.where(lane == target, lane_roll(last, target - (COLS - 2)), east)
+                    west = jnp.where(lane == target, lane_roll(first, target), west)
             carried = later
-        if -2 <= row <= ROWS:
-            for k in range(9):
-                target = place + 16 + k
-                array, half = EAST_FIELDS[k]
-                piece = sums_ref[array, pl.ds(LANES * half + 5 * (row + 5), 8), :]
-                east = jnp.where(lane == target, lane_roll(piece, target - (COLS - 2)), east)
-                array, half = WEST_FIELDS[k]
-                piece = sums_ref[array, pl.ds(LANES * half + 5 * (row + 5), 8), :]
-                west = jnp.where(lane == target, lane_roll(piece, target), west)
+            before = sums
         if place == 96:
             to_near_ref[8 * part : 8 * part + 8, :] = jnp.where(even_lon, east, west)
             to_far_ref[8 * part : 8 * part + 8, :] = jnp.where(even_lon, west, east)
@@ -411,18 +438,14 @@
     lane64 = lax.broadcasted_iota(jnp.int32, (HID, LANES), 1)
     for row in range(-1, ROWS + 1):
         part, place = strip_place(row)
-        main = hidden_ref[:, at(row)].astype(F32)
-        strip = hidden_ref[:, tile(STRIP + part)].astype(F32)
-        hid_minus_ref[:, at(row)] = jnp.where(
-            lane64 == 0, lane_roll(strip, -(place + 7)), lane_roll(main, 1)
-        ).astype(BF16)
-        hid_plus_ref[:, at(row)] = jnp.where(
-            lane64 == 127, lane_roll(strip, 127 - (place + 24)), lane_roll(main, -1)
-        ).astype(BF16)
+        main = hidden_ref[:, at(row)]
+        strip = hidden_ref[:, tile(STRIP + part)]
+        hid_minus_ref[:, at(row)] = jnp.where(lane64 == 0, lane_roll(strip, -(place + 7)), lane_roll(main, 1))
+        hid_plus_ref[:, at(row)] = jnp.where(lane64 == 127, lane_roll(strip, 127 - (place + 24)), lane_roll(main, -1))
     gradient(-1, 16, -2, 17)
     carried = zero
     for row in range(-2, ROWS + 1):
-        now, later = adjoint_terms(sums_ref, row + 5, est_ref[:, at(row)], est_ref[:, at(row + 1)])
+        now, later = adjoint_terms(base_sums(sums_ref, row), est_ref[:, at(row)], est_ref[:, at(row + 1)])
         if row > -2:
             total = grad_ref[:, at(row)] + carried + now
             grad_ref[:, at(row)] = total if 0 <= row < ROWS else total * mask_ref[:, at(row)]
@@ -430,18 +453,14 @@
     here = est_ref[:, strips]
     above = lane_roll(here, -32)
 
-    def edge_term(source, lane_at, lanes, e0, e1, e2, e3):
-        d, f0, f1, f2, f3 = [lane_roll(source, lane_at - (16 + k)) for k in lanes]
-        return f0 * e0 + f1 * e1 + f2 * e2 + f3 * e3 - d
-
-    west = (lane_roll(here, 1), here, lane_roll(above, 1), above)
-    east = (here, lane_roll(here, -1), above, lane_roll(above, -1))
-    extra_w = edge_term(from_west, 7, EAST_LANES[0], *west) + lane_roll(
-        edge_term(from_west, 7, EAST_LANES[1], *west), 32
-    )
-    extra_e = edge_term(from_east, 24, WEST_LANES[0], *east) + lane_roll(
-        edge_term(from_east, 24, WEST_LANES[1], *east), 32
-    )
+    def edge_term(source, lane_at, inner):
+        constant, own, beside, up, up_beside, down_beside = [lane_roll(source, lane_at - (16 + k)) for k in range(6)]
+        here_beside = lane_roll(here, inner)
+        total = own * here + beside * here_beside + up * above + up_beside * lane_roll(above, inner) - constant
+        return total + lane_roll(up * here + down_beside * here_beside, 32)
+
+    extra_w = edge_term(from_west, 7, 1)
+    extra_e = edge_term(from_east, 24, -1)
     grad_ref[:, strips] = (
         grad_ref[:, strips] + jnp.where(strip_lane % 32 < 16, extra_w, extra_e)
     ) * mask_ref[:, strips]
@@ -494,12 +513,13 @@
     track, lat_near, lat_far = pl.pallas_call(
         track_kernel,
         out_shape=(
-            jax.ShapeDtypeStruct((lat_count * 8, TRACK), BF16),
+            jax.ShapeDtypeStruct((lat_count * 8, SENT), BF16),
             jax.ShapeDtypeStruct((DAYS * HALO, LANES), F32),
             jax.ShapeDtypeStruct((DAYS * HALO, LANES), F32),
         ),
         in_specs=[vmem] * 7,
         out_specs=(vmem, vmem, vmem),
+        compiler_params=pltpu.CompilerParams(vmem_limit_bytes=16 * 1024 * 1024),
         cost_estimate=pl.CostEstimate(flops=100_000, bytes_accessed=150_000, transcendentals=0),
         name="track",
     )(
@@ -512,8 +532,8 @@
         mid,
     )
     gathered = lax.all_to_all(
-        track.reshape(lat_count, 8, TRACK), "lat", split_axis=0, concat_axis=0, tiled=True
-    ).reshape(lat_count * 8, TRACK)
+        track.reshape(lat_count, 8, SENT), "lat", split_axis=0, concat_axis=0, tiled=True
+    ).reshape(lat_count * 8, SENT)
     far = swap(lat_far, "lat", 1, lat_count, False)
     near = swap(lat_near, "lat", 0, lat_count, False)
     w_gate, w_in, w_out, w_inc = pl.pallas_call(

time: 48.6 us -> 49.8 us (1.025)
  local copies, waits for them, and re-layouts: 2.12 us -> 5.83 us
  Pallas kernels: 17.7 us -> 14.9 us
    unnamed x14 -> x28, local copies, waits for them, and re-layouts: 2.12 us -> 5.83 us
    pallas_call x1, Pallas kernels: 4.52 us -> 2.42 us  [on_device(): pl.pallas_call(sums_kernel, out_shape=jax.ShapeDtypeStruct((8, 256, LANES...]
  transfers between devices with their start and end apart: 5 -> 5, of which waited for: 0 -> 0; matrix products, arithmetic and copies ran while one was open for 0% -> 0% of each run, Pallas kernels for 13% -> 8%
where the time goes in v5:
time: 49.8 us; the launch traced here: 49.2 us
  starting transfers between devices  27.7 us (56%)
  Pallas kernels  14.9 us (30%)
  local copies, waits for them, and re-layouts  5.83 us (12%)
  between operations  0.78 us (2%)
    ppermute x4, starting transfers between devices, swap(): lax.ppermute(value, axis, pairs + [(target, source) for source, target in...  16.3 us
    all_to_all x1, starting transfers between devices, on_device(): lax.all_to_all(track.reshape(lat_count, 8, SENT), 'lat', split_axis=0, co...  11.4 us
    pallas_call x1, Pallas kernels, on_device(): pl.pallas_call(solve, out_shape=(jax.ShapeDtypeStruct((DAYS * ROWS, LANES...  7.49 us
    unnamed x28, local copies, waits for them, and re-layouts  5.83 us
    pallas_call x1, Pallas kernels, on_device(): pl.pallas_call(sums_kernel, out_shape=jax.ShapeDtypeStruct((8, 256, LANES...  2.42 us
    pallas_call x1, Pallas kernels, on_device(): pl.pallas_call(edges_kernel, out_shape=(jax.ShapeDtypeStruct((24, 8, LANE...  2.12 us
    pallas_call x1, Pallas kernels, on_device(): pl.pallas_call(track_kernel, out_shape=(jax.ShapeDtypeStruct((lat_count *...  1.29 us
    pallas_call x1, Pallas kernels, on_device(): pl.pallas_call(first, out_shape=jax.ShapeDtypeStruct((24, 8, LANES), F32)...  1.29 us
  transfers between devices with their start and end apart: 5, of which 0 were waited for; matrix products, arithmetic and copies ran while one was open for 0% of the time, Pallas kernels for 8%

profile of v5, /device:TPU:3, one launch (start us, length us, event | category | flops | bytes accessed | tf_op | source)
XLA Modules:
  0.0 49.2 jit_solution(10240970025779967327)
XLA Ops:
  0.7 0.7 %copy-done.5 = f32[4,512]{1,0:T(4,128)S(1)} copy-done((f32[4,512]{1,0:T(4,128)S(1)}, f32[4,512]{1,0:T(4,128)}, u32[]{:S(2)}) %copy-start.5) | copy-done | bytes 8216
  1.3 0.8 %copy-done = f32[5,16,128]{2,1,0:T(8,128)S(1)} copy-done((f32[5,16,128]{2,1,0:T(8,128)S(1)}, f32[5,16,128]{2,1,0:T(8,128)}, u32[]{:S(2)}) %copy-start) | copy-done | bytes 40984
  2.1 0.7 %copy-done.8 = s32[512,1]{0,1:T(1,128)S(1)} copy-done((s32[512,1]{0,1:T(1,128)S(1)}, s32[512,1]{0,1:T(1,128)}, u32[]{:S(2)}) %copy-start.8) | copy-done | bytes 2072
  2.8 0.7 %copy-done.9 = s32[512]{0:T(512)S(1)} copy-done((s32[512]{0:T(512)S(1)}, s32[512]{0:T(512)}, u32[]{:S(2)}) %copy-start.9) | copy-done | bytes 2072
  3.5 0.7 %copy-done.10 = s32[512]{0:T(512)S(1)} copy-done((s32[512]{0:T(512)S(1)}, s32[512]{0:T(512)}, u32[]{:S(2)}) %copy-start.10) | copy-done | bytes 2072
  4.2 0.7 %copy-done.11 = s32[512]{0:T(512)S(1)} copy-done((s32[512]{0:T(512)S(1)}, s32[512]{0:T(512)}, u32[]{:S(2)}) %copy-start.11) | copy-done | bytes 2072
  4.8 1.3 %track.1 = (bf16[128,384]{1,0:T(8,128)(2,1)}, f32[40,128]{1,0:T(8,128)S(1)}, f32[40,128]{1,0:T(8,128)S(1)}) custom-call(f32[1,512]{1,0:T(1,128)S(1)} %bitcast.21, f32[4,512]{1,0:T(4,128)S(1)} %copy-done.5, s32[1,512]{1,0:T(1,128)S(1)} %bitcast.22, s32[1,512]{1,0:T(1,128)S(1)} %bitcast.23, s32[1,512]{1,0:T(1,128)S(1)} %bitcast.24, s32[1,512]{1,0:T(1,128)S(1)} %bitcast.25, ...), custom_call_target="tpu_custom_call" | custom-call | flops 100000 | bytes 150000 | tf_op jit(solution)/shard_map/track/pallas_call | solution.py:513
  6.1 11.4 %all-to-all-start = ((bf16[16,8,384]{2,1,0:T(8,128)(2,1)}), bf16[16,8,384]{2,1,0:T(8,128)(2,1)S(1)}, u32[]{:S(2)}, u32[]{:S(2)}) async-start(bf16[16,8,384]{2,1,0:T(8,128)(2,1)} %bitcast.6), calls=%async_computation | async-start | bytes 196608 | tf_op jit(solution)/shard_map/all_to_all | solution.py:534
  17.5 3.1 %collective-permute-start = (f32[40,128]{1,0:T(8,128)S(1)}, f32[40,128]{1,0:T(8,128)S(1)}, u32[]{:S(2)}, u32[]{:S(2)}) collective-permute-start(f32[40,128]{1,0:T(8,128)S(1)} %get-tuple-element.14), channel_id=1, source_target_pairs={{0,1},{2,3},{4,5},{6,7},{8,9},{10,11},{12,13},{14,15},{1,0},{3,2},... | collective-permute-start | bytes 61448 | tf_op jit(solution)/shard_map/ppermute | solution.py:490
  20.6 4.3 %collective-permute-start.1 = (f32[40,128]{1,0:T(8,128)S(1)}, f32[40,128]{1,0:T(8,128)S(1)}, u32[]{:S(2)}, u32[]{:S(2)}) collective-permute-start(f32[40,128]{1,0:T(8,128)S(1)} %get-tuple-element.15), channel_id=1, source_target_pairs={{1,2},{3,4},{5,6},{7,8},{9,10},{11,12},{13,14},{2,1},{4,3},{6,5},{... | collective-permute-start | bytes 61448 | tf_op jit(solution)/shard_map/ppermute | solution.py:490
  24.9 0.0 copy-start.6
  24.9 0.0 copy-start.12
  24.9 0.0 copy-start.13
  24.9 0.0 copy-done.3
  24.9 0.0 copy-done.4
  25.0 0.6 %copy-done.6 = bf16[5,64]{1,0:T(8,128)(2,1)S(1)} copy-done((bf16[5,64]{1,0:T(8,128)(2,1)S(1)}, bf16[5,64]{1,0:T(8,128)(2,1)}, u32[]{:S(2)}) %copy-start.6) | copy-done | bytes 664
  25.6 0.0 copy-done.12
  25.6 1.0 %copy-done.2 = bf16[9,256,69]{1,2,0:T(8,128)(2,1)S(1)} copy-done((bf16[9,256,69]{1,2,0:T(8,128)(2,1)S(1)}, bf16[9,256,69]{1,2,0:T(8,128)(2,1)}, u32[]{:S(2)}) %copy-start.2) | copy-done | bytes 317976
  26.6 0.3 prepare.1
  26.9 0.0 all-to-all-done
  26.9 0.0 copy-start.1
  26.9 2.4 %sums.1.sums_ref.refs_3_ = f32[8,256,128]{2,1,0:T(8,128)S(1)} custom-call(bf16[128,384]{1,0:T(8,128)(2,1)S(1)} %bitcast.19), custom_call_target="tpu_custom_call" | custom-call | flops 4000000000 | bytes 1500000 | tf_op jit(solution)/shard_map/sums/pallas_call | solution.py:582
  29.3 0.0 collective-permute-done.near_ref.refs_1_
  29.3 0.0 collective-permute-done.1.far_ref.refs_2_
  29.3 0.0 copy-done.1
  29.3 2.1 %edges.1 = (f32[24,8,128]{2,1,0:T(8,128)S(1)}, f32[56,128]{1,0:T(8,128)S(1)}, f32[56,128]{1,0:T(8,128)S(1)}) custom-call(f32[80,128]{1,0:T(8,128)S(1)} %bitcast.15, f32[40,128]{1,0:T(8,128)S(1)} %collective-permute-done.near_ref.refs_1_, f32[40,128]{1,0:T(8,128)S(1)} %collective-permute-done.1.far_ref.refs_2_, f32[8,256,128]{2,1,0:T(8,128)S(1)} %sums.1.sums_ref.refs_3_), custom_call_target="tpu_custom_call" | custom-call | flops 1000000 | bytes 1500000 | tf_op jit(solution)/shard_map/edges/pallas_call | solution.py:595
  31.5 5.4 %collective-permute-start.2 = (f32[56,128]{1,0:T(8,128)S(1)}, f32[56,128]{1,0:T(8,128)S(1)}, u32[]{:S(2)}, u32[]{:S(2)}) collective-permute-start(f32[56,128]{1,0:T(8,128)S(1)} %get-tuple-element.20.refs_6_), channel_id=1, source_target_pairs={{16,32},{48,64},{80,96},{112,128},{144,160},{176,192},{208,224},{2... | collective-permute-start | bytes 86024 | tf_op jit(solution)/shard_map/ppermute | solution.py:490
  36.9 3.5 %collective-permute-start.3 = (f32[56,128]{1,0:T(8,128)S(1)}, f32[56,128]{1,0:T(8,128)S(1)}, u32[]{:S(2)}, u32[]{:S(2)}) collective-permute-start(f32[56,128]{1,0:T(8,128)S(1)} %get-tuple-element.21.refs_7_), channel_id=1, source_target_pairs={{0,16},{32,48},{64,80},{96,112},{128,144},{160,176},{192,208},{224... | collective-permute-start | bytes 86024 | tf_op jit(solution)/shard_map/ppermute | solution.py:490
  40.4 1.3 %first.1.refs_5_ = f32[24,8,128]{2,1,0:T(8,128)S(1)} custom-call(f32[80,128]{1,0:T(8,128)S(1)} %bitcast.16, f32[40,128]{1,0:T(8,128)S(1)} %collective-permute-done.near_ref.refs_1_, f32[40,128]{1,0:T(8,128)S(1)} %collective-permute-done.1.far_ref.refs_2_, bf16[64,128]{1,0:T(8,128)(2,1)S(1)} %get-tuple-element.18.refs_3_.refs_10_, ...), custom_call_target="tpu_custom_call" | custom-call | flops 2000000000 | bytes 500000 | tf_op jit(solution)/shard_map/first/pallas_call | solution.py:566
  41.7 0.0 collective-permute-done.2.refs_8_
  41.7 0.0 collective-permute-done.3.refs_9_
  41.7 7.5 %solve.1 = (f32[80,128]{1,0:T(8,128)}, f32[1024,128]{1,0:T(8,128)}) custom-call(f32[80,128]{1,0:T(8,128)S(1)} %bitcast.17, f32[40,128]{1,0:T(8,128)S(1)} %collective-permute-done.near_ref.refs_1_, f32[40,128]{1,0:T(8,128)S(1)} %collective-permute-done.1.far_ref.refs_2_, f32[8,256,128]{2,1,0:T(8,128)S(1)} %sums.1.sums_ref.refs_3_, ...), custom_call_target="tpu_custom_call" | custom-call | tf_op jit(solution)/shard_map/solve/pallas_call | solution.py:615
  (12 shorter events, 0.0 us)
Async XLA Ops:
  0.6 0.7 %copy-start.5 = (f32[4,512]{1,0:T(4,128)S(1)}, f32[4,512]{1,0:T(4,128)}, u32[]{:S(2)}) copy-start(f32[4,512]{1,0:T(4,128)} %weight_ref.1) | copy-start | bytes 24580
  0.6 0.7 %copy-start.7 = (f32[512]{0:T(512)S(1)}, f32[512]{0:T(512)}, u32[]{:S(2)}) copy-start(f32[512]{0:T(512)} %param.20) | copy-start | bytes 6148
  1.3 0.8 %copy-start = (f32[5,16,128]{2,1,0:T(8,128)S(1)}, f32[5,16,128]{2,1,0:T(8,128)}, u32[]{:S(2)}) copy-start(f32[5,16,128]{2,1,0:T(8,128)} %param.13) | copy-start | bytes 122884
  2.1 0.7 %copy-start.8 = (s32[512,1]{0,1:T(1,128)S(1)}, s32[512,1]{0,1:T(1,128)}, u32[]{:S(2)}) copy-start(s32[512,1]{0,1:T(1,128)} %param.22) | copy-start | bytes 6148
  2.8 0.7 %copy-start.9 = (s32[512]{0:T(512)S(1)}, s32[512]{0:T(512)}, u32[]{:S(2)}) copy-start(s32[512]{0:T(512)} %param.23) | copy-start | bytes 6148
  3.5 0.7 %copy-start.10 = (s32[512]{0:T(512)S(1)}, s32[512]{0:T(512)}, u32[]{:S(2)}) copy-start(s32[512]{0:T(512)} %param.24) | copy-start | bytes 6148
  4.2 0.7 %copy-start.11 = (s32[512]{0:T(512)S(1)}, s32[512]{0:T(512)}, u32[]{:S(2)}) copy-start(s32[512]{0:T(512)} %param.25) | copy-start | bytes 6148
  6.1 18.8 %copy-start.3 = (bf16[9,64,5]{1,2,0:T(8,128)(2,1)S(1)}, bf16[9,64,5]{1,2,0:T(8,128)(2,1)}, u32[]{:S(2)}) copy-start(bf16[9,64,5]{1,2,0:T(8,128)(2,1)} %param.14) | copy-start | bytes 17284
  6.1 18.8 %copy-start.4 = (bf16[9,5,64]{2,1,0:T(8,128)(2,1)S(1)}, bf16[9,5,64]{2,1,0:T(8,128)(2,1)}, u32[]{:S(2)}) copy-start(bf16[9,5,64]{2,1,0:T(8,128)(2,1)} %out_ref.1) | copy-start | bytes 17284
  6.1 20.7 %all-to-all-start = ((bf16[16,8,384]{2,1,0:T(8,128)(2,1)}), bf16[16,8,384]{2,1,0:T(8,128)(2,1)S(1)}, u32[]{:S(2)}, u32[]{:S(2)}) async-start(bf16[16,8,384]{2,1,0:T(8,128)(2,1)} %bitcast.6), calls=%async_computation | async-start | bytes 196608 | tf_op jit(solution)/shard_map/all_to_all | solution.py:534
  17.5 11.8 %collective-permute-start = (f32[40,128]{1,0:T(8,128)S(1)}, f32[40,128]{1,0:T(8,128)S(1)}, u32[]{:S(2)}, u32[]{:S(2)}) collective-permute-start(f32[40,128]{1,0:T(8,128)S(1)} %get-tuple-element.14), channel_id=1, source_target_pairs={{0,1},{2,3},{4,5},{6,7},{8,9},{10,11},{12,13},{14,15},{1,0},{3,2},... | collective-permute-start | bytes 61448 | tf_op jit(solution)/shard_map/ppermute | solution.py:490
  20.6 8.7 %collective-permute-start.1 = (f32[40,128]{1,0:T(8,128)S(1)}, f32[40,128]{1,0:T(8,128)S(1)}, u32[]{:S(2)}, u32[]{:S(2)}) collective-permute-start(f32[40,128]{1,0:T(8,128)S(1)} %get-tuple-element.15), channel_id=1, source_target_pairs={{1,2},{3,4},{5,6},{7,8},{9,10},{11,12},{13,14},{2,1},{4,3},{6,5},{... | collective-permute-start | bytes 61448 | tf_op jit(solution)/shard_map/ppermute | solution.py:490
  24.9 0.7 %copy-start.6 = (bf16[5,64]{1,0:T(8,128)(2,1)S(1)}, bf16[5,64]{1,0:T(8,128)(2,1)}, u32[]{:S(2)}) copy-start(bf16[5,64]{1,0:T(8,128)(2,1)} %inc_ref.1) | copy-start | bytes 1924
  24.9 0.7 %copy-start.12 = (f32[256]{0:T(256)S(1)}, f32[256]{0:T(256)}, u32[]{:S(2)}) copy-start(f32[256]{0:T(256)} %param.18) | copy-start | bytes 3076
  24.9 0.7 %copy-start.13 = (f32[64]{0:T(128)S(1)}, f32[64]{0:T(128)}, u32[]{:S(2)}) copy-start(f32[64]{0:T(128)} %param.15) | copy-start | bytes 772
  25.6 1.0 %copy-start.2 = (bf16[9,256,69]{1,2,0:T(8,128)(2,1)S(1)}, bf16[9,256,69]{1,2,0:T(8,128)(2,1)}, u32[]{:S(2)}) copy-start(bf16[9,256,69]{1,2,0:T(8,128)(2,1)} %param.17) | copy-start | bytes 953860
  26.9 2.5 %copy-start.1 = (f32[5,16,128]{2,1,0:T(8,128)S(1)}, f32[5,16,128]{2,1,0:T(8,128)}, u32[]{:S(2)}) copy-start(f32[5,16,128]{2,1,0:T(8,128)} %param.13) | copy-start | bytes 122884
  31.5 10.3 %collective-permute-start.2 = (f32[56,128]{1,0:T(8,128)S(1)}, f32[56,128]{1,0:T(8,128)S(1)}, u32[]{:S(2)}, u32[]{:S(2)}) collective-permute-start(f32[56,128]{1,0:T(8,128)S(1)} %get-tuple-element.20.refs_6_), channel_id=1, source_target_pairs={{16,32},{48,64},{80,96},{112,128},{144,160},{176,192},{208,224},{2... | collective-permute-start | bytes 86024 | tf_op jit(solution)/shard_map/ppermute | solution.py:490
  36.9 4.8 %collective-permute-start.3 = (f32[56,128]{1,0:T(8,128)S(1)}, f32[56,128]{1,0:T(8,128)S(1)}, u32[]{:S(2)}, u32[]{:S(2)}) collective-permute-start(f32[56,128]{1,0:T(8,128)S(1)} %get-tuple-element.21.refs_7_), channel_id=1, source_target_pairs={{0,16},{32,48},{64,80},{96,112},{128,144},{160,176},{192,208},{224... | collective-permute-start | bytes 86024 | tf_op jit(solution)/shard_map/ppermute | solution.py:490

commit v6 on v5

--- a/solution.py
+++ b/solution.py
@@ -53,7 +53,7 @@
 
 
 def base_sums(sums_ref, row):
-    first = 5 * (row + 5)
+    first = 5 * (row + 5) + jnp.minimum(lax.axis_index("lat"), 0)
     return {name: sums_ref[array, pl.ds(LANES * half + first, 8), :] for name, (array, half) in PLACES.items()}
 
 
@@ -193,7 +193,7 @@
             accumulate(0, slice(ALWAYS, SENT), range(first, min(first + 2 * size, pairs)), False)
 
 
-def edges_kernel(mid_ref, near_ref, far_ref, sums_ref, adjoint_ref, to_far_ref, to_near_ref):
+def edges_kernel(mid_ref, near_ref, far_ref, sums_ref, adjoint_ref, to_far_ref, to_near_ref, field_ref):
     even_lat = lax.axis_index("lat") % 2 == 0
     even_lon = lax.axis_index("lon") % 2 == 0
     lane = lax.broadcasted_iota(jnp.int32, (8, LANES), 1)
@@ -201,13 +201,15 @@
     east, west = zero, zero
     carried = zero
     for row in range(-6, ROWS + 6):
+        field_ref[row + 6] = day_rows(near_ref, mid_ref, far_ref, even_lat, row)
+    for row in range(-6, ROWS + 6):
         part, place = strip_place(row)
-        here = day_rows(near_ref, mid_ref, far_ref, even_lat, row)
+        here = field_ref[row + 6]
         picked = lane // 8 == place // 8
         east = jnp.where(picked, lane_roll(here, place - 120), east)
         west = jnp.where(picked, lane_roll(here, place), west)
         if -5 <= row <= 19:
-            above = day_rows(near_ref, mid_ref, far_ref, even_lat, row + 1)
+            above = field_ref[row + 7]
             sums = base_sums(sums_ref, row)
             now, later = adjoint_terms(sums, here, above)
             if row > -5:
@@ -255,11 +257,10 @@
 
 
 def first_kernel(
-    mid_ref, near_ref, far_ref, w_in_ref, w_out_ref, out_ref, est_ref, minus_ref, plus_ref, window_ref, spread_ref, *, lat_count
+    field_ref, w_in_ref, w_out_ref, out_ref, est_ref, minus_ref, plus_ref, window_ref, spread_ref, *, lat_count
 ):
-    even_lat = lax.axis_index("lat") % 2 == 0
     for row in range(-6, 22):
-        value = day_rows(near_ref, mid_ref, far_ref, even_lat, row)
+        value = field_ref[row + 6]
         est_ref[:, at(row)] = value
         minus_ref[:, at(row)] = lane_roll(value, 1)
         plus_ref[:, at(row)] = lane_roll(value, -1)
@@ -285,9 +286,7 @@
 
 
 def solve_kernel(
-    mid_ref,
-    near_ref,
-    far_ref,
+    field_ref,
     sums_ref,
     adjoint_ref,
     first_ref,
@@ -315,7 +314,6 @@
     *,
     lat_count,
 ):
-    even_lat = lax.axis_index("lat") % 2 == 0
     even_lon = lax.axis_index("lon") % 2 == 0
     lane = lax.broadcasted_iota(jnp.int32, (8, LANES), 1)
     zero = jnp.zeros((8, LANES), F32)
@@ -339,7 +337,7 @@
     est_ref[:, at(-7)] = zero
     est_ref[:, at(22)] = zero
     for row in range(-6, 22):
-        est_ref[:, at(row)] = day_rows(near_ref, mid_ref, far_ref, even_lat, row)
+        est_ref[:, at(row)] = field_ref[row + 6]
     quarter = (lane % 32) // 8
     from_west, from_east, adjoint_strip = [], [], []
     for part in range(TILES - STRIP):
@@ -519,7 +517,6 @@
         ),
         in_specs=[vmem] * 7,
         out_specs=(vmem, vmem, vmem),
-        compiler_params=pltpu.CompilerParams(vmem_limit_bytes=16 * 1024 * 1024),
         cost_estimate=pl.CostEstimate(flops=100_000, bytes_accessed=150_000, transcendentals=0),
         name="track",
     )(
@@ -546,7 +543,6 @@
         ),
         in_specs=[vmem] * 6,
         out_specs=(vmem,) * 4,
-        compiler_params=pltpu.CompilerParams(vmem_limit_bytes=16 * 1024 * 1024),
         cost_estimate=pl.CostEstimate(flops=2_000_000, bytes_accessed=1_500_000, transcendentals=0),
         name="prepare",
     )(
@@ -557,28 +553,6 @@
         prior_out,
         lstm_out,
     )
-    width = TILES * LANES
-    main_width = STRIP * LANES
-
-    def first(*refs):
-        first_kernel(*refs, lat_count=lat_count)
-
-    started = pl.pallas_call(
-        first,
-        out_shape=jax.ShapeDtypeStruct((24, 8, LANES), F32),
-        in_specs=[vmem] * 5,
-        out_specs=vmem,
-        scratch_shapes=[
-            pltpu.VMEM((8, main_width), F32),
-            pltpu.VMEM((8, main_width), F32),
-            pltpu.VMEM((8, main_width), F32),
-            pltpu.VMEM((80, main_width), BF16),
-            pltpu.VMEM((80, main_width), F32),
-        ],
-        compiler_params=pltpu.CompilerParams(vmem_limit_bytes=16 * 1024 * 1024),
-        cost_estimate=pl.CostEstimate(flops=2_000_000_000, bytes_accessed=500_000, transcendentals=0),
-        name="first",
-    )(mid, near, far, w_in, w_out)
     sums = pl.pallas_call(
         sums_kernel,
         out_shape=jax.ShapeDtypeStruct((8, 256, LANES), F32),
@@ -592,20 +566,43 @@
         cost_estimate=pl.CostEstimate(flops=4_000_000_000, bytes_accessed=1_500_000, transcendentals=0),
         name="sums",
     )(gathered)
-    adjoint, to_far, to_near = pl.pallas_call(
+    adjoint, to_far, to_near, field = pl.pallas_call(
         edges_kernel,
         out_shape=(
             jax.ShapeDtypeStruct((24, 8, LANES), F32),
             jax.ShapeDtypeStruct((56, LANES), F32),
             jax.ShapeDtypeStruct((56, LANES), F32),
+            jax.ShapeDtypeStruct((28, 8, LANES), F32),
         ),
         in_specs=[vmem] * 4,
-        out_specs=(vmem, vmem, vmem),
+        out_specs=(vmem, vmem, vmem, vmem),
         compiler_params=pltpu.CompilerParams(vmem_limit_bytes=16 * 1024 * 1024),
         cost_estimate=pl.CostEstimate(flops=1_000_000, bytes_accessed=1_500_000, transcendentals=0),
         name="edges",
     )(mid, near, far, sums)
 
+    width = TILES * LANES
+    main_width = STRIP * LANES
+
+    def first(*refs):
+        first_kernel(*refs, lat_count=lat_count)
+
+    started = pl.pallas_call(
+        first,
+        out_shape=jax.ShapeDtypeStruct((24, 8, LANES), F32),
+        in_specs=[vmem] * 3,
+        out_specs=vmem,
+        scratch_shapes=[
+            pltpu.VMEM((8, main_width), F32),
+            pltpu.VMEM((8, main_width), F32),
+            pltpu.VMEM((8, main_width), F32),
+            pltpu.VMEM((80, main_width), BF16),
+            pltpu.VMEM((80, main_width), F32),
+        ],
+        compiler_params=pltpu.CompilerParams(vmem_limit_bytes=16 * 1024 * 1024),
+        cost_estimate=pl.CostEstimate(flops=2_000_000_000, bytes_accessed=500_000, transcendentals=0),
+        name="first",
+    )(field, w_in, w_out)
     from_far = swap(to_far, "lon", 1, lon_count, True)
     from_near = swap(to_near, "lon", 0, lon_count, True)
 
@@ -618,7 +615,7 @@
             jax.ShapeDtypeStruct((DAYS * ROWS, LANES), F32),
             jax.ShapeDtypeStruct((HID * ROWS, LANES), F32),
         ),
-        in_specs=[vmem] * 14,
+        in_specs=[vmem] * 12,
         out_specs=(vmem, vmem),
         scratch_shapes=[
             pltpu.VMEM((8, width), F32),
@@ -635,7 +632,7 @@
         ],
         compiler_params=pltpu.CompilerParams(vmem_limit_bytes=32 * 1024 * 1024),
         name="solve",
-    )(mid, near, far, sums, adjoint, started, to_far, to_near, from_far, from_near, w_in, w_out, w_gate, w_inc)
+    )(field, sums, adjoint, started, to_far, to_near, from_far, from_near, w_in, w_out, w_gate, w_inc)
     return (
         estimate.reshape(DAYS, ROWS, LANES),
         cell_state.reshape(HID, ROWS, LANES),

time: 49.8 us -> 47.1 us (0.946)
  local copies, waits for them, and re-layouts: 5.83 us -> 0.68 us
  Pallas kernels: 14.9 us -> 17.5 us
    unnamed x28 -> x14, local copies, waits for them, and re-layouts: 5.83 us -> 0.68 us
    pallas_call x1, Pallas kernels: 0.3 us -> 2.05 us  [on_device(): pl.pallas_call(prepare_kernel, out_shape=(jax.ShapeDtypeStruct((4 * HID,...]
    pallas_call x1, Pallas kernels: 1.29 us -> 2.17 us  [on_device(): pl.pallas_call(track_kernel, out_shape=(jax.ShapeDtypeStruct((lat_count *...]
  transfers between devices with their start and end apart: 5 -> 5, of which waited for: 0 -> 0; matrix products, arithmetic and copies ran while one was open for 0% -> 0% of each run, Pallas kernels for 8% -> 12%
where the time goes in v6:
time: 47.1 us; the launch traced here: 46.7 us
  starting transfers between devices  27.7 us (59%)
  Pallas kernels  17.5 us (37%)
  between operations  0.78 us (2%)
  local copies, waits for them, and re-layouts  0.68 us (1%)
    ppermute x4, starting transfers between devices, swap(): lax.ppermute(value, axis, pairs + [(target, source) for source, target in...  16.4 us
    all_to_all x1, starting transfers between devices, on_device(): lax.all_to_all(track.reshape(lat_count, 8, SENT), 'lat', split_axis=0, co...  11.4 us
    pallas_call x1, Pallas kernels, on_device(): pl.pallas_call(solve, out_shape=(jax.ShapeDtypeStruct((DAYS * ROWS, LANES...  7.48 us
    pallas_call x1, Pallas kernels, on_device(): pl.pallas_call(sums_kernel, out_shape=jax.ShapeDtypeStruct((8, 256, LANES...  2.42 us
    pallas_call x1, Pallas kernels, on_device(): pl.pallas_call(track_kernel, out_shape=(jax.ShapeDtypeStruct((lat_count *...  2.17 us
    pallas_call x1, Pallas kernels, on_device(): pl.pallas_call(edges_kernel, out_shape=(jax.ShapeDtypeStruct((24, 8, LANE...  2.1 us
    pallas_call x1, Pallas kernels, on_device(): pl.pallas_call(prepare_kernel, out_shape=(jax.ShapeDtypeStruct((4 * HID,...  2.05 us
    pallas_call x1, Pallas kernels, on_device(): pl.pallas_call(first, out_shape=jax.ShapeDtypeStruct((24, 8, LANES), F32)...  1.27 us
  transfers between devices with their start and end apart: 5, of which 0 were waited for; matrix products, arithmetic and copies ran while one was open for 0% of the time, Pallas kernels for 12%

profile of v6, /device:TPU:3, one launch (start us, length us, event | category | flops | bytes accessed | tf_op | source)
XLA Modules:
  0.0 46.7 jit_solution(17459733118113259064)
XLA Ops:
  0.6 2.2 %track.1 = (bf16[128,384]{1,0:T(8,128)(2,1)}, f32[40,128]{1,0:T(8,128)}, f32[40,128]{1,0:T(8,128)}) custom-call(f32[1,512]{1,0:T(1,128)} %bitcast.20, f32[4,512]{1,0:T(4,128)} %weight_ref.1, s32[1,512]{1,0:T(1,128)} %bitcast.21, s32[1,512]{1,0:T(1,128)} %bitcast.22, s32[1,512]{1,0:T(1,128)} %bitcast.23, s32[1,512]{1,0:T(1,128)} %bitcast.24, f32[80,128]{1,0:T(8,128)} %bitcast.14), custom_call_target="tpu_custom_call" | custom-call | flops 100000 | bytes 150000 | tf_op jit(solution)/shard_map/track/pallas_call | solution.py:511
  2.8 0.0 copy-start.6
  2.8 0.0 copy-start.5
  2.8 11.4 %all-to-all-start = ((bf16[16,8,384]{2,1,0:T(8,128)(2,1)}), bf16[16,8,384]{2,1,0:T(8,128)(2,1)S(1)}, u32[]{:S(2)}, u32[]{:S(2)}) async-start(bf16[16,8,384]{2,1,0:T(8,128)(2,1)} %bitcast.18), calls=%async_computation | async-start | bytes 196608 | tf_op jit(solution)/shard_map/all_to_all | solution.py:531
  14.2 0.0 copy-done.6
  14.2 3.1 %collective-permute-start = (f32[40,128]{1,0:T(8,128)S(1)}, f32[40,128]{1,0:T(8,128)S(1)}, u32[]{:S(2)}, u32[]{:S(2)}) collective-permute-start(f32[40,128]{1,0:T(8,128)S(1)} %copy-done.6), channel_id=1, source_target_pairs={{0,1},{2,3},{4,5},{6,7},{8,9},{10,11},{12,13},{14,15},{1,0},{3,2},... | collective-permute-start | bytes 61448 | tf_op jit(solution)/shard_map/ppermute | solution.py:488
  17.3 0.0 copy-done.5
  17.3 4.3 %collective-permute-start.1 = (f32[40,128]{1,0:T(8,128)S(1)}, f32[40,128]{1,0:T(8,128)S(1)}, u32[]{:S(2)}, u32[]{:S(2)}) collective-permute-start(f32[40,128]{1,0:T(8,128)S(1)} %copy-done.5), channel_id=1, source_target_pairs={{1,2},{3,4},{5,6},{7,8},{9,10},{11,12},{13,14},{2,1},{4,3},{6,5},{... | collective-permute-start | bytes 61448 | tf_op jit(solution)/shard_map/ppermute | solution.py:488
  21.6 2.1 %prepare.1 = (bf16[256,768]{1,0:T(8,128)(2,1)}, bf16[64,128]{1,0:T(8,128)(2,1)}, bf16[80,64]{1,0:T(8,128)(2,1)}, bf16[16,64]{1,0:T(8,128)(2,1)}) custom-call(bf16[9,69,256]{2,1,0:T(8,128)(2,1)} %bitcast.17, f32[1,256]{1,0:T(1,128)} %bitcast.25, bf16[9,5,64]{2,1,0:T(8,128)(2,1)} %bitcast.19, f32[1,64]{1,0:T(1,128)} %bitcast.26, bf16[9,5,64]{2,1,0:T(8,128)(2,1)} %out_ref.1, ...), custom_call_target="tpu_custom_call" | custom-call | flops 2000000 | bytes 1500000 | tf_op jit(solution)/shard_map/prepare/pallas_call | solution.py:536
  23.7 0.0 all-to-all-done
  23.7 0.0 copy-start.1
  23.7 2.4 %sums.1.sums_ref.refs_1_ = f32[8,256,128]{2,1,0:T(8,128)S(1)} custom-call(bf16[128,384]{1,0:T(8,128)(2,1)S(1)} %bitcast.16), custom_call_target="tpu_custom_call" | custom-call | flops 4000000000 | bytes 1500000 | tf_op jit(solution)/shard_map/sums/pallas_call | solution.py:556
  26.1 0.0 copy-start.2
  26.1 0.0 copy-start.3
  26.1 0.0 collective-permute-done.near_ref
  26.1 0.0 collective-permute-done.1.far_ref
  26.1 0.0 copy-done.1
  26.1 2.1 %edges.1 = (f32[24,8,128]{2,1,0:T(8,128)S(1)}, f32[56,128]{1,0:T(8,128)S(1)}, f32[56,128]{1,0:T(8,128)S(1)}, f32[28,8,128]{2,1,0:T(8,128)S(1)}) custom-call(f32[80,128]{1,0:T(8,128)S(1)} %bitcast.15, f32[40,128]{1,0:T(8,128)S(1)} %collective-permute-done.near_ref, f32[40,128]{1,0:T(8,128)S(1)} %collective-permute-done.1.far_ref, ...), custom_call_target="tpu_custom_call" | custom-call | flops 1000000 | bytes 1500000 | tf_op jit(solution)/shard_map/edges/pallas_call | solution.py:569
  28.3 5.4 %collective-permute-start.2 = (f32[56,128]{1,0:T(8,128)S(1)}, f32[56,128]{1,0:T(8,128)S(1)}, u32[]{:S(2)}, u32[]{:S(2)}) collective-permute-start(f32[56,128]{1,0:T(8,128)S(1)} %get-tuple-element.22.refs_4_), channel_id=1, source_target_pairs={{16,32},{48,64},{80,96},{112,128},{144,160},{176,192},{208,224},{2... | collective-permute-start | bytes 86024 | tf_op jit(solution)/shard_map/ppermute | solution.py:488
  33.7 3.5 %collective-permute-start.3 = (f32[56,128]{1,0:T(8,128)S(1)}, f32[56,128]{1,0:T(8,128)S(1)}, u32[]{:S(2)}, u32[]{:S(2)}) collective-permute-start(f32[56,128]{1,0:T(8,128)S(1)} %get-tuple-element.23.refs_5_), channel_id=1, source_target_pairs={{0,16},{32,48},{64,80},{96,112},{128,144},{160,176},{192,208},{224... | collective-permute-start | bytes 86024 | tf_op jit(solution)/shard_map/ppermute | solution.py:488
  37.2 0.0 copy-done.2
  37.2 0.0 copy-done.3
  37.3 0.0 copy-start
  37.3 1.3 %first.1.refs_3_ = f32[24,8,128]{2,1,0:T(8,128)S(1)} custom-call(f32[28,8,128]{2,1,0:T(8,128)S(1)} %get-tuple-element.18.refs_0_, bf16[64,128]{1,0:T(8,128)(2,1)S(1)} %copy-done.3, bf16[80,64]{1,0:T(8,128)(2,1)S(1)} %copy-done.2), custom_call_target="tpu_custom_call" | custom-call | flops 2000000000 | bytes 500000 | tf_op jit(solution)/shard_map/first/pallas_call | solution.py:590
  38.5 0.0 copy-start.4
  38.5 0.0 collective-permute-done.2.refs_6_
  38.5 0.0 collective-permute-done.3.refs_7_
  38.6 0.0 copy-done
  38.6 0.6 %copy-done.4 = bf16[16,64]{1,0:T(8,128)(2,1)S(1)} copy-done((bf16[16,64]{1,0:T(8,128)(2,1)S(1)}, bf16[16,64]{1,0:T(8,128)(2,1)}, u32[]{:S(2)}) %copy-start.4) | copy-done | bytes 2072
  39.2 7.5 %solve.1 = (f32[80,128]{1,0:T(8,128)}, f32[1024,128]{1,0:T(8,128)}) custom-call(f32[28,8,128]{2,1,0:T(8,128)S(1)} %get-tuple-element.18.refs_0_, f32[8,256,128]{2,1,0:T(8,128)S(1)} %sums.1.sums_ref.refs_1_, f32[24,8,128]{2,1,0:T(8,128)S(1)} %get-tuple-element.19.refs_2_, f32[24,8,128]{2,1,0:T(8,128)S(1)} %first.1.refs_3_, ...), custom_call_target="tpu_custom_call" | custom-call | tf_op jit(solution)/shard_map/solve/pallas_call | solution.py:612
Async XLA Ops:
  2.8 11.4 %copy-start.6 = (f32[40,128]{1,0:T(8,128)S(1)}, f32[40,128]{1,0:T(8,128)}, u32[]{:S(2)}) copy-start(f32[40,128]{1,0:T(8,128)} %get-tuple-element.15) | copy-start | bytes 61444
  2.8 14.5 %copy-start.5 = (f32[40,128]{1,0:T(8,128)S(1)}, f32[40,128]{1,0:T(8,128)}, u32[]{:S(2)}) copy-start(f32[40,128]{1,0:T(8,128)} %get-tuple-element.16) | copy-start | bytes 61444
  2.8 20.8 %all-to-all-start = ((bf16[16,8,384]{2,1,0:T(8,128)(2,1)}), bf16[16,8,384]{2,1,0:T(8,128)(2,1)S(1)}, u32[]{:S(2)}, u32[]{:S(2)}) async-start(bf16[16,8,384]{2,1,0:T(8,128)(2,1)} %bitcast.18), calls=%async_computation | async-start | bytes 196608 | tf_op jit(solution)/shard_map/all_to_all | solution.py:531
  14.2 11.9 %collective-permute-start = (f32[40,128]{1,0:T(8,128)S(1)}, f32[40,128]{1,0:T(8,128)S(1)}, u32[]{:S(2)}, u32[]{:S(2)}) collective-permute-start(f32[40,128]{1,0:T(8,128)S(1)} %copy-done.6), channel_id=1, source_target_pairs={{0,1},{2,3},{4,5},{6,7},{8,9},{10,11},{12,13},{14,15},{1,0},{3,2},... | collective-permute-start | bytes 61448 | tf_op jit(solution)/shard_map/ppermute | solution.py:488
  17.3 8.8 %collective-permute-start.1 = (f32[40,128]{1,0:T(8,128)S(1)}, f32[40,128]{1,0:T(8,128)S(1)}, u32[]{:S(2)}, u32[]{:S(2)}) collective-permute-start(f32[40,128]{1,0:T(8,128)S(1)} %copy-done.5), channel_id=1, source_target_pairs={{1,2},{3,4},{5,6},{7,8},{9,10},{11,12},{13,14},{2,1},{4,3},{6,5},{... | collective-permute-start | bytes 61448 | tf_op jit(solution)/shard_map/ppermute | solution.py:488
  23.7 2.5 %copy-start.1 = (f32[5,16,128]{2,1,0:T(8,128)S(1)}, f32[5,16,128]{2,1,0:T(8,128)}, u32[]{:S(2)}) copy-start(f32[5,16,128]{2,1,0:T(8,128)} %param.13) | copy-start | bytes 122884
  26.1 11.1 %copy-start.2 = (bf16[80,64]{1,0:T(8,128)(2,1)S(1)}, bf16[80,64]{1,0:T(8,128)(2,1)}, u32[]{:S(2)}) copy-start(bf16[80,64]{1,0:T(8,128)(2,1)} %get-tuple-element.21.refs_2_.refs_9_) | copy-start | bytes 30724
  26.1 11.1 %copy-start.3 = (bf16[64,128]{1,0:T(8,128)(2,1)S(1)}, bf16[64,128]{1,0:T(8,128)(2,1)}, u32[]{:S(2)}) copy-start(bf16[64,128]{1,0:T(8,128)(2,1)} %get-tuple-element.20.refs_1_.refs_8_) | copy-start | bytes 49156
  28.3 10.3 %collective-permute-start.2 = (f32[56,128]{1,0:T(8,128)S(1)}, f32[56,128]{1,0:T(8,128)S(1)}, u32[]{:S(2)}, u32[]{:S(2)}) collective-permute-start(f32[56,128]{1,0:T(8,128)S(1)} %get-tuple-element.22.refs_4_), channel_id=1, source_target_pairs={{16,32},{48,64},{80,96},{112,128},{144,160},{176,192},{208,224},{2... | collective-permute-start | bytes 86024 | tf_op jit(solution)/shard_map/ppermute | solution.py:488
  33.7 4.9 %collective-permute-start.3 = (f32[56,128]{1,0:T(8,128)S(1)}, f32[56,128]{1,0:T(8,128)S(1)}, u32[]{:S(2)}, u32[]{:S(2)}) collective-permute-start(f32[56,128]{1,0:T(8,128)S(1)} %get-tuple-element.23.refs_5_), channel_id=1, source_target_pairs={{0,16},{32,48},{64,80},{96,112},{128,144},{160,176},{192,208},{224... | collective-permute-start | bytes 86024 | tf_op jit(solution)/shard_map/ppermute | solution.py:488
  37.3 1.3 %copy-start = (bf16[256,768]{1,0:T(8,128)(2,1)S(1)}, bf16[256,768]{1,0:T(8,128)(2,1)}, u32[]{:S(2)}) copy-start(bf16[256,768]{1,0:T(8,128)(2,1)} %get-tuple-element.24.refs_10_) | copy-start | bytes 1179652
  38.5 0.7 %copy-start.4 = (bf16[16,64]{1,0:T(8,128)(2,1)S(1)}, bf16[16,64]{1,0:T(8,128)(2,1)}, u32[]{:S(2)}) copy-start(bf16[16,64]{1,0:T(8,128)(2,1)} %get-tuple-element.25.refs_11_) | copy-start | bytes 6148

commit v7 on v6

--- a/solution.py
+++ b/solution.py
@@ -65,6 +65,9 @@
     g2 = s["02"] * here + s["12"] * here_right + s["22"] * above + s["23"] * above_right - s["d2"]
     g3 = s["03"] * here + s["13"] * here_right + s["23"] * above + s["33"] * above_right - s["d3"]
     return g0 + lane_roll(g1, 1), g2 + lane_roll(g3, 1)
+
+
+FACTOR_LANES = (16, 17, 20, 21, 24, 25)
 
 
 def edge_factors(now, before):
@@ -198,7 +201,7 @@
     even_lon = lax.axis_index("lon") % 2 == 0
     lane = lax.broadcasted_iota(jnp.int32, (8, LANES), 1)
     zero = jnp.zeros((8, LANES), F32)
-    east, west = zero, zero
+    east, west, factors = zero, zero, zero
     carried = zero
     for row in range(-6, ROWS + 6):
         field_ref[row + 6] = day_rows(near_ref, mid_ref, far_ref, even_lat, row)
@@ -220,12 +223,15 @@
                 west = jnp.where(picked, lane_roll(total, place + 8), west)
             if -2 <= row <= ROWS:
                 for k, (last, first) in enumerate(zip(*edge_factors(sums, before))):
-                    target = place + 16 + k
-                    east = jnp.where(lane == target, lane_roll(last, target - (COLS - 2)), east)
-                    west = jnp.where(lane == target, lane_roll(first, target), west)
+                    target = place + FACTOR_LANES[k]
+                    both = lane_roll(jnp.where(lane < 64, first, last), target - (COLS - 2))
+                    factors = jnp.where((lane == target) | (lane == target + 2), both, factors)
             carried = later
             before = sums
         if place == 96:
+            east = jnp.where(lane % 32 >= 16, factors, east)
+            west = jnp.where(lane % 32 >= 16, factors, west)
+            factors = zero
             to_near_ref[8 * part : 8 * part + 8, :] = jnp.where(even_lon, east, west)
             to_far_ref[8 * part : 8 * part + 8, :] = jnp.where(even_lon, west, east)
             east, west = zero, zero
@@ -452,13 +458,13 @@
     above = lane_roll(here, -32)
 
     def edge_term(source, lane_at, inner):
-        constant, own, beside, up, up_beside, down_beside = [lane_roll(source, lane_at - (16 + k)) for k in range(6)]
+        constant, own, beside, up, up_beside, down_beside = [lane_roll(source, lane_at - k) for k in FACTOR_LANES]
         here_beside = lane_roll(here, inner)
         total = own * here + beside * here_beside + up * above + up_beside * lane_roll(above, inner) - constant
         return total + lane_roll(up * here + down_beside * here_beside, 32)
 
     extra_w = edge_term(from_west, 7, 1)
-    extra_e = edge_term(from_east, 24, -1)
+    extra_e = edge_term(from_east, 24 - 2, -1)
     grad_ref[:, strips] = (
         grad_ref[:, strips] + jnp.where(strip_lane % 32 < 16, extra_w, extra_e)
     ) * mask_ref[:, strips]
@@ -543,6 +549,7 @@
         ),
         in_specs=[vmem] * 6,
         out_specs=(vmem,) * 4,
+        compiler_params=pltpu.CompilerParams(vmem_limit_bytes=16 * 1024 * 1024),
         cost_estimate=pl.CostEstimate(flops=2_000_000, bytes_accessed=1_500_000, transcendentals=0),
         name="prepare",
     )(

time: 47.1 us -> 45.7 us (0.970)
  Pallas kernels: 17.5 us -> 15.1 us
  local copies, waits for them, and re-layouts: 0.68 us -> 1.65 us
    pallas_call x1, Pallas kernels: 2.05 us -> 0.3 us  [on_device(): pl.pallas_call(prepare_kernel, out_shape=(jax.ShapeDtypeStruct((4 * HID,...]
    unnamed x14 -> x18, local copies, waits for them, and re-layouts: 0.68 us -> 1.65 us
    pallas_call x1, Pallas kernels: 2.1 us -> 1.46 us  [on_device(): pl.pallas_call(edges_kernel, out_shape=(jax.ShapeDtypeStruct((24, 8, LANE...]
  transfers between devices with their start and end apart: 5 -> 5, of which waited for: 0 -> 0; matrix products, arithmetic and copies ran while one was open for 0% -> 0% of each run, Pallas kernels for 12% -> 9%
where the time goes in v7:
time: 45.7 us; the launch traced here: 45.3 us
  starting transfers between devices  27.7 us (61%)
  Pallas kernels  15.1 us (33%)
  local copies, waits for them, and re-layouts  1.65 us (4%)
  between operations  0.79 us (2%)
    ppermute x4, starting transfers between devices, swap(): lax.ppermute(value, axis, pairs + [(target, source) for source, target in...  16.4 us
    all_to_all x1, starting transfers between devices, on_device(): lax.all_to_all(track.reshape(lat_count, 8, SENT), 'lat', split_axis=0, co...  11.4 us
    pallas_call x1, Pallas kernels, on_device(): pl.pallas_call(solve, out_shape=(jax.ShapeDtypeStruct((DAYS * ROWS, LANES...  7.46 us
    pallas_call x1, Pallas kernels, on_device(): pl.pallas_call(sums_kernel, out_shape=jax.ShapeDtypeStruct((8, 256, LANES...  2.42 us
    pallas_call x1, Pallas kernels, on_device(): pl.pallas_call(track_kernel, out_shape=(jax.ShapeDtypeStruct((lat_count *...  2.17 us
    unnamed x18, local copies, waits for them, and re-layouts  1.65 us
    pallas_call x1, Pallas kernels, on_device(): pl.pallas_call(edges_kernel, out_shape=(jax.ShapeDtypeStruct((24, 8, LANE...  1.46 us
    pallas_call x1, Pallas kernels, on_device(): pl.pallas_call(first, out_shape=jax.ShapeDtypeStruct((24, 8, LANES), F32)...  1.26 us
  transfers between devices with their start and end apart: 5, of which 0 were waited for; matrix products, arithmetic and copies ran while one was open for 0% of the time, Pallas kernels for 9%

profile of v7, /device:TPU:3, one launch (start us, length us, event | category | flops | bytes accessed | tf_op | source)
XLA Modules:
  0.0 45.3 jit_solution(12159095490835857188)
XLA Ops:
  0.6 2.2 %track.1 = (bf16[128,384]{1,0:T(8,128)(2,1)}, f32[40,128]{1,0:T(8,128)}, f32[40,128]{1,0:T(8,128)}) custom-call(f32[1,512]{1,0:T(1,128)} %bitcast.22, f32[4,512]{1,0:T(4,128)} %weight_ref.1, s32[1,512]{1,0:T(1,128)} %bitcast.23, s32[1,512]{1,0:T(1,128)} %bitcast.24, s32[1,512]{1,0:T(1,128)} %bitcast.25, s32[1,512]{1,0:T(1,128)} %bitcast.26, f32[80,128]{1,0:T(8,128)} %bitcast.15), custom_call_target="tpu_custom_call" | custom-call | flops 100000 | bytes 150000 | tf_op jit(solution)/shard_map/track/pallas_call | solution.py:517
  2.8 0.0 copy-start.8
  2.8 0.0 copy-start.7
  2.8 0.0 copy-start.3
  2.8 11.4 %all-to-all-start = ((bf16[16,8,384]{2,1,0:T(8,128)(2,1)}), bf16[16,8,384]{2,1,0:T(8,128)(2,1)S(1)}, u32[]{:S(2)}, u32[]{:S(2)}) async-start(bf16[16,8,384]{2,1,0:T(8,128)(2,1)} %bitcast.21), calls=%async_computation | async-start | bytes 196608 | tf_op jit(solution)/shard_map/all_to_all | solution.py:537
  14.2 0.0 copy-done.8
  14.2 3.1 %collective-permute-start = (f32[40,128]{1,0:T(8,128)S(1)}, f32[40,128]{1,0:T(8,128)S(1)}, u32[]{:S(2)}, u32[]{:S(2)}) collective-permute-start(f32[40,128]{1,0:T(8,128)S(1)} %copy-done.8), channel_id=1, source_target_pairs={{0,1},{2,3},{4,5},{6,7},{8,9},{10,11},{12,13},{14,15},{1,0},{3,2},... | collective-permute-start | bytes 61448 | tf_op jit(solution)/shard_map/ppermute | solution.py:494
  17.3 0.0 copy-done.7
  17.3 4.3 %collective-permute-start.1 = (f32[40,128]{1,0:T(8,128)S(1)}, f32[40,128]{1,0:T(8,128)S(1)}, u32[]{:S(2)}, u32[]{:S(2)}) collective-permute-start(f32[40,128]{1,0:T(8,128)S(1)} %copy-done.7), channel_id=1, source_target_pairs={{1,2},{3,4},{5,6},{7,8},{9,10},{11,12},{13,14},{2,1},{4,3},{6,5},{... | collective-permute-start | bytes 61448 | tf_op jit(solution)/shard_map/ppermute | solution.py:494
  21.6 0.0 copy-start.4
  21.6 0.0 copy-start.5
  21.7 0.0 copy-start.6
  21.7 0.0 copy-done.2
  21.7 0.0 copy-done.3
  21.7 0.6 %copy-done.4 = bf16[5,64]{1,0:T(8,128)(2,1)S(1)} copy-done((bf16[5,64]{1,0:T(8,128)(2,1)S(1)}, bf16[5,64]{1,0:T(8,128)(2,1)}, u32[]{:S(2)}) %copy-start.4) | copy-done | bytes 664
  22.3 0.0 copy-done.5
  22.3 0.0 copy-done.6
  22.3 1.0 %copy-done = bf16[9,256,69]{1,2,0:T(8,128)(2,1)S(1)} copy-done((bf16[9,256,69]{1,2,0:T(8,128)(2,1)S(1)}, bf16[9,256,69]{1,2,0:T(8,128)(2,1)}, u32[]{:S(2)}) %copy-start) | copy-done | bytes 317976
  23.3 0.3 prepare.1
  23.6 0.0 all-to-all-done
  23.6 0.0 copy-start.1
  23.6 2.4 %sums.1.sums_ref.refs_1_ = f32[8,256,128]{2,1,0:T(8,128)S(1)} custom-call(bf16[128,384]{1,0:T(8,128)(2,1)S(1)} %bitcast.17), custom_call_target="tpu_custom_call" | custom-call | flops 4000000000 | bytes 1500000 | tf_op jit(solution)/shard_map/sums/pallas_call | solution.py:563
  26.1 0.0 collective-permute-done.near_ref
  26.1 0.0 collective-permute-done.1.far_ref
  26.1 0.0 copy-done.1
  26.1 1.5 %edges.1 = (f32[24,8,128]{2,1,0:T(8,128)S(1)}, f32[56,128]{1,0:T(8,128)S(1)}, f32[56,128]{1,0:T(8,128)S(1)}, f32[28,8,128]{2,1,0:T(8,128)S(1)}) custom-call(f32[80,128]{1,0:T(8,128)S(1)} %bitcast.16, f32[40,128]{1,0:T(8,128)S(1)} %collective-permute-done.near_ref, f32[40,128]{1,0:T(8,128)S(1)} %collective-permute-done.1.far_ref, ...), custom_call_target="tpu_custom_call" | custom-call | flops 1000000 | bytes 1500000 | tf_op jit(solution)/shard_map/edges/pallas_call | solution.py:576
  27.6 5.4 %collective-permute-start.2 = (f32[56,128]{1,0:T(8,128)S(1)}, f32[56,128]{1,0:T(8,128)S(1)}, u32[]{:S(2)}, u32[]{:S(2)}) collective-permute-start(f32[56,128]{1,0:T(8,128)S(1)} %get-tuple-element.22.refs_4_), channel_id=1, source_target_pairs={{16,32},{48,64},{80,96},{112,128},{144,160},{176,192},{208,224},{2... | collective-permute-start | bytes 86024 | tf_op jit(solution)/shard_map/ppermute | solution.py:494
  33.0 3.5 %collective-permute-start.3 = (f32[56,128]{1,0:T(8,128)S(1)}, f32[56,128]{1,0:T(8,128)S(1)}, u32[]{:S(2)}, u32[]{:S(2)}) collective-permute-start(f32[56,128]{1,0:T(8,128)S(1)} %get-tuple-element.23.refs_5_), channel_id=1, source_target_pairs={{0,16},{32,48},{64,80},{96,112},{128,144},{160,176},{192,208},{224... | collective-permute-start | bytes 86024 | tf_op jit(solution)/shard_map/ppermute | solution.py:494
  36.5 1.3 %first.1.refs_3_ = f32[24,8,128]{2,1,0:T(8,128)S(1)} custom-call(f32[28,8,128]{2,1,0:T(8,128)S(1)} %get-tuple-element.18.refs_0_, bf16[64,128]{1,0:T(8,128)(2,1)S(1)} %get-tuple-element.20.refs_1_.refs_8_, bf16[80,64]{1,0:T(8,128)(2,1)S(1)} %get-tuple-element.21.refs_2_.refs_9_), custom_call_target="tpu_custom_call" | custom-call | flops 2000000000 | bytes 500000 | tf_op jit(solution)/shard_map/first/pallas_call | solution.py:597
  37.8 0.0 collective-permute-done.2.refs_6_
  37.8 0.0 collective-permute-done.3.refs_7_
  37.8 7.5 %solve.1 = (f32[80,128]{1,0:T(8,128)}, f32[1024,128]{1,0:T(8,128)}) custom-call(f32[28,8,128]{2,1,0:T(8,128)S(1)} %get-tuple-element.18.refs_0_, f32[8,256,128]{2,1,0:T(8,128)S(1)} %sums.1.sums_ref.refs_1_, f32[24,8,128]{2,1,0:T(8,128)S(1)} %get-tuple-element.19.refs_2_, f32[24,8,128]{2,1,0:T(8,128)S(1)} %first.1.refs_3_, ...), custom_call_target="tpu_custom_call" | custom-call | tf_op jit(solution)/shard_map/solve/pallas_call | solution.py:619
  (2 shorter events, 0.0 us)
Async XLA Ops:
  2.8 11.4 %copy-start.8 = (f32[40,128]{1,0:T(8,128)S(1)}, f32[40,128]{1,0:T(8,128)}, u32[]{:S(2)}) copy-start(f32[40,128]{1,0:T(8,128)} %get-tuple-element.15) | copy-start | bytes 61444
  2.8 14.5 %copy-start.7 = (f32[40,128]{1,0:T(8,128)S(1)}, f32[40,128]{1,0:T(8,128)}, u32[]{:S(2)}) copy-start(f32[40,128]{1,0:T(8,128)} %get-tuple-element.16) | copy-start | bytes 61444
  2.8 18.9 %copy-start.2 = (bf16[9,64,5]{1,2,0:T(8,128)(2,1)S(1)}, bf16[9,64,5]{1,2,0:T(8,128)(2,1)}, u32[]{:S(2)}) copy-start(bf16[9,64,5]{1,2,0:T(8,128)(2,1)} %param.14) | copy-start | bytes 17284
  2.8 18.9 %copy-start.3 = (bf16[9,5,64]{2,1,0:T(8,128)(2,1)S(1)}, bf16[9,5,64]{2,1,0:T(8,128)(2,1)}, u32[]{:S(2)}) copy-start(bf16[9,5,64]{2,1,0:T(8,128)(2,1)} %out_ref.1) | copy-start | bytes 17284
  2.8 20.8 %all-to-all-start = ((bf16[16,8,384]{2,1,0:T(8,128)(2,1)}), bf16[16,8,384]{2,1,0:T(8,128)(2,1)S(1)}, u32[]{:S(2)}, u32[]{:S(2)}) async-start(bf16[16,8,384]{2,1,0:T(8,128)(2,1)} %bitcast.21), calls=%async_computation | async-start | bytes 196608 | tf_op jit(solution)/shard_map/all_to_all | solution.py:537
  14.2 11.8 %collective-permute-start = (f32[40,128]{1,0:T(8,128)S(1)}, f32[40,128]{1,0:T(8,128)S(1)}, u32[]{:S(2)}, u32[]{:S(2)}) collective-permute-start(f32[40,128]{1,0:T(8,128)S(1)} %copy-done.8), channel_id=1, source_target_pairs={{0,1},{2,3},{4,5},{6,7},{8,9},{10,11},{12,13},{14,15},{1,0},{3,2},... | collective-permute-start | bytes 61448 | tf_op jit(solution)/shard_map/ppermute | solution.py:494
  17.3 8.7 %collective-permute-start.1 = (f32[40,128]{1,0:T(8,128)S(1)}, f32[40,128]{1,0:T(8,128)S(1)}, u32[]{:S(2)}, u32[]{:S(2)}) collective-permute-start(f32[40,128]{1,0:T(8,128)S(1)} %copy-done.7), channel_id=1, source_target_pairs={{1,2},{3,4},{5,6},{7,8},{9,10},{11,12},{13,14},{2,1},{4,3},{6,5},{... | collective-permute-start | bytes 61448 | tf_op jit(solution)/shard_map/ppermute | solution.py:494
  21.6 0.7 %copy-start.4 = (bf16[5,64]{1,0:T(8,128)(2,1)S(1)}, bf16[5,64]{1,0:T(8,128)(2,1)}, u32[]{:S(2)}) copy-start(bf16[5,64]{1,0:T(8,128)(2,1)} %inc_ref.1) | copy-start | bytes 1924
  21.6 0.7 %copy-start.5 = (f32[256]{0:T(256)S(1)}, f32[256]{0:T(256)}, u32[]{:S(2)}) copy-start(f32[256]{0:T(256)} %param.18) | copy-start | bytes 3076
  21.7 0.7 %copy-start.6 = (f32[64]{0:T(128)S(1)}, f32[64]{0:T(128)}, u32[]{:S(2)}) copy-start(f32[64]{0:T(128)} %param.15) | copy-start | bytes 772
  22.3 1.0 %copy-start = (bf16[9,256,69]{1,2,0:T(8,128)(2,1)S(1)}, bf16[9,256,69]{1,2,0:T(8,128)(2,1)}, u32[]{:S(2)}) copy-start(bf16[9,256,69]{1,2,0:T(8,128)(2,1)} %param.17) | copy-start | bytes 953860
  23.6 2.5 %copy-start.1 = (f32[5,16,128]{2,1,0:T(8,128)S(1)}, f32[5,16,128]{2,1,0:T(8,128)}, u32[]{:S(2)}) copy-start(f32[5,16,128]{2,1,0:T(8,128)} %param.13) | copy-start | bytes 122884
  27.6 10.2 %collective-permute-start.2 = (f32[56,128]{1,0:T(8,128)S(1)}, f32[56,128]{1,0:T(8,128)S(1)}, u32[]{:S(2)}, u32[]{:S(2)}) collective-permute-start(f32[56,128]{1,0:T(8,128)S(1)} %get-tuple-element.22.refs_4_), channel_id=1, source_target_pairs={{16,32},{48,64},{80,96},{112,128},{144,160},{176,192},{208,224},{2... | collective-permute-start | bytes 86024 | tf_op jit(solution)/shard_map/ppermute | solution.py:494
  33.0 4.8 %collective-permute-start.3 = (f32[56,128]{1,0:T(8,128)S(1)}, f32[56,128]{1,0:T(8,128)S(1)}, u32[]{:S(2)}, u32[]{:S(2)}) collective-permute-start(f32[56,128]{1,0:T(8,128)S(1)} %get-tuple-element.23.refs_5_), channel_id=1, source_target_pairs={{0,16},{32,48},{64,80},{96,112},{128,144},{160,176},{192,208},{224... | collective-permute-start | bytes 86024 | tf_op jit(solution)/shard_map/ppermute | solution.py:494

commit v8 on v7

--- a/solution.py
+++ b/solution.py
@@ -330,15 +330,17 @@
     def within(row):
         return row_mask(lat_count, row)
 
-    def left(main, strip, row):
-        part, place = strip_place(row)
-        edge = lane_roll(strip[:, tile(part)], -(place + 7))
-        return jnp.where(lane[: main.shape[0]] == 0, edge, lane_roll(main, 1))
-
-    def right(main, strip, row):
-        part, place = strip_place(row)
-        edge = lane_roll(strip[:, tile(part)], 127 - (place + 24))
-        return jnp.where(lane[: main.shape[0]] == 127, edge, lane_roll(main, -1))
+    def edge_lanes(left_strip, right_strip):
+        place = lax.broadcasted_iota(jnp.int32, left_strip.shape, 1)
+        return jnp.where(place % 32 == 8, lane_roll(right_strip, -16), left_strip)
+
+    def beside(left_main, right_main, edges, place):
+        lanes = lax.broadcasted_iota(jnp.int32, left_main.shape, 1)
+        edge = lane_roll(edges, 120 - place)
+        return (
+            lane_roll(jnp.where(lanes == 127, edge, left_main), 1),
+            lane_roll(jnp.where(lanes == 0, edge, right_main), -1),
+        )
 
     est_ref[:, at(-7)] = zero
     est_ref[:, at(22)] = zero
@@ -373,10 +375,11 @@
 
     def windows(ref, first_row, last_row, with_strips):
         strip = ref[:, strips]
+        edges = edge_lanes(strip, strip)
         for row in range(first_row - 1, last_row + 2) if first_row <= last_row else ():
             main = ref[:, at(row)]
-            minus_ref[:, at(row)] = left(main, strip, row)
-            plus_ref[:, at(row)] = right(main, strip, row)
+            part, place = strip_place(row)
+            minus_ref[:, at(row)], plus_ref[:, at(row)] = beside(main, main, edges[:, tile(part)], place)
         for row in range(first_row, last_row + 1):
             pieces = [source[:, at(row + a)] for a in (-1, 0, 1) for source in (minus_ref, ref, plus_ref)]
             window_ref[:, at(row)] = jnp.concatenate(pieces + [ones], axis=0).astype(BF16)
@@ -409,10 +412,12 @@
             totals.append(total)
         strip = est_ref[:, strips] - (totals[1] + lane_roll(totals[0], 1) + lane_roll(totals[2], -1))
         grad_ref[:, strips] = strip
+        edges = edge_lanes(totals[0], totals[2])
         for row in range(first_row, last_row + 1):
             columns = spread_terms(spread_ref, row)
-            term = columns[1] + left(columns[0], totals[0], row) + right(columns[2], totals[2], row)
-            grad_ref[:, at(row)] = est_ref[:, at(row)] - term
+            part, place = strip_place(row)
+            from_left, from_right = beside(columns[0], columns[2], edges[:, tile(part)], place)
+            grad_ref[:, at(row)] = est_ref[:, at(row)] - (columns[1] + from_left + from_right)
         return strip
 
     strip = gradient(0, -1, 0, -1)
@@ -439,13 +444,14 @@
         update = jnp.dot(w_inc_ref[...], hidden, preferred_element_type=F32)
         est_ref[:, where] -= update[0:8]
 
-    lane64 = lax.broadcasted_iota(jnp.int32, (HID, LANES), 1)
+    hidden_edges = {}
     for row in range(-1, ROWS + 1):
         part, place = strip_place(row)
+        if part not in hidden_edges:
+            strip = hidden_ref[:, tile(STRIP + part)]
+            hidden_edges[part] = edge_lanes(strip, strip)
         main = hidden_ref[:, at(row)]
-        strip = hidden_ref[:, tile(STRIP + part)]
-        hid_minus_ref[:, at(row)] = jnp.where(lane64 == 0, lane_roll(strip, -(place + 7)), lane_roll(main, 1))
-        hid_plus_ref[:, at(row)] = jnp.where(lane64 == 127, lane_roll(strip, 127 - (place + 24)), lane_roll(main, -1))
+        hid_minus_ref[:, at(row)], hid_plus_ref[:, at(row)] = beside(main, main, hidden_edges[part], place)
     gradient(-1, 16, -2, 17)
     carried = zero
     for row in range(-2, ROWS + 1):

time: 45.7 us -> 46.6 us (1.020)
  Pallas kernels: 15.1 us -> 16 us
    pallas_call x1, Pallas kernels: 7.46 us -> 8.34 us  [on_device(): pl.pallas_call(solve, out_shape=(jax.ShapeDtypeStruct((DAYS * ROWS, LANES...]
where the time goes in v8:
time: 46.6 us; the launch traced here: 46.2 us
  starting transfers between devices  27.7 us (59%)
  Pallas kernels  16 us (34%)
  local copies, waits for them, and re-layouts  1.65 us (4%)
  between operations  0.79 us (2%)
    ppermute x4, starting transfers between devices, swap(): lax.ppermute(value, axis, pairs + [(target, source) for source, target in...  16.4 us
    all_to_all x1, starting transfers between devices, on_device(): lax.all_to_all(track.reshape(lat_count, 8, SENT), 'lat', split_axis=0, co...  11.4 us
    pallas_call x1, Pallas kernels, on_device(): pl.pallas_call(solve, out_shape=(jax.ShapeDtypeStruct((DAYS * ROWS, LANES...  8.34 us
    pallas_call x1, Pallas kernels, on_device(): pl.pallas_call(sums_kernel, out_shape=jax.ShapeDtypeStruct((8, 256, LANES...  2.42 us
    pallas_call x1, Pallas kernels, on_device(): pl.pallas_call(track_kernel, out_shape=(jax.ShapeDtypeStruct((lat_count *...  2.17 us
    unnamed x18, local copies, waits for them, and re-layouts  1.65 us
    pallas_call x1, Pallas kernels, on_device(): pl.pallas_call(edges_kernel, out_shape=(jax.ShapeDtypeStruct((24, 8, LANE...  1.46 us
    pallas_call x1, Pallas kernels, on_device(): pl.pallas_call(first, out_shape=jax.ShapeDtypeStruct((24, 8, LANES), F32)...  1.26 us
  transfers between devices with their start and end apart: 5, of which 0 were waited for; matrix products, arithmetic and copies ran while one was open for 0% of the time, Pallas kernels for 9%

profile of v8, /device:TPU:3, one launch (start us, length us, event | category | flops | bytes accessed | tf_op | source)
XLA Modules:
  0.0 46.2 jit_solution(11050115829553191093)
XLA Ops:
  0.6 2.2 %track.1 = (bf16[128,384]{1,0:T(8,128)(2,1)}, f32[40,128]{1,0:T(8,128)}, f32[40,128]{1,0:T(8,128)}) custom-call(f32[1,512]{1,0:T(1,128)} %bitcast.22, f32[4,512]{1,0:T(4,128)} %weight_ref.1, s32[1,512]{1,0:T(1,128)} %bitcast.23, s32[1,512]{1,0:T(1,128)} %bitcast.24, s32[1,512]{1,0:T(1,128)} %bitcast.25, s32[1,512]{1,0:T(1,128)} %bitcast.26, f32[80,128]{1,0:T(8,128)} %bitcast.15), custom_call_target="tpu_custom_call" | custom-call | flops 100000 | bytes 150000 | tf_op jit(solution)/shard_map/track/pallas_call | solution.py:523
  2.8 0.0 copy-start.8
  2.8 0.0 copy-start.7
  2.8 0.0 copy-start.3
  2.8 11.4 %all-to-all-start = ((bf16[16,8,384]{2,1,0:T(8,128)(2,1)}), bf16[16,8,384]{2,1,0:T(8,128)(2,1)S(1)}, u32[]{:S(2)}, u32[]{:S(2)}) async-start(bf16[16,8,384]{2,1,0:T(8,128)(2,1)} %bitcast.21), calls=%async_computation | async-start | bytes 196608 | tf_op jit(solution)/shard_map/all_to_all | solution.py:543
  14.2 0.0 copy-done.8
  14.2 3.1 %collective-permute-start = (f32[40,128]{1,0:T(8,128)S(1)}, f32[40,128]{1,0:T(8,128)S(1)}, u32[]{:S(2)}, u32[]{:S(2)}) collective-permute-start(f32[40,128]{1,0:T(8,128)S(1)} %copy-done.8), channel_id=1, source_target_pairs={{0,1},{2,3},{4,5},{6,7},{8,9},{10,11},{12,13},{14,15},{1,0},{3,2},... | collective-permute-start | bytes 61448 | tf_op jit(solution)/shard_map/ppermute | solution.py:500
  17.3 0.0 copy-done.7
  17.3 4.3 %collective-permute-start.1 = (f32[40,128]{1,0:T(8,128)S(1)}, f32[40,128]{1,0:T(8,128)S(1)}, u32[]{:S(2)}, u32[]{:S(2)}) collective-permute-start(f32[40,128]{1,0:T(8,128)S(1)} %copy-done.7), channel_id=1, source_target_pairs={{1,2},{3,4},{5,6},{7,8},{9,10},{11,12},{13,14},{2,1},{4,3},{6,5},{... | collective-permute-start | bytes 61448 | tf_op jit(solution)/shard_map/ppermute | solution.py:500
  21.6 0.0 copy-start.4
  21.6 0.0 copy-start.5
  21.7 0.0 copy-start.6
  21.7 0.0 copy-done.2
  21.7 0.0 copy-done.3
  21.7 0.6 %copy-done.4 = bf16[5,64]{1,0:T(8,128)(2,1)S(1)} copy-done((bf16[5,64]{1,0:T(8,128)(2,1)S(1)}, bf16[5,64]{1,0:T(8,128)(2,1)}, u32[]{:S(2)}) %copy-start.4) | copy-done | bytes 664
  22.3 0.0 copy-done.5
  22.3 0.0 copy-done.6
  22.3 1.0 %copy-done = bf16[9,256,69]{1,2,0:T(8,128)(2,1)S(1)} copy-done((bf16[9,256,69]{1,2,0:T(8,128)(2,1)S(1)}, bf16[9,256,69]{1,2,0:T(8,128)(2,1)}, u32[]{:S(2)}) %copy-start) | copy-done | bytes 317976
  23.3 0.3 prepare.1
  23.6 0.0 all-to-all-done
  23.6 0.0 copy-start.1
  23.6 2.4 %sums.1.sums_ref.refs_1_ = f32[8,256,128]{2,1,0:T(8,128)S(1)} custom-call(bf16[128,384]{1,0:T(8,128)(2,1)S(1)} %bitcast.17), custom_call_target="tpu_custom_call" | custom-call | flops 4000000000 | bytes 1500000 | tf_op jit(solution)/shard_map/sums/pallas_call | solution.py:569
  26.1 0.0 collective-permute-done.near_ref
  26.1 0.0 collective-permute-done.1.far_ref
  26.1 0.0 copy-done.1
  26.1 1.5 %edges.1 = (f32[24,8,128]{2,1,0:T(8,128)S(1)}, f32[56,128]{1,0:T(8,128)S(1)}, f32[56,128]{1,0:T(8,128)S(1)}, f32[28,8,128]{2,1,0:T(8,128)S(1)}) custom-call(f32[80,128]{1,0:T(8,128)S(1)} %bitcast.16, f32[40,128]{1,0:T(8,128)S(1)} %collective-permute-done.near_ref, f32[40,128]{1,0:T(8,128)S(1)} %collective-permute-done.1.far_ref, ...), custom_call_target="tpu_custom_call" | custom-call | flops 1000000 | bytes 1500000 | tf_op jit(solution)/shard_map/edges/pallas_call | solution.py:582
  27.6 5.4 %collective-permute-start.2 = (f32[56,128]{1,0:T(8,128)S(1)}, f32[56,128]{1,0:T(8,128)S(1)}, u32[]{:S(2)}, u32[]{:S(2)}) collective-permute-start(f32[56,128]{1,0:T(8,128)S(1)} %get-tuple-element.22.refs_4_), channel_id=1, source_target_pairs={{16,32},{48,64},{80,96},{112,128},{144,160},{176,192},{208,224},{2... | collective-permute-start | bytes 86024 | tf_op jit(solution)/shard_map/ppermute | solution.py:500
  33.0 3.5 %collective-permute-start.3 = (f32[56,128]{1,0:T(8,128)S(1)}, f32[56,128]{1,0:T(8,128)S(1)}, u32[]{:S(2)}, u32[]{:S(2)}) collective-permute-start(f32[56,128]{1,0:T(8,128)S(1)} %get-tuple-element.23.refs_5_), channel_id=1, source_target_pairs={{0,16},{32,48},{64,80},{96,112},{128,144},{160,176},{192,208},{224... | collective-permute-start | bytes 86024 | tf_op jit(solution)/shard_map/ppermute | solution.py:500
  36.5 1.3 %first.1.refs_3_ = f32[24,8,128]{2,1,0:T(8,128)S(1)} custom-call(f32[28,8,128]{2,1,0:T(8,128)S(1)} %get-tuple-element.18.refs_0_, bf16[64,128]{1,0:T(8,128)(2,1)S(1)} %get-tuple-element.20.refs_1_.refs_8_, bf16[80,64]{1,0:T(8,128)(2,1)S(1)} %get-tuple-element.21.refs_2_.refs_9_), custom_call_target="tpu_custom_call" | custom-call | flops 2000000000 | bytes 500000 | tf_op jit(solution)/shard_map/first/pallas_call | solution.py:603
  37.8 0.0 collective-permute-done.2.refs_6_
  37.8 0.0 collective-permute-done.3.refs_7_
  37.8 8.3 %solve.1 = (f32[80,128]{1,0:T(8,128)}, f32[1024,128]{1,0:T(8,128)}) custom-call(f32[28,8,128]{2,1,0:T(8,128)S(1)} %get-tuple-element.18.refs_0_, f32[8,256,128]{2,1,0:T(8,128)S(1)} %sums.1.sums_ref.refs_1_, f32[24,8,128]{2,1,0:T(8,128)S(1)} %get-tuple-element.19.refs_2_, f32[24,8,128]{2,1,0:T(8,128)S(1)} %first.1.refs_3_, ...), custom_call_target="tpu_custom_call" | custom-call | tf_op jit(solution)/shard_map/solve/pallas_call | solution.py:625
  (2 shorter events, 0.0 us)
Async XLA Ops:
  2.8 11.4 %copy-start.8 = (f32[40,128]{1,0:T(8,128)S(1)}, f32[40,128]{1,0:T(8,128)}, u32[]{:S(2)}) copy-start(f32[40,128]{1,0:T(8,128)} %get-tuple-element.15) | copy-start | bytes 61444
  2.8 14.5 %copy-start.7 = (f32[40,128]{1,0:T(8,128)S(1)}, f32[40,128]{1,0:T(8,128)}, u32[]{:S(2)}) copy-start(f32[40,128]{1,0:T(8,128)} %get-tuple-element.16) | copy-start | bytes 61444
  2.8 18.9 %copy-start.2 = (bf16[9,64,5]{1,2,0:T(8,128)(2,1)S(1)}, bf16[9,64,5]{1,2,0:T(8,128)(2,1)}, u32[]{:S(2)}) copy-start(bf16[9,64,5]{1,2,0:T(8,128)(2,1)} %param.14) | copy-start | bytes 17284
  2.8 18.9 %copy-start.3 = (bf16[9,5,64]{2,1,0:T(8,128)(2,1)S(1)}, bf16[9,5,64]{2,1,0:T(8,128)(2,1)}, u32[]{:S(2)}) copy-start(bf16[9,5,64]{2,1,0:T(8,128)(2,1)} %out_ref.1) | copy-start | bytes 17284
  2.8 20.8 %all-to-all-start = ((bf16[16,8,384]{2,1,0:T(8,128)(2,1)}), bf16[16,8,384]{2,1,0:T(8,128)(2,1)S(1)}, u32[]{:S(2)}, u32[]{:S(2)}) async-start(bf16[16,8,384]{2,1,0:T(8,128)(2,1)} %bitcast.21), calls=%async_computation | async-start | bytes 196608 | tf_op jit(solution)/shard_map/all_to_all | solution.py:543
  14.2 11.8 %collective-permute-start = (f32[40,128]{1,0:T(8,128)S(1)}, f32[40,128]{1,0:T(8,128)S(1)}, u32[]{:S(2)}, u32[]{:S(2)}) collective-permute-start(f32[40,128]{1,0:T(8,128)S(1)} %copy-done.8), channel_id=1, source_target_pairs={{0,1},{2,3},{4,5},{6,7},{8,9},{10,11},{12,13},{14,15},{1,0},{3,2},... | collective-permute-start | bytes 61448 | tf_op jit(solution)/shard_map/ppermute | solution.py:500
  17.3 8.7 %collective-permute-start.1 = (f32[40,128]{1,0:T(8,128)S(1)}, f32[40,128]{1,0:T(8,128)S(1)}, u32[]{:S(2)}, u32[]{:S(2)}) collective-permute-start(f32[40,128]{1,0:T(8,128)S(1)} %copy-done.7), channel_id=1, source_target_pairs={{1,2},{3,4},{5,6},{7,8},{9,10},{11,12},{13,14},{2,1},{4,3},{6,5},{... | collective-permute-start | bytes 61448 | tf_op jit(solution)/shard_map/ppermute | solution.py:500
  21.6 0.7 %copy-start.4 = (bf16[5,64]{1,0:T(8,128)(2,1)S(1)}, bf16[5,64]{1,0:T(8,128)(2,1)}, u32[]{:S(2)}) copy-start(bf16[5,64]{1,0:T(8,128)(2,1)} %inc_ref.1) | copy-start | bytes 1924
  21.6 0.7 %copy-start.5 = (f32[256]{0:T(256)S(1)}, f32[256]{0:T(256)}, u32[]{:S(2)}) copy-start(f32[256]{0:T(256)} %param.18) | copy-start | bytes 3076
  21.7 0.7 %copy-start.6 = (f32[64]{0:T(128)S(1)}, f32[64]{0:T(128)}, u32[]{:S(2)}) copy-start(f32[64]{0:T(128)} %param.15) | copy-start | bytes 772
  22.3 1.0 %copy-start = (bf16[9,256,69]{1,2,0:T(8,128)(2,1)S(1)}, bf16[9,256,69]{1,2,0:T(8,128)(2,1)}, u32[]{:S(2)}) copy-start(bf16[9,256,69]{1,2,0:T(8,128)(2,1)} %param.17) | copy-start | bytes 953860
  23.6 2.5 %copy-start.1 = (f32[5,16,128]{2,1,0:T(8,128)S(1)}, f32[5,16,128]{2,1,0:T(8,128)}, u32[]{:S(2)}) copy-start(f32[5,16,128]{2,1,0:T(8,128)} %param.13) | copy-start | bytes 122884
  27.6 10.2 %collective-permute-start.2 = (f32[56,128]{1,0:T(8,128)S(1)}, f32[56,128]{1,0:T(8,128)S(1)}, u32[]{:S(2)}, u32[]{:S(2)}) collective-permute-start(f32[56,128]{1,0:T(8,128)S(1)} %get-tuple-element.22.refs_4_), channel_id=1, source_target_pairs={{16,32},{48,64},{80,96},{112,128},{144,160},{176,192},{208,224},{2... | collective-permute-start | bytes 86024 | tf_op jit(solution)/shard_map/ppermute | solution.py:500
  33.0 4.8 %collective-permute-start.3 = (f32[56,128]{1,0:T(8,128)S(1)}, f32[56,128]{1,0:T(8,128)S(1)}, u32[]{:S(2)}, u32[]{:S(2)}) collective-permute-start(f32[56,128]{1,0:T(8,128)S(1)} %get-tuple-element.23.refs_5_), channel_id=1, source_target_pairs={{0,16},{32,48},{64,80},{96,112},{128,144},{160,176},{192,208},{224... | collective-permute-start | bytes 86024 | tf_op jit(solution)/shard_map/ppermute | solution.py:500
